TPU v7x, 32 devices: a whole 2x2x4 slice. The times are simulated.
32 devices in a mesh: expert: 8 (over z, x), tensor: 4 (over y, core).
Axes of the slice: x: 2, y: 2, z: 4, core: 2. Of those that a mesh axis runs over, the one named last changes fastest.
Arguments:
- tokens: bfloat16 [1024, 4096], P('expert'), may hold values from -6 to 6
- cotangent: bfloat16 [1024, 4096], P('expert'), may hold values from -6 to 6
- expert_ids: int32 [1024, 8], P('expert'), may hold values from 0 to 63, all different within a row; in each aligned block of 128 rows (0 to 127, 128 to 255, ...) at most 18 rows name the same one
- gate_probs: float32 [1024, 8], P('expert'), may hold values from 0.05 to 1
- w_gate: bfloat16 [64, 896, 4096], P('expert', 'tensor'), may hold values from -0.09375 to 0.09375
- w_up: bfloat16 [64, 896, 4096], P('expert', 'tensor'), may hold values from -0.09375 to 0.09375
- w_down: bfloat16 [64, 896, 4096], P('expert', 'tensor'), may hold values from -0.1875 to 0.1875
Outputs:
- mixed: bfloat16 [1024, 4096], P('expert')
- grad_tokens: bfloat16 [1024, 4096], P('expert')
Inputs may be any that keep to these rules, and one draw needn't show every extreme that they name: `expert_ids`: each token names 8 different experts; the 128 tokens of one index of the expert axis name one expert at most 18 times, a bound that some block reaches.
All inputs are finite; a program needn't handle non-finite values.
Results may differ from a plain program's by a relative error of at most 0.017.
Values may be sent and summed in bfloat16 or wider, within the bound.
No kernel may reach another device: no remote copies, remote signals or barrier semaphores. Data moves between devices by JAX's collectives and lax.ppermute only.
A program may use at most 192 MiB of HBM per device.

v0:
```python
import jax
import jax.numpy as jnp
from jax import lax
from jax.sharding import PartitionSpec as P


def expert_work(segment, w_gate, w_up, w_down, features):
    token_part = segment[..., :features]
    scaled_part = segment[..., features:]
    pre_gate = jnp.einsum("sicd,ihd->sich", token_part, w_gate, preferred_element_type=jnp.float32)
    up_value = jnp.einsum("sicd,ihd->sich", token_part, w_up, preferred_element_type=jnp.float32)
    sigmoid_gate = jax.nn.sigmoid(pre_gate)
    activated = pre_gate * sigmoid_gate
    hidden = (activated * up_value).astype(jnp.bfloat16)
    output_rows = jnp.einsum("sich,ihd->sicd", hidden, w_down, preferred_element_type=jnp.float32)
    grad_hidden = jnp.einsum(
        "sicd,ihd->sich", scaled_part, w_down, preferred_element_type=jnp.float32
    )
    grad_gate = (
        grad_hidden * up_value * sigmoid_gate * (1.0 + pre_gate * (1.0 - sigmoid_gate))
    ).astype(jnp.bfloat16)
    grad_up = (grad_hidden * activated).astype(jnp.bfloat16)
    grad_rows = jnp.einsum("sich,ihd->sicd", grad_gate, w_gate, preferred_element_type=jnp.float32)
    grad_rows = grad_rows + jnp.einsum(
        "sich,ihd->sicd", grad_up, w_up, preferred_element_type=jnp.float32
    )
    return jnp.concatenate([output_rows, grad_rows], axis=-1)


def body(tokens, cotangent, expert_ids, gate_probs, w_gate, w_up, w_down):
    tok_count, features = tokens.shape
    top_count = expert_ids.shape[1]
    expert_devs = lax.axis_size("expert")
    tensor_devs = lax.axis_size("tensor")
    local_experts = w_gate.shape[0]
    all_experts = local_experts * expert_devs
    capacity = max(2, 9 * tok_count * top_count // (8 * all_experts))
    own_share = local_experts // tensor_devs
    highest = lax.Precision.HIGHEST
    matches = expert_ids[:, :, None] == jnp.arange(all_experts, dtype=jnp.int32)[None, None, :]
    chosen = jnp.sum(matches.astype(jnp.float32), axis=1)
    prob_table = jnp.sum(jnp.where(matches, gate_probs[:, :, None], 0.0), axis=1)
    positions = jnp.arange(tok_count, dtype=jnp.int32)
    earlier = (positions[:, None] > positions[None, :]).astype(jnp.float32)
    slot_table = jnp.dot(earlier, chosen, precision=highest)
    slot_ids = jnp.arange(capacity, dtype=jnp.float32)
    place = jnp.where(
        chosen.T[:, None, :] > 0.5,
        (slot_table.T[:, None, :] == slot_ids[None, :, None]).astype(jnp.float32),
        0.0,
    )
    token_rows = jnp.einsum(
        "est,td->esd", place.astype(jnp.bfloat16), tokens, preferred_element_type=jnp.float32
    ).astype(jnp.bfloat16)
    place_prob = place * prob_table.T[:, None, :]
    scaled_rows = jnp.einsum(
        "est,td->esd", place_prob, cotangent.astype(jnp.float32), precision=highest
    ).astype(jnp.bfloat16)
    buffer = jnp.concatenate([token_rows, scaled_rows], axis=-1)
    buffer = buffer.reshape(expert_devs, local_experts, capacity, 2 * features)
    arrived = lax.all_to_all(buffer, "expert", split_axis=0, concat_axis=0, tiled=True)
    results = expert_work(arrived, w_gate, w_up, w_down, features)
    reduced = lax.psum_scatter(
        results.astype(jnp.bfloat16), "tensor", scatter_dimension=1, tiled=True
    )
    returned_rows = lax.all_to_all(reduced, "expert", split_axis=0, concat_axis=0, tiled=True)
    row_total = expert_devs * own_share * capacity
    returned_rows = returned_rows.reshape(row_total, 2 * features)
    tensor_place = lax.axis_index("tensor")
    chosen_mine = lax.dynamic_slice_in_dim(
        chosen.reshape(tok_count, expert_devs, tensor_devs, own_share), tensor_place, 1, 2
    )[:, :, 0, :]
    slot_mine = lax.dynamic_slice_in_dim(
        slot_table.reshape(tok_count, expert_devs, tensor_devs, own_share), tensor_place, 1, 2
    )[:, :, 0, :]
    prob_mine = lax.dynamic_slice_in_dim(
        prob_table.reshape(tok_count, expert_devs, tensor_devs, own_share), tensor_place, 1, 2
    )[:, :, 0, :]
    collect = jnp.where(
        chosen_mine[..., None] > 0.5,
        (slot_mine[..., None] == slot_ids[None, None, None, :]).astype(jnp.float32),
        0.0,
    )
    collect_prob = (collect * prob_mine[..., None]).reshape(tok_count, row_total)
    collect = collect.reshape(tok_count, row_total)
    output_part = jnp.dot(
        collect_prob, returned_rows[:, :features].astype(jnp.float32), precision=highest
    )
    input_part = jnp.dot(
        collect.astype(jnp.bfloat16),
        returned_rows[:, features:],
        preferred_element_type=jnp.float32,
    )
    mixed, grad_tokens = (
        lax.psum(output_part.astype(jnp.bfloat16), "tensor").astype(jnp.float32),
        lax.psum(input_part.astype(jnp.bfloat16), "tensor").astype(jnp.float32),
    )
    return (mixed.astype(jnp.bfloat16), grad_tokens.astype(jnp.bfloat16))


def solution(mesh):
    return jax.shard_map(
        body,
        mesh=mesh,
        in_specs=(
            P("expert", None),
            P("expert", None),
            P("expert", None),
            P("expert", None),
            P("expert", "tensor", None),
            P("expert", "tensor", None),
            P("expert", "tensor", None),
        ),
        out_specs=(P("expert", None), P("expert", None)),
        check_vma=False,
    )
```

profile of v0, /device:TPU:0, one launch (start us, length us, event | category | flops | bytes accessed | tf_op | source)
XLA Modules:
  0.0 953.7 jit_solution(10083617192439904968)
XLA Ops:
  7.2 0.0 reduce-scatter.2.cloned.1.call-start
  7.2 0.9 convert_reduce_fusion
  8.1 0.2 fusion.52
  8.4 0.1 copy-done
  8.4 2.8 convolution_convert_fusion.1
  11.2 7.9 convolution_convert_fusion
  19.1 1.8 maximum_bitcast_fusion
  20.9 6.7 copy.43
  27.6 415.5 %all_to_all.10 = bf16[8,8,18,8192]{3,1,2,0:T(8,128)(2,1)S(1)} all-to-all(bf16[8,8,18,8192]{3,1,2,0:T(8,128)(2,1)} %copy.43), channel_id=1, replica_groups=mesh['expert'=8,'tensor'=4] {'expert'}, dimensions={0} | all-to-all | bytes 37748736 | tf_op jit(solution)/shard_map/all_to_all | solution.py:61
  443.1 6.7 fusion.60
  449.8 14.5 %fusion.6 = f32[8,8,18,224]{3,2,1,0:T(8,128)S(1)} fusion(bf16[8,224,4096]{2,1,0:T(8,128)(2,1)} %param.11, bf16[8,8,18,4096]{3,1,2,0:T(8,128)(2,1)} %get-tuple-element.6), kind=kOutput, calls=%fused_computation.9 | convolution fusion | flops 2113929216 | bytes 25149440 | tf_op jit(solution)/shard_map/sicd,ihd->sich/dot_general | solution.py:10
  464.4 14.5 %fusion.2 = f32[8,8,18,224]{3,2,1,0:T(8,128)S(1)} fusion(bf16[8,224,4096]{2,1,0:T(8,128)(2,1)} %param.12, bf16[8,8,18,4096]{3,1,2,0:T(8,128)(2,1)} %get-tuple-element.6), kind=kOutput, calls=%fused_computation.5 | convolution fusion | flops 2113929216 | bytes 25149440 | tf_op jit(solution)/shard_map/sicd,ihd->sich/dot_general | solution.py:11
  478.9 16.1 %fusion.8 = f32[8,8,18,224]{3,2,1,0:T(8,128)} fusion(bf16[8,224,4096]{2,1,0:T(8,128)(2,1)} %param.13, bf16[8,8,18,4096]{3,1,2,0:T(8,128)(2,1)} %get-tuple-element.7), kind=kOutput, calls=%fused_computation.11 | convolution fusion | flops 2113929216 | bytes 25149440 | tf_op jit(solution)/shard_map/sicd,ihd->sich/dot_general | solution.py:16
  495.0 17.5 %fusion = f32[8,8,18,4096]{3,2,1,0:T(8,128)} fusion(bf16[8,224,4096]{2,1,0:T(8,128)(2,1)} %param.12, f32[8,8,18,224]{3,2,1,0:T(8,128)} %fusion.8, f32[8,8,18,224]{3,2,1,0:T(8,128)S(1)} %fusion.6), kind=kOutput, calls=%fused_computation.3 | convolution fusion | flops 2115477504 | bytes 35618816 | tf_op jit(solution)/shard_map/sich,ihd->sicd/dot_general | solution.py:24
  512.5 13.2 %convert_bitcast_fusion = bf16[8,8,18,4096]{3,2,0,1:T(8,128)(2,1)} fusion(bf16[8,224,4096]{2,1,0:T(8,128)(2,1)} %param.13, f32[8,8,18,224]{3,2,1,0:T(8,128)S(1)} %fusion.2, f32[8,8,18,224]{3,2,1,0:T(8,128)S(1)} %fusion.6), kind=kOutput, calls=%fused_computation.19 | convolution fusion | flops 2120196096 | bytes 26181632 | tf_op jit(solution)/shard_map/sich,ihd->sicd/dot_general | solution.py:15
  525.7 22.8 %fusion.14 = bf16[8,8,18,4096]{3,2,0,1:T(8,128)(2,1)} fusion(f32[8,8,18,4096]{3,2,1,0:T(8,128)} %fusion, bf16[8,224,4096]{2,1,0:T(8,128)(2,1)} %param.11, f32[8,8,18,224]{3,2,1,0:T(8,128)} %fusion.8, f32[8,8,18,224]{3,2,1,0:T(8,128)} %copy-done.2, f32[8,8,18,224]{3,2,1,0:T(8,128)S(1)} %fusion.6), kind=kOutput, calls=%fused_computation.17 | convolution fusion | flops 2125946880 | bytes 46088192 | tf_op jit(solution)/shard_map/sich,ihd->sicd/dot_general | solution.py:23
  548.5 21.5 %pad_maximum_fusion = bf16[8,8,18,8192]{3,2,0,1:T(8,128)(2,1)} fusion(bf16[8,8,18,4096]{3,2,0,1:T(8,128)(2,1)} %fusion.14, bf16[8,8,18,4096]{3,2,0,1:T(8,128)(2,1)} %convert_bitcast_fusion), kind=kLoop, calls=%fused_computation | loop fusion | flops 37748736 | bytes 37748736 | tf_op jit(solution)/shard_map/concatenate | solution.py:27
  570.0 0.0 reduce-scatter.2.cloned.1.call-update
  570.0 179.6 %reduce-scatter.2.cloned.1.call-done = bf16[8,2,18,8192]{3,2,0,1:T(8,128)(2,1)} async-done(((bf16[8,8,18,8192]{3,2,0,1:T(8,128)(2,1)}), bf16[8,2,18,8192]{3,2,0,1:T(8,128)(2,1)}) %reduce-scatter.2.cloned.1.call-update) | async-done | bytes 4718608 | tf_op jit(solution)/shard_map/reduce_scatter | solution.py:63
  749.6 9.8 %copy.46 = bf16[8,2,18,8192]{3,1,2,0:T(2,128)(2,1)} copy(bf16[8,2,18,8192]{3,2,0,1:T(8,128)(2,1)} %reduce-scatter.2.cloned.1.call-done) | data formatting | bytes 9437184 | tf_op jit(solution)/shard_map/reduce_scatter | solution.py:63
  759.4 5.5 all-to-all-start.1
  764.9 0.3 all-reduce.3.cloned.1.call-start
  765.3 0.1 eq.56
  765.6 0.1 broadcast_compare_fusion
  765.7 103.8 %all-to-all-done.1 = bf16[8,2,18,8192]{3,1,2,0:T(2,128)(2,1)} async-done(((bf16[8,2,18,8192]{3,1,2,0:T(2,128)(2,1)}), bf16[8,2,18,8192]{3,1,2,0:T(2,128)(2,1)}, u32[]{:S(2)}, u32[]{:S(2)}) %all-to-all-start.1) | async-done | bytes 4718624 | tf_op jit(solution)/shard_map/all_to_all | solution.py:66
  869.5 8.6 copy.47
  878.1 6.1 reshape.49
  884.3 3.4 convolution_convert_fusion.2
  887.7 4.5 convolution_convert_fusion.3
  892.1 49.8 %all-reduce.3.cloned.1.call-done = (bf16[128,4096]{1,0:T(8,128)(2,1)}, bf16[128,4096]{1,0:T(8,128)(2,1)}) async-done(((bf16[128,4096]{1,0:T(8,128)(2,1)}, bf16[128,4096]{1,0:T(8,128)(2,1)}), (bf16[128,4096]{1,0:T(8,128)(2,1)}, bf16[128,4096]{1,0:T(8,128)(2,1)})) %all-reduce.3.cloned.1.call-update) | async-done | bytes 2097168 | tf_op jit(solution)/shard_map/psum | solution.py:95
  942.0 2.3 copy.68
  944.3 2.3 copy.69
  (21 shorter events, 0.2 us)
Async XLA Ops:
  7.2 1.3 copy-start
  7.2 4.0 copy-start.3
  7.2 742.4 %reduce-scatter.2.cloned.1.call-start = ((), (), s32[]{:S(2)}) async-start(), calls=%async_computation.3 | async-start | bytes 31457280 | tf_op jit(solution)/shard_map/reduce_scatter | solution.py:63
  478.9 33.6 %copy-start.2 = (f32[8,8,18,224]{3,2,1,0:T(8,128)}, f32[8,8,18,224]{3,2,1,0:T(8,128)S(1)}, u32[]{:S(2)}) copy-start(f32[8,8,18,224]{3,2,1,0:T(8,128)S(1)} %fusion.2) | copy-start | bytes 3096580
  759.4 110.0 %all-to-all-start.1 = ((bf16[8,2,18,8192]{3,1,2,0:T(2,128)(2,1)}), bf16[8,2,18,8192]{3,1,2,0:T(2,128)(2,1)}, u32[]{:S(2)}, u32[]{:S(2)}) async-start(bf16[8,2,18,8192]{3,1,2,0:T(2,128)(2,1)} %copy.46), calls=%async_computation.2 | async-start | bytes 9437184 | tf_op jit(solution)/shard_map/all_to_all | solution.py:66
  764.9 177.0 %all-reduce.3.cloned.1.call-start = ((), (), s32[]{:S(2)}) async-start(), calls=%async_computation.4 | async-start | bytes 4194304 | tf_op jit(solution)/shard_map/psum | solution.py:95
  878.1 68.5 %copy-start.1 = (bf16[128,4096]{1,0:T(8,128)(2,1)S(1)}, bf16[128,4096]{1,0:T(8,128)(2,1)}, u32[]{:S(2)}) copy-start(bf16[128,4096]{1,0:T(8,128)(2,1)} %param.7) | copy-start | bytes 3145732
Sparse Core Ops, SparseCore 0:
  570.1 179.4 reduce-scatter.1
  892.3 49.6 all-reduce.2
where the time goes:
time: 958 us; the launch traced here: 954 us
  blocking collectives  416 us (43%)
  waiting for transfers between devices  333 us (35%)
  matrix products  117 us (12%)
  local copies, waits for them, and re-layouts  42.9 us (4%)
  other arithmetic  24.3 us (3%)
  between operations  14.5 us (2%)
    all_to_all x1, blocking collectives, body(): lax.all_to_all(buffer, 'expert', split_axis=0, concat_axis=0, tiled=True)  416 us
    reduce_scatter x1, waiting for transfers between devices, body(): lax.psum_scatter(results.astype(jnp.bfloat16), 'tensor', scatter_dimensio...  180 us
    all_to_all x1, waiting for transfers between devices, body(): lax.all_to_all(reduced, 'expert', split_axis=0, concat_axis=0, tiled=True)  104 us
    psum x1, waiting for transfers between devices, body(): lax.psum(output_part.astype(jnp.bfloat16), 'tensor').astype(jnp.float32)  49.8 us
    dot_general x1, matrix products, expert_work(): jnp.einsum('sich,ihd->sicd', grad_gate, w_gate, preferred_element_type=jn...  22.8 us
    concatenate x1, other arithmetic, expert_work(): return jnp.concatenate([output_rows, grad_rows], axis=-1)  21.5 us
  transfers between devices with their start and end apart: 3, of which 3 were waited for; matrix products, arithmetic and copies ran while one was open for 0% of the time, Pallas kernels for 0%

commit v1 on v0

v1 whole, which is shorter than its diff:
```python
import functools

import jax
import jax.numpy as jnp
from jax import lax
from jax.experimental import pallas as pl
from jax.experimental.pallas import tpu as pltpu
from jax.sharding import PartitionSpec as P

AXES = ("expert", "tensor")
CHUNK = 512
ROW_TILE = 16


def chip_moves():
    def pairs(step):
        found = []
        for z in range(4):
            for x in range(2):
                for y in range(2):
                    for core in range(2):
                        to_z, to_x, to_y, to_core = step(z, x, y, core)
                        source = (z * 2 + x) * 4 + y * 2 + core
                        found.append((source, ((to_z % 4) * 2 + to_x) * 4 + to_y * 2 + to_core))
        return found

    return dict(
        ahead=pairs(lambda z, x, y, core: (z + 1 - 2 * y, x, y, core)),
        back=pairs(lambda z, x, y, core: (z - 1 + 2 * y, x, y, core)),
        x=pairs(lambda z, x, y, core: (z, 1 - x, y, core)),
        y=pairs(lambda z, x, y, core: (z, x, 1 - y, core)),
        core=pairs(lambda z, x, y, core: (z, x, y, 1 - core)),
    )


MOVES = chip_moves()


def move(array, name):
    return lax.ppermute(array, AXES, MOVES[name])


def add(*terms):
    total = terms[0].astype(jnp.float32)
    for term in terms[1:]:
        total = total + term.astype(jnp.float32)
    return total.astype(jnp.bfloat16)


def spread(array, core, through_x):
    half = array.shape[1] // 2
    q0 = lax.dynamic_slice_in_dim(array, core * half, half, 1)
    own_other = lax.dynamic_slice_in_dim(array, (1 - core) * half, half, 1)
    q1, r0 = move(q0, "ahead"), move(q0, "x")
    q2, r1, q3 = move(q1, "ahead"), move(q1, "x"), move(q1, "y")
    r3 = move(r1, "y")
    r2 = move(q2, "x") if through_x else move(r1, "ahead")
    mine = [q0, r0, q1, r1, q2, r2, q3, r3]
    other = [own_other] + [move(block, "core") for block in mine[1:]]
    return mine + other


def collect(to_other, to_mine, core, through_x):
    arrived = move(to_other, "core")
    rows = to_mine.shape[0] // 8
    own, r0, q1, r1, q2, r2, q3, r3 = [
        add(to_mine[j * rows : (j + 1) * rows], arrived[j * rows : (j + 1) * rows]) for j in range(8)
    ]
    from_y_r, from_y_q, from_x = move(r3, "y"), move(q3, "y"), move(r0, "x")
    if through_x:
        r1 = add(r1, from_y_r)
        q2 = add(q2, move(r2, "x"))
    else:
        r1 = add(r1, from_y_r, move(r2, "back"))
    q1 = add(q1, from_y_q, move(r1, "x"), move(q2, "back"))
    own = add(own, from_x, move(q1, "back"))
    final = add(own, move(own, "y"))
    final_other = move(final, "core")
    return jnp.concatenate(
        [jnp.where(core == 0, final, final_other), jnp.where(core == 0, final_other, final)], axis=1
    )


def expert_kernel(backward, sources, group, experts, slots, half, *refs):
    core_ref, place_ref, place_t_ref, prob_ref = refs[:4]
    piece_refs = refs[4 : 4 + 2 * sources]
    gate_ref, up_ref, down_ref = refs[4 + 2 * sources : 7 + 2 * sources]
    first_ref, second_ref, other_ref, mine_ref, block_ref, rows_ref, sem_ref = refs[7 + 2 * sources :]
    step = pl.program_id(0)
    core = core_ref[0]
    tokens = block_ref.shape[1] // sources
    span = group * tokens
    groups = sources // group
    nt = (((1,), (1,)), ((), ()))

    @pl.when(step == 0)
    def _():
        def copy(side, j):
            place = block_ref.at[side, pl.ds(j * tokens, tokens)]
            return pltpu.make_async_copy(
                piece_refs[side * sources + j], place, sem_ref.at[side * sources + j]
            )

        for k in range(groups):
            for side in range(2):
                for j in range(k * group, (k + 1) * group):
                    copy(side, j).start()
        for k in range(groups):
            for side in range(2):
                for j in range(k * group, (k + 1) * group):
                    copy(side, j).wait()
                base = (core if side == 0 else 1 - core) * half

                @pl.loop(0, half // CHUNK)
                def _(i):
                    column = pl.multiple_of(i * CHUNK, CHUNK)
                    block = block_ref[side, pl.ds(k * span, span), pl.ds(column, CHUNK)]
                    picked = jnp.dot(place_ref[k], block, preferred_element_type=jnp.float32)
                    if backward:
                        picked = picked * prob_ref[k]
                    to = pl.multiple_of(base + column, CHUNK)
                    rows_ref[:, pl.ds(k * slots, slots), pl.ds(to, CHUNK)] = picked.astype(
                        jnp.bfloat16
                    ).reshape(experts, slots, CHUNK)

    @pl.when(step < experts)
    def _():
        rows = rows_ref[step]
        if backward:
            grad_hidden = lax.dot_general(rows, down_ref[0], nt, preferred_element_type=jnp.float32)
            left = (grad_hidden * first_ref[0]).astype(jnp.bfloat16)
            right = (grad_hidden * second_ref[0]).astype(jnp.bfloat16)
        else:
            pre_gate = lax.dot_general(rows, gate_ref[0], nt, preferred_element_type=jnp.float32)
            up_value = lax.dot_general(rows, up_ref[0], nt, preferred_element_type=jnp.float32)
            sigmoid = jax.nn.sigmoid(pre_gate)
            activated = pre_gate * sigmoid
            left = (activated * up_value).astype(jnp.bfloat16)
            first_ref[0] = up_value * sigmoid * (1.0 + pre_gate * (1.0 - sigmoid))
            second_ref[0] = activated

        @pl.loop(0, 2 * half // CHUNK)
        def _(i):
            columns = pl.ds(pl.multiple_of(i * CHUNK, CHUNK), CHUNK)
            if backward:
                result = jnp.dot(
                    left, gate_ref[0, :, columns], preferred_element_type=jnp.float32
                ) + jnp.dot(right, up_ref[0, :, columns], preferred_element_type=jnp.float32)
            else:
                result = jnp.dot(left, down_ref[0, :, columns], preferred_element_type=jnp.float32)
                result = result * prob_ref[0]
            rows_ref[step, :, columns] = result.astype(jnp.bfloat16)

    def combine(part, out_ref, side):
        base = (core if side == 0 else 1 - core) * half
        columns = pl.ds(pl.multiple_of(base + part * CHUNK, CHUNK), CHUNK)
        for k in range(groups):
            rows = rows_ref[:, pl.ds(k * slots, slots), columns].reshape(experts * slots, CHUNK)
            out_ref[pl.ds(k * span, span), :] = jnp.dot(
                place_t_ref[k], rows, preferred_element_type=jnp.float32
            ).astype(jnp.bfloat16)

    parts = half // CHUNK

    @pl.when((step >= experts) & (step < experts + parts))
    def _():
        combine(step - experts, other_ref, 1)

    @pl.when(step >= experts + parts)
    def _():
        combine(step - experts - parts, mine_ref, 0)


def expert_call(backward, core, place, place_t, prob, pieces, weights, factors, group):
    w_gate, w_up, w_down = weights
    experts, hidden, features = w_gate.shape
    sources = len(pieces) // 2
    tokens, half = pieces[0].shape
    groups, height, span = place.shape
    slots = height // experts
    total = groups * slots
    parts = half // CHUNK
    last = experts - 1
    whole = lambda shape: pl.BlockSpec(shape, lambda i, c: (0,) * len(shape))
    per_expert = lambda shape: pl.BlockSpec(shape, lambda i, c: (jnp.minimum(i, last), 0, 0))
    factor_spec = per_expert((1, total, hidden))
    factor_shape = jax.ShapeDtypeStruct((experts, total, hidden), jnp.float32)
    out_shape = jax.ShapeDtypeStruct((sources * tokens, half), jnp.bfloat16)
    out_specs = [
        pl.BlockSpec((sources * tokens, CHUNK), lambda i, c: (0, jnp.clip(i - experts, 0, parts - 1))),
        pl.BlockSpec(
            (sources * tokens, CHUNK), lambda i, c: (0, jnp.clip(i - experts - parts, 0, parts - 1))
        ),
    ]
    in_specs = [
        whole(place.shape),
        whole(place_t.shape),
        whole(prob.shape) if backward else per_expert((1, total, 1)),
    ]
    in_specs += [pl.BlockSpec(memory_space=pl.ANY)] * (2 * sources)
    in_specs += [per_expert((1, hidden, features))] * 3
    if backward:
        in_specs += [factor_spec, factor_spec]
        out_shapes = [out_shape, out_shape]
    else:
        out_specs = [factor_spec, factor_spec] + out_specs
        out_shapes = [factor_shape, factor_shape, out_shape, out_shape]
    flops = 2 * features * (3 * experts * total * hidden + 2 * groups * height * span)
    return pl.pallas_call(
        functools.partial(expert_kernel, backward, sources, group, experts, slots, half),
        grid_spec=pltpu.PrefetchScalarGridSpec(
            num_scalar_prefetch=1,
            grid=(experts + 2 * parts,),
            in_specs=in_specs,
            out_specs=out_specs,
            scratch_shapes=[
                pltpu.VMEM((2, sources * tokens, half), jnp.bfloat16),
                pltpu.VMEM((experts, total, features), jnp.bfloat16),
                pltpu.SemaphoreType.DMA((2 * sources,)),
            ],
        ),
        out_shape=out_shapes,
        compiler_params=pltpu.CompilerParams(vmem_limit_bytes=58 * 1024 * 1024),
        cost_estimate=pl.CostEstimate(
            flops=flops,
            bytes_accessed=3 * experts * hidden * features * 2 + 4 * sources * tokens * features,
            transcendentals=0,
        ),
        name="experts_backward" if backward else "experts_forward",
    )(core, place, place_t, prob, *pieces, w_gate, w_up, w_down, *factors)


def routing(expert_ids, gate_probs, local_experts, capacity, group):
    sources, tokens, _ = expert_ids.shape
    groups = sources // group
    slots = -(-group * capacity // ROW_TILE) * ROW_TILE
    first = lax.axis_index("expert") * local_experts
    matches = (expert_ids - first)[..., None] == jnp.arange(local_experts, dtype=jnp.int32)
    chosen = jnp.any(matches, axis=2)
    prob = jnp.sum(jnp.where(matches, gate_probs[..., None], 0.0), axis=2)
    earlier = jnp.arange(tokens)[:, None] > jnp.arange(tokens)[None, :]
    position = jnp.einsum(
        "tu,sue->ste",
        earlier.astype(jnp.bfloat16),
        chosen.astype(jnp.bfloat16),
        preferred_element_type=jnp.float32,
    ).astype(jnp.int32)
    position = position + (jnp.arange(sources, dtype=jnp.int32) % group * capacity)[:, None, None]
    position = jnp.where(chosen, position, -1)
    position = position.reshape(groups, group * tokens, local_experts)
    prob = prob.reshape(groups, group * tokens, local_experts).transpose(0, 2, 1)
    slot = jnp.arange(slots, dtype=jnp.int32)
    place = position.transpose(0, 2, 1)[:, :, None, :] == slot[:, None]
    place_t = position[:, :, :, None] == slot
    row_prob = jnp.sum(jnp.where(place, prob[:, :, None, :], 0.0), axis=3)
    height = local_experts * slots
    place = place.astype(jnp.bfloat16).reshape(groups, height, group * tokens)
    place_t = place_t.astype(jnp.bfloat16).reshape(groups, group * tokens, height)
    forward_prob = row_prob.transpose(1, 0, 2).reshape(local_experts, groups * slots, 1)
    return place, place_t, forward_prob, row_prob.reshape(groups, height, 1)


def body(fast, tokens, cotangent, expert_ids, gate_probs, w_gate, w_up, w_down):
    tok_count, features = tokens.shape
    top = expert_ids.shape[1]
    expert_devs = lax.axis_size("expert")
    local_experts = w_gate.shape[0]
    capacity = max(2, 9 * tok_count * top // (8 * local_experts * expert_devs))
    group = max(1, expert_devs // 4)
    weights = (w_gate, w_up, w_down)
    half = features // 2
    if fast:
        core = lax.axis_index("tensor") % 2
        choice = jnp.concatenate([expert_ids.astype(jnp.float32).T, gate_probs.T], axis=0)
        choice0 = jnp.stack([choice, move(choice, "x")])
        choice1 = move(choice0, "ahead")
        choice = jnp.concatenate([choice0, choice1, move(choice1, "ahead"), move(choice1, "y")])
        choice = choice.transpose(0, 2, 1)
        ids, probs = choice[..., :top].astype(jnp.int32), choice[..., top:]
        token_pieces = spread(tokens, core, True)
        cotangent_pieces = spread(cotangent, core, False)
    else:
        core = jnp.int32(0)

        def everywhere(array):
            return lax.all_gather(array, "expert", tiled=False)

        def split(array):
            blocks = everywhere(array)
            return [
                blocks[j, :, side * half : (side + 1) * half]
                for side in range(2)
                for j in range(expert_devs)
            ]

        ids, probs = everywhere(expert_ids), everywhere(gate_probs)
        token_pieces, cotangent_pieces = split(tokens), split(cotangent)
    place, place_t, forward_prob, backward_prob = routing(ids, probs, local_experts, capacity, group)
    core_ref = core.astype(jnp.int32).reshape(1)
    first, second, out_other, out_mine = expert_call(
        False, core_ref, place, place_t, forward_prob, token_pieces, weights, (), group
    )
    grad_other, grad_mine = expert_call(
        True, core_ref, place, place_t, backward_prob, cotangent_pieces, weights, (first, second), group
    )
    if fast:
        return collect(out_other, out_mine, core, True), collect(grad_other, grad_mine, core, False)

    def total(mine, other):
        partial = jnp.concatenate([mine, other], axis=1)
        own = lax.psum_scatter(partial, "expert", scatter_dimension=0, tiled=True)
        return lax.psum(own, "tensor")

    return total(out_mine, out_other), total(grad_mine, grad_other)


def solution(mesh):
    fast = mesh.shape["expert"] == 8 and mesh.shape["tensor"] == 4
    return jax.shard_map(
        functools.partial(body, fast),
        mesh=mesh,
        in_specs=(
            P("expert", None),
            P("expert", None),
            P("expert", None),
            P("expert", None),
            P("expert", "tensor", None),
            P("expert", "tensor", None),
            P("expert", "tensor", None),
        ),
        out_specs=(P("expert", None), P("expert", None)),
        check_vma=False,
    )
```

time: 958 us -> 299 us (0.31)
  blocking collectives: 416 us -> 0 us
  waiting for transfers between devices: 333 us -> 113 us
  matrix products: 117 us -> 0.11 us
  Pallas kernels: 0 us -> 92.9 us
  starting transfers between devices: 5.82 us -> 68 us
  local copies, waits for them, and re-layouts: 42.9 us -> 9.33 us
  between operations: 14.5 us -> 1.18 us
  other arithmetic: 24.3 us -> 14.4 us
    all_to_all x1 -> x0, blocking collectives: 416 us -> none  [body(): lax.all_to_all(buffer, 'expert', split_axis=0, concat_axis=0, tiled=True)]
    reduce_scatter x1 -> x0, waiting for transfers between devices: 180 us -> none  [body(): lax.psum_scatter(results.astype(jnp.bfloat16), 'tensor', scatter_dimensio...]
    dot_general x11 -> x1, matrix products: 117 us -> 0.11 us  [routing(): jnp.einsum('tu,sue->ste', earlier.astype(jnp.bfloat16), chosen.astype(jnp...]
    ppermute x0 -> x52, waiting for transfers between devices: none -> 113 us  [move(): return lax.ppermute(array, AXES, MOVES[name])]
    all_to_all x1 -> x0, waiting for transfers between devices: 104 us -> none  [body(): lax.all_to_all(reduced, 'expert', split_axis=0, concat_axis=0, tiled=True)]
    pallas_call x0 -> x2, Pallas kernels: none -> 92.9 us  [expert_call(): pl.pallas_call(functools.partial(expert_kernel, backward, sources, group,...]
    ppermute x0 -> x52, starting transfers between devices: none -> 68 us  [move(): return lax.ppermute(array, AXES, MOVES[name])]
    psum x1 -> x0, waiting for transfers between devices: 49.8 us -> none  [body(): lax.psum(output_part.astype(jnp.bfloat16), 'tensor').astype(jnp.float32)]
  transfers between devices with their start and end apart: 3 -> 52, of which waited for: 3 -> 20; matrix products, arithmetic and copies ran while one was open for 0% -> 6% of each run, Pallas kernels for 0% -> 31%
where the time goes in v1:
time: 299 us
  waiting for transfers between devices  113 us (38%)
  Pallas kernels  92.9 us (31%)
  starting transfers between devices  68 us (23%)
  other arithmetic  14.4 us (5%)
  local copies, waits for them, and re-layouts  9.33 us (3%)
    ppermute x52, waiting for transfers between devices, move(): return lax.ppermute(array, AXES, MOVES[name])  113 us
    pallas_call x2, Pallas kernels, expert_call(): pl.pallas_call(functools.partial(expert_kernel, backward, sources, group,...  92.9 us
    ppermute x52, starting transfers between devices, move(): return lax.ppermute(array, AXES, MOVES[name])  68 us
    convert_element_type x10, other arithmetic, add(): return total.astype(jnp.bfloat16)  9.6 us
  transfers between devices with their start and end apart: 52, of which 20 were waited for; matrix products, arithmetic and copies ran while one was open for 6% of the time, Pallas kernels for 31%

profile of v1, /device:TPU:0, one launch (start us, length us, event | category | flops | bytes accessed | tf_op | source)
XLA Modules:
  0.0 299.2 jit_solution(18400848241457831029)
XLA Ops:
  0.7 2.1 constant_dynamic-slice_fusion.2
  2.8 2.9 collective-permute-start.4
  7.3 2.1 constant_dynamic-slice_fusion
  11.5 17.6 %collective-permute-done = f32[16,128]{1,0:T(8,128)S(1)} collective-permute-done((f32[16,128]{1,0:T(8,128)S(1)}, f32[16,128]{1,0:T(8,128)S(1)}, u32[]{:S(2)}, u32[]{:S(2)}) %collective-permute-start) | collective-permute-done | bytes 8224 | tf_op jit(solution)/shard_map/ppermute | solution.py:40
  29.1 1.8 collective-permute-start.1
  30.9 3.7 %collective-permute-done.1 = f32[2,16,128]{2,1,0:T(8,128)S(1)} collective-permute-done((f32[2,16,128]{2,1,0:T(8,128)S(1)}, f32[2,16,128]{2,1,0:T(8,128)S(1)}, u32[]{:S(2)}, u32[]{:S(2)}) %collective-permute-start.1) | collective-permute-done | bytes 16416 | tf_op jit(solution)/shard_map/ppermute | solution.py:40
  34.6 5.3 %collective-permute-start.3 = (f32[2,16,128]{2,1,0:T(8,128)S(1)}, f32[2,16,128]{2,1,0:T(8,128)S(1)}, u32[]{:S(2)}, u32[]{:S(2)}) collective-permute-start(f32[2,16,128]{2,1,0:T(8,128)S(1)} %collective-permute-done.1), channel_id=1, source_target_pairs={{0,2},{1,3},{2,0},{3,1},{4,6},{5,7},{6,4},{7,5},{8,10},{9,11},{10,... | collective-permute-start | bytes 49160 | tf_op jit(solution)/shard_map/ppermute | solution.py:40
  40.2 1.8 collective-permute-start.6
  42.0 5.1 %collective-permute-start.9 = (bf16[128,2048]{1,0:T(8,128)(2,1)S(1)}, bf16[128,2048]{1,0:T(8,128)(2,1)}, u32[]{:S(2)}, u32[]{:S(2)}) collective-permute-start(bf16[128,2048]{1,0:T(8,128)(2,1)S(1)} %collective-permute-done.5.refs_6_), channel_id=1, source_target_pairs={{0,2},{1,3},{2,0},{3,1},{4,6},{5,7},{6,4},{7,5},{8,10},{9,11},{10,... | collective-permute-start | bytes 1572872 | tf_op jit(solution)/shard_map/ppermute | solution.py:40
  47.3 9.7 %collective-permute-done.29.refs_6_ = bf16[128,2048]{1,0:T(8,128)(2,1)} collective-permute-done((bf16[128,2048]{1,0:T(8,128)(2,1)S(1)}, bf16[128,2048]{1,0:T(8,128)(2,1)}, u32[]{:S(2)}, u32[]{:S(2)}) %collective-permute-start.29) | collective-permute-done | bytes 524320 | tf_op jit(solution)/shard_map/ppermute | solution.py:40
  58.7 5.5 %collective-permute-done.7.refs_8_ = bf16[128,2048]{1,0:T(8,128)(2,1)} collective-permute-done((bf16[128,2048]{1,0:T(8,128)(2,1)S(1)}, bf16[128,2048]{1,0:T(8,128)(2,1)}, u32[]{:S(2)}, u32[]{:S(2)}) %collective-permute-start.7) | collective-permute-done | bytes 524320 | tf_op jit(solution)/shard_map/ppermute | solution.py:40
  64.2 4.9 %collective-permute-start.33 = (bf16[128,2048]{1,0:T(8,128)(2,1)}, bf16[128,2048]{1,0:T(8,128)(2,1)S(1)}, u32[]{:S(2)}, u32[]{:S(2)}) collective-permute-start(bf16[128,2048]{1,0:T(8,128)(2,1)} %collective-permute-done.29.refs_6_), channel_id=1, source_target_pairs={{0,2},{1,3},{2,0},{3,1},{4,6},{5,7},{6,4},{7,5},{8,10},{9,11},{10,... | collective-permute-start | bytes 1572872 | tf_op jit(solution)/shard_map/ppermute | solution.py:40
  69.8 1.7 collective-permute-done.30.refs_7_
  72.4 3.7 %collective-permute-done.31.refs_8_ = bf16[128,2048]{1,0:T(8,128)(2,1)S(1)} collective-permute-done((bf16[128,2048]{1,0:T(8,128)(2,1)}, bf16[128,2048]{1,0:T(8,128)(2,1)S(1)}, u32[]{:S(2)}, u32[]{:S(2)}) %collective-permute-start.31) | collective-permute-done | bytes 524320 | tf_op jit(solution)/shard_map/ppermute | solution.py:40
  76.2 3.7 %collective-permute-done.33.refs_10_ = bf16[128,2048]{1,0:T(8,128)(2,1)S(1)} collective-permute-done((bf16[128,2048]{1,0:T(8,128)(2,1)}, bf16[128,2048]{1,0:T(8,128)(2,1)S(1)}, u32[]{:S(2)}, u32[]{:S(2)}) %collective-permute-start.33) | collective-permute-done | bytes 524320 | tf_op jit(solution)/shard_map/ppermute | solution.py:40
  83.9 7.0 %collective-permute-done.8.refs_9_ = bf16[128,2048]{1,0:T(8,128)(2,1)} collective-permute-done((bf16[128,2048]{1,0:T(8,128)(2,1)}, bf16[128,2048]{1,0:T(8,128)(2,1)}, u32[]{:S(2)}, u32[]{:S(2)}) %collective-permute-start.8) | collective-permute-done | bytes 524320 | tf_op jit(solution)/shard_map/ppermute | solution.py:40
  96.8 3.1 %collective-permute-done.32.refs_9_ = bf16[128,2048]{1,0:T(8,128)(2,1)} collective-permute-done((bf16[128,2048]{1,0:T(8,128)(2,1)}, bf16[128,2048]{1,0:T(8,128)(2,1)}, u32[]{:S(2)}, u32[]{:S(2)}) %collective-permute-start.32) | collective-permute-done | bytes 524320 | tf_op jit(solution)/shard_map/ppermute | solution.py:40
  101.5 46.8 %experts_forward.1 = (f32[8,192,224]{2,1,0:T(8,128)}, f32[8,192,224]{2,1,0:T(8,128)}, bf16[1024,2048]{1,0:T(8,128)(2,1)}, bf16[1024,2048]{1,0:T(8,128)(2,1)}) custom-call(s32[1]{0:T(128)} %bitcast.refs_0_, bf16[4,384,256]{2,1,0:T(8,128)(2,1)} %fusion.refs_1_, bf16[4,256,384]{2,1,0:T(8,128)(2,1)} %compare_convert_fusion.refs_2_, ...), custom_call_target="tpu_custom_call" | custom-call | flops 14898167808 | bytes 60817408 | tf_op jit(solution)/shard_map/experts_forward/pallas_call | solution.py:209
  150.1 46.1 %experts_backward.1 = (bf16[1024,2048]{1,0:T(8,128)(2,1)}, bf16[1024,2048]{1,0:T(8,128)(2,1)}) custom-call(s32[1]{0:T(128)} %bitcast.refs_0_, bf16[4,384,256]{2,1,0:T(8,128)(2,1)} %fusion.refs_1_, bf16[4,256,384]{2,1,0:T(8,128)(2,1)} %compare_convert_fusion.refs_2_, f32[4,384,1]{2,1,0:T(8,128)} %reshape.47.refs_3_, bf16[128,2048]{1,0:T(8,128)(2,1)} %copy-done.2, ...), custom_call_target="tpu_custom_call" | custom-call | flops 14898167808 | bytes 60817408 | tf_op jit(solution)/shard_map/experts_backward/pallas_call | solution.py:209
  196.3 2.5 add_convert_fusion.23
  204.9 6.6 %collective-permute-start.46 = (bf16[128,2048]{1,0:T(8,128)(2,1)S(1)}, bf16[128,2048]{1,0:T(8,128)(2,1)S(1)}, u32[]{:S(2)}, u32[]{:S(2)}) collective-permute-start(bf16[128,2048]{1,0:T(8,128)(2,1)S(1)} %get-tuple-element.16), channel_id=1, source_target_pairs={{0,24},{1,25},{2,10},{3,11},{4,28},{5,29},{6,14},{7,15},{8,0},{9,1... | collective-permute-start | bytes 1572872 | tf_op jit(solution)/shard_map/ppermute | solution.py:40
  211.5 2.1 collective-permute-done.21
  213.6 1.7 add_convert_fusion.18
  215.3 7.8 %collective-permute-start.24 = (bf16[128,2048]{1,0:T(8,128)(2,1)S(1)}, bf16[128,2048]{1,0:T(8,128)(2,1)S(1)}, u32[]{:S(2)}, u32[]{:S(2)}) collective-permute-start(bf16[128,2048]{1,0:T(8,128)(2,1)S(1)} %get-tuple-element.24), channel_id=1, source_target_pairs={{0,24},{1,25},{2,10},{3,11},{4,28},{5,29},{6,14},{7,15},{8,0},{9,1... | collective-permute-start | bytes 1572872 | tf_op jit(solution)/shard_map/ppermute | solution.py:40
  225.1 10.6 %collective-permute-done.45 = bf16[128,2048]{1,0:T(8,128)(2,1)S(1)} collective-permute-done((bf16[128,2048]{1,0:T(8,128)(2,1)S(1)}, bf16[128,2048]{1,0:T(8,128)(2,1)S(1)}, u32[]{:S(2)}, u32[]{:S(2)}) %collective-permute-start.45) | collective-permute-done | bytes 524320 | tf_op jit(solution)/shard_map/ppermute | solution.py:40
  235.7 6.6 %collective-permute-start.48 = (bf16[128,2048]{1,0:T(8,128)(2,1)S(1)}, bf16[128,2048]{1,0:T(8,128)(2,1)S(1)}, u32[]{:S(2)}, u32[]{:S(2)}) collective-permute-start(bf16[128,2048]{1,0:T(8,128)(2,1)S(1)} %get-tuple-element.15), channel_id=1, source_target_pairs={{0,24},{1,25},{2,10},{3,11},{4,28},{5,29},{6,14},{7,15},{8,0},{9,1... | collective-permute-start | bytes 1572872 | tf_op jit(solution)/shard_map/ppermute | solution.py:40
  246.3 7.2 %collective-permute-done.48 = bf16[128,2048]{1,0:T(8,128)(2,1)S(1)} collective-permute-done((bf16[128,2048]{1,0:T(8,128)(2,1)S(1)}, bf16[128,2048]{1,0:T(8,128)(2,1)S(1)}, u32[]{:S(2)}, u32[]{:S(2)}) %collective-permute-start.48) | collective-permute-done | bytes 524320 | tf_op jit(solution)/shard_map/ppermute | solution.py:40
  253.5 4.3 %collective-permute-start.25 = (bf16[128,2048]{1,0:T(8,128)(2,1)S(1)}, bf16[128,2048]{1,0:T(8,128)(2,1)S(1)}, u32[]{:S(2)}, u32[]{:S(2)}) collective-permute-start(bf16[128,2048]{1,0:T(8,128)(2,1)S(1)} %add_convert_fusion.14), channel_id=1, source_target_pairs={{0,24},{1,25},{2,10},{3,11},{4,28},{5,29},{6,14},{7,15},{8,0},{9,1... | collective-permute-start | bytes 1572872 | tf_op jit(solution)/shard_map/ppermute | solution.py:40
  257.8 12.1 %collective-permute-done.47 = bf16[128,2048]{1,0:T(8,128)(2,1)S(1)} collective-permute-done((bf16[128,2048]{1,0:T(8,128)(2,1)S(1)}, bf16[128,2048]{1,0:T(8,128)(2,1)S(1)}, u32[]{:S(2)}, u32[]{:S(2)}) %collective-permute-start.47) | collective-permute-done | bytes 524320 | tf_op jit(solution)/shard_map/ppermute | solution.py:40
  272.3 10.2 %collective-permute-done.49 = bf16[128,2048]{1,0:T(8,128)(2,1)S(1)} collective-permute-done((bf16[128,2048]{1,0:T(8,128)(2,1)S(1)}, bf16[128,2048]{1,0:T(8,128)(2,1)S(1)}, u32[]{:S(2)}, u32[]{:S(2)}) %collective-permute-start.49) | collective-permute-done | bytes 524320 | tf_op jit(solution)/shard_map/ppermute | solution.py:40
  283.9 2.7 collective-permute-done.26
  286.8 9.1 %collective-permute-done.50 = bf16[128,2048]{1,0:T(8,128)(2,1)S(1)} collective-permute-done((bf16[128,2048]{1,0:T(8,128)(2,1)S(1)}, bf16[128,2048]{1,0:T(8,128)(2,1)S(1)}, u32[]{:S(2)}, u32[]{:S(2)}) %collective-permute-start.50) | collective-permute-done | bytes 524320 | tf_op jit(solution)/shard_map/ppermute | solution.py:40
  (160 shorter events, 40.0 us)
Async XLA Ops:
  2.8 39.2 %collective-permute-start.4 = (bf16[128,2048]{1,0:T(8,128)(2,1)S(1)}, bf16[128,2048]{1,0:T(8,128)(2,1)S(1)}, u32[]{:S(2)}, u32[]{:S(2)}) collective-permute-start(bf16[128,2048]{1,0:T(8,128)(2,1)S(1)} %get-tuple-element.32.refs_4_), channel_id=1, source_target_pairs={{0,4},{1,5},{2,6},{3,7},{4,0},{5,1},{6,2},{7,3},{8,12},{9,13},{10,... | collective-permute-start | bytes 1572872 | tf_op jit(solution)/shard_map/ppermute | solution.py:40
  5.7 34.4 %collective-permute-start.5 = (bf16[128,2048]{1,0:T(8,128)(2,1)S(1)}, bf16[128,2048]{1,0:T(8,128)(2,1)S(1)}, u32[]{:S(2)}, u32[]{:S(2)}) collective-permute-start(bf16[128,2048]{1,0:T(8,128)(2,1)S(1)} %get-tuple-element.32.refs_4_), channel_id=1, source_target_pairs={{0,8},{1,9},{2,26},{3,27},{4,12},{5,13},{6,30},{7,31},{8,16},{9,17... | collective-permute-start | bytes 1572872 | tf_op jit(solution)/shard_map/ppermute | solution.py:40
  9.4 37.7 %collective-permute-start.28 = (bf16[128,2048]{1,0:T(8,128)(2,1)S(1)}, bf16[128,2048]{1,0:T(8,128)(2,1)S(1)}, u32[]{:S(2)}, u32[]{:S(2)}) collective-permute-start(bf16[128,2048]{1,0:T(8,128)(2,1)S(1)} %get-tuple-element.28.refs_4_), channel_id=1, source_target_pairs={{0,4},{1,5},{2,6},{3,7},{4,0},{5,1},{6,2},{7,3},{8,12},{9,13},{10,... | collective-permute-start | bytes 1572872 | tf_op jit(solution)/shard_map/ppermute | solution.py:40
  9.9 19.1 %collective-permute-start = (f32[16,128]{1,0:T(8,128)S(1)}, f32[16,128]{1,0:T(8,128)S(1)}, u32[]{:S(2)}, u32[]{:S(2)}) collective-permute-start(f32[16,128]{1,0:T(8,128)S(1)} %get-tuple-element.34), channel_id=1, source_target_pairs={{0,4},{1,5},{2,6},{3,7},{4,0},{5,1},{6,2},{7,3},{8,12},{9,13},{10,... | collective-permute-start | bytes 24584 | tf_op jit(solution)/shard_map/ppermute | solution.py:40
  40.2 16.8 %collective-permute-start.29 = (bf16[128,2048]{1,0:T(8,128)(2,1)S(1)}, bf16[128,2048]{1,0:T(8,128)(2,1)}, u32[]{:S(2)}, u32[]{:S(2)}) collective-permute-start(bf16[128,2048]{1,0:T(8,128)(2,1)S(1)} %get-tuple-element.28.refs_4_), channel_id=1, source_target_pairs={{0,8},{1,9},{2,26},{3,27},{4,12},{5,13},{6,30},{7,31},{8,16},{9,17... | collective-permute-start | bytes 1572872 | tf_op jit(solution)/shard_map/ppermute | solution.py:40
  40.2 16.8 %collective-permute-start.6 = (bf16[128,2048]{1,0:T(8,128)(2,1)S(1)}, bf16[128,2048]{1,0:T(8,128)(2,1)}, u32[]{:S(2)}, u32[]{:S(2)}) collective-permute-start(bf16[128,2048]{1,0:T(8,128)(2,1)S(1)} %collective-permute-done.5.refs_6_), channel_id=1, source_target_pairs={{0,4},{1,5},{2,6},{3,7},{4,0},{5,1},{6,2},{7,3},{8,12},{9,13},{10,... | collective-permute-start | bytes 1572872 | tf_op jit(solution)/shard_map/ppermute | solution.py:40
  42.0 22.2 %collective-permute-start.7 = (bf16[128,2048]{1,0:T(8,128)(2,1)S(1)}, bf16[128,2048]{1,0:T(8,128)(2,1)}, u32[]{:S(2)}, u32[]{:S(2)}) collective-permute-start(bf16[128,2048]{1,0:T(8,128)(2,1)S(1)} %collective-permute-done.5.refs_6_), channel_id=1, source_target_pairs={{0,8},{1,9},{2,26},{3,27},{4,12},{5,13},{6,30},{7,31},{8,16},{9,17... | collective-permute-start | bytes 1572872 | tf_op jit(solution)/shard_map/ppermute | solution.py:40
  42.0 22.2 %collective-permute-start.9 = (bf16[128,2048]{1,0:T(8,128)(2,1)S(1)}, bf16[128,2048]{1,0:T(8,128)(2,1)}, u32[]{:S(2)}, u32[]{:S(2)}) collective-permute-start(bf16[128,2048]{1,0:T(8,128)(2,1)S(1)} %collective-permute-done.5.refs_6_), channel_id=1, source_target_pairs={{0,2},{1,3},{2,0},{3,1},{4,6},{5,7},{6,4},{7,5},{8,10},{9,11},{10,... | collective-permute-start | bytes 1572872 | tf_op jit(solution)/shard_map/ppermute | solution.py:40
  47.1 22.0 %collective-permute-start.11 = (bf16[128,2048]{1,0:T(8,128)(2,1)S(1)}, bf16[128,2048]{1,0:T(8,128)(2,1)S(1)}, u32[]{:S(2)}, u32[]{:S(2)}) collective-permute-start(bf16[128,2048]{1,0:T(8,128)(2,1)S(1)} %collective-permute-done.4.refs_5_), channel_id=1, source_target_pairs={{0,1},{1,0},{2,3},{3,2},{4,5},{5,4},{6,7},{7,6},{8,9},{9,8},{10,11... | collective-permute-start | bytes 1572872 | tf_op jit(solution)/shard_map/ppermute | solution.py:40
  64.2 15.7 %collective-permute-start.33 = (bf16[128,2048]{1,0:T(8,128)(2,1)}, bf16[128,2048]{1,0:T(8,128)(2,1)S(1)}, u32[]{:S(2)}, u32[]{:S(2)}) collective-permute-start(bf16[128,2048]{1,0:T(8,128)(2,1)} %collective-permute-done.29.refs_6_), channel_id=1, source_target_pairs={{0,2},{1,3},{2,0},{3,1},{4,6},{5,7},{6,4},{7,5},{8,10},{9,11},{10,... | collective-permute-start | bytes 1572872 | tf_op jit(solution)/shard_map/ppermute | solution.py:40
  69.2 14.6 %collective-permute-start.36 = (bf16[128,2048]{1,0:T(8,128)(2,1)}, bf16[128,2048]{1,0:T(8,128)(2,1)}, u32[]{:S(2)}, u32[]{:S(2)}) collective-permute-start(bf16[128,2048]{1,0:T(8,128)(2,1)} %collective-permute-done.29.refs_6_), channel_id=1, source_target_pairs={{0,1},{1,0},{2,3},{3,2},{4,5},{5,4},{6,7},{7,6},{8,9},{9,8},{10,11... | collective-permute-start | bytes 1572872 | tf_op jit(solution)/shard_map/ppermute | solution.py:40
  71.5 20.3 %collective-permute-start.10 = (bf16[128,2048]{1,0:T(8,128)(2,1)}, bf16[128,2048]{1,0:T(8,128)(2,1)}, u32[]{:S(2)}, u32[]{:S(2)}) collective-permute-start(bf16[128,2048]{1,0:T(8,128)(2,1)} %collective-permute-done.6.refs_7_), channel_id=1, source_target_pairs={{0,2},{1,3},{2,0},{3,1},{4,6},{5,7},{6,4},{7,5},{8,10},{9,11},{10,... | collective-permute-start | bytes 1572872 | tf_op jit(solution)/shard_map/ppermute | solution.py:40
  76.2 15.6 %collective-permute-start.13 = (bf16[128,2048]{1,0:T(8,128)(2,1)}, bf16[128,2048]{1,0:T(8,128)(2,1)}, u32[]{:S(2)}, u32[]{:S(2)}) collective-permute-start(bf16[128,2048]{1,0:T(8,128)(2,1)} %collective-permute-done.6.refs_7_), channel_id=1, source_target_pairs={{0,1},{1,0},{2,3},{3,2},{4,5},{5,4},{6,7},{7,6},{8,9},{9,8},{10,11... | collective-permute-start | bytes 1572872 | tf_op jit(solution)/shard_map/ppermute | solution.py:40
  83.9 16.0 %collective-permute-start.32 = (bf16[128,2048]{1,0:T(8,128)(2,1)}, bf16[128,2048]{1,0:T(8,128)(2,1)}, u32[]{:S(2)}, u32[]{:S(2)}) collective-permute-start(bf16[128,2048]{1,0:T(8,128)(2,1)} %copy-done.4), channel_id=1, source_target_pairs={{0,8},{1,9},{2,26},{3,27},{4,12},{5,13},{6,30},{7,31},{8,16},{9,17... | collective-permute-start | bytes 1572872 | tf_op jit(solution)/shard_map/ppermute | solution.py:40
  96.3 51.9 %collective-permute-start.37 = (bf16[128,2048]{1,0:T(8,128)(2,1)S(1)}, bf16[128,2048]{1,0:T(8,128)(2,1)S(1)}, u32[]{:S(2)}, u32[]{:S(2)}) collective-permute-start(bf16[128,2048]{1,0:T(8,128)(2,1)S(1)} %copy-done.5), channel_id=1, source_target_pairs={{0,1},{1,0},{2,3},{3,2},{4,5},{5,4},{6,7},{7,6},{8,9},{9,8},{10,11... | collective-permute-start | bytes 1572872 | tf_op jit(solution)/shard_map/ppermute | solution.py:40
  99.8 49.0 %collective-permute-start.38 = (bf16[128,2048]{1,0:T(8,128)(2,1)S(1)}, bf16[128,2048]{1,0:T(8,128)(2,1)S(1)}, u32[]{:S(2)}, u32[]{:S(2)}) collective-permute-start(bf16[128,2048]{1,0:T(8,128)(2,1)S(1)} %copy-done.7), channel_id=1, source_target_pairs={{0,1},{1,0},{2,3},{3,2},{4,5},{5,4},{6,7},{7,6},{8,9},{9,8},{10,11... | collective-permute-start | bytes 1572872 | tf_op jit(solution)/shard_map/ppermute | solution.py:40
  100.9 48.0 %collective-permute-start.40 = (bf16[128,2048]{1,0:T(8,128)(2,1)S(1)}, bf16[128,2048]{1,0:T(8,128)(2,1)S(1)}, u32[]{:S(2)}, u32[]{:S(2)}) collective-permute-start(bf16[128,2048]{1,0:T(8,128)(2,1)S(1)} %copy-done.9), channel_id=1, source_target_pairs={{0,1},{1,0},{2,3},{3,2},{4,5},{5,4},{6,7},{7,6},{8,9},{9,8},{10,11... | collective-permute-start | bytes 1572872 | tf_op jit(solution)/shard_map/ppermute | solution.py:40
  100.9 48.0 %collective-permute-start.39 = (bf16[128,2048]{1,0:T(8,128)(2,1)}, bf16[128,2048]{1,0:T(8,128)(2,1)S(1)}, u32[]{:S(2)}, u32[]{:S(2)}) collective-permute-start(bf16[128,2048]{1,0:T(8,128)(2,1)} %collective-permute-done.32.refs_9_), channel_id=1, source_target_pairs={{0,1},{1,0},{2,3},{3,2},{4,5},{5,4},{6,7},{7,6},{8,9},{9,8},{10,11... | collective-permute-start | bytes 1572872 | tf_op jit(solution)/shard_map/ppermute | solution.py:40
  101.4 47.5 %collective-permute-start.41 = (bf16[128,2048]{1,0:T(8,128)(2,1)}, bf16[128,2048]{1,0:T(8,128)(2,1)S(1)}, u32[]{:S(2)}, u32[]{:S(2)}) collective-permute-start(bf16[128,2048]{1,0:T(8,128)(2,1)} %collective-permute-done.34.refs_11_), channel_id=1, source_target_pairs={{0,1},{1,0},{2,3},{3,2},{4,5},{5,4},{6,7},{7,6},{8,9},{9,8},{10,11... | collective-permute-start | bytes 1572872 | tf_op jit(solution)/shard_map/ppermute | solution.py:40
  148.3 48.0 %collective-permute-start.18 = (bf16[1024,2048]{1,0:T(8,128)(2,1)}, bf16[1024,2048]{1,0:T(8,128)(2,1)}, u32[]{:S(2)}, u32[]{:S(2)}) collective-permute-start(bf16[1024,2048]{1,0:T(8,128)(2,1)} %get-tuple-element.9), channel_id=1, source_target_pairs={{0,1},{1,0},{2,3},{3,2},{4,5},{5,4},{6,7},{7,6},{8,9},{9,8},{10,11... | collective-permute-start | bytes 12582920 | tf_op jit(solution)/shard_map/ppermute | solution.py:40
  198.8 14.8 %collective-permute-start.21 = (bf16[128,2048]{1,0:T(8,128)(2,1)S(1)}, bf16[128,2048]{1,0:T(8,128)(2,1)S(1)}, u32[]{:S(2)}, u32[]{:S(2)}) collective-permute-start(bf16[128,2048]{1,0:T(8,128)(2,1)S(1)} %get-tuple-element.21), channel_id=1, source_target_pairs={{0,2},{1,3},{2,0},{3,1},{4,6},{5,7},{6,4},{7,5},{8,10},{9,11},{10,... | collective-permute-start | bytes 1572872 | tf_op jit(solution)/shard_map/ppermute | solution.py:40
  200.7 41.9 %collective-permute-start.20 = (bf16[128,2048]{1,0:T(8,128)(2,1)S(1)}, bf16[128,2048]{1,0:T(8,128)(2,1)S(1)}, u32[]{:S(2)}, u32[]{:S(2)}) collective-permute-start(bf16[128,2048]{1,0:T(8,128)(2,1)S(1)} %get-tuple-element.22), channel_id=1, source_target_pairs={{0,2},{1,3},{2,0},{3,1},{4,6},{5,7},{6,4},{7,5},{8,10},{9,11},{10,... | collective-permute-start | bytes 1572872 | tf_op jit(solution)/shard_map/ppermute | solution.py:40
  204.9 19.7 %collective-permute-start.46 = (bf16[128,2048]{1,0:T(8,128)(2,1)S(1)}, bf16[128,2048]{1,0:T(8,128)(2,1)S(1)}, u32[]{:S(2)}, u32[]{:S(2)}) collective-permute-start(bf16[128,2048]{1,0:T(8,128)(2,1)S(1)} %get-tuple-element.16), channel_id=1, source_target_pairs={{0,24},{1,25},{2,10},{3,11},{4,28},{5,29},{6,14},{7,15},{8,0},{9,1... | collective-permute-start | bytes 1572872 | tf_op jit(solution)/shard_map/ppermute | solution.py:40
  211.5 24.2 %collective-permute-start.45 = (bf16[128,2048]{1,0:T(8,128)(2,1)S(1)}, bf16[128,2048]{1,0:T(8,128)(2,1)S(1)}, u32[]{:S(2)}, u32[]{:S(2)}) collective-permute-start(bf16[128,2048]{1,0:T(8,128)(2,1)S(1)} %get-tuple-element.17), channel_id=1, source_target_pairs={{0,2},{1,3},{2,0},{3,1},{4,6},{5,7},{6,4},{7,5},{8,10},{9,11},{10,... | collective-permute-start | bytes 1572872 | tf_op jit(solution)/shard_map/ppermute | solution.py:40
  215.3 27.4 %collective-permute-start.24 = (bf16[128,2048]{1,0:T(8,128)(2,1)S(1)}, bf16[128,2048]{1,0:T(8,128)(2,1)S(1)}, u32[]{:S(2)}, u32[]{:S(2)}) collective-permute-start(bf16[128,2048]{1,0:T(8,128)(2,1)S(1)} %get-tuple-element.24), channel_id=1, source_target_pairs={{0,24},{1,25},{2,10},{3,11},{4,28},{5,29},{6,14},{7,15},{8,0},{9,1... | collective-permute-start | bytes 1572872 | tf_op jit(solution)/shard_map/ppermute | solution.py:40
  223.1 21.2 %collective-permute-start.22 = (bf16[128,2048]{1,0:T(8,128)(2,1)S(1)}, bf16[128,2048]{1,0:T(8,128)(2,1)S(1)}, u32[]{:S(2)}, u32[]{:S(2)}) collective-permute-start(bf16[128,2048]{1,0:T(8,128)(2,1)S(1)} %get-tuple-element.23), channel_id=1, source_target_pairs={{0,4},{1,5},{2,6},{3,7},{4,0},{5,1},{6,2},{7,3},{8,12},{9,13},{10,... | collective-permute-start | bytes 1572872 | tf_op jit(solution)/shard_map/ppermute | solution.py:40
  224.6 46.1 %collective-permute-start.19 = (bf16[128,2048]{1,0:T(8,128)(2,1)S(1)}, bf16[128,2048]{1,0:T(8,128)(2,1)S(1)}, u32[]{:S(2)}, u32[]{:S(2)}) collective-permute-start(bf16[128,2048]{1,0:T(8,128)(2,1)S(1)} %get-tuple-element.19), channel_id=1, source_target_pairs={{0,4},{1,5},{2,6},{3,7},{4,0},{5,1},{6,2},{7,3},{8,12},{9,13},{10,... | collective-permute-start | bytes 1572872 | tf_op jit(solution)/shard_map/ppermute | solution.py:40
  235.7 17.7 %collective-permute-start.48 = (bf16[128,2048]{1,0:T(8,128)(2,1)S(1)}, bf16[128,2048]{1,0:T(8,128)(2,1)S(1)}, u32[]{:S(2)}, u32[]{:S(2)}) collective-permute-start(bf16[128,2048]{1,0:T(8,128)(2,1)S(1)} %get-tuple-element.15), channel_id=1, source_target_pairs={{0,24},{1,25},{2,10},{3,11},{4,28},{5,29},{6,14},{7,15},{8,0},{9,1... | collective-permute-start | bytes 1572872 | tf_op jit(solution)/shard_map/ppermute | solution.py:40
  242.7 15.1 %collective-permute-start.44 = (bf16[128,2048]{1,0:T(8,128)(2,1)S(1)}, bf16[128,2048]{1,0:T(8,128)(2,1)S(1)}, u32[]{:S(2)}, u32[]{:S(2)}) collective-permute-start(bf16[128,2048]{1,0:T(8,128)(2,1)S(1)} %get-tuple-element.18), channel_id=1, source_target_pairs={{0,2},{1,3},{2,0},{3,1},{4,6},{5,7},{6,4},{7,5},{8,10},{9,11},{10,... | collective-permute-start | bytes 1572872 | tf_op jit(solution)/shard_map/ppermute | solution.py:40
  242.8 29.5 %collective-permute-start.43 = (bf16[128,2048]{1,0:T(8,128)(2,1)S(1)}, bf16[128,2048]{1,0:T(8,128)(2,1)S(1)}, u32[]{:S(2)}, u32[]{:S(2)}) collective-permute-start(bf16[128,2048]{1,0:T(8,128)(2,1)S(1)} %get-tuple-element.14), channel_id=1, source_target_pairs={{0,4},{1,5},{2,6},{3,7},{4,0},{5,1},{6,2},{7,3},{8,12},{9,13},{10,... | collective-permute-start | bytes 1572872 | tf_op jit(solution)/shard_map/ppermute | solution.py:40
  244.3 25.5 %collective-permute-start.47 = (bf16[128,2048]{1,0:T(8,128)(2,1)S(1)}, bf16[128,2048]{1,0:T(8,128)(2,1)S(1)}, u32[]{:S(2)}, u32[]{:S(2)}) collective-permute-start(bf16[128,2048]{1,0:T(8,128)(2,1)S(1)} %add_convert_fusion.4), channel_id=1, source_target_pairs={{0,4},{1,5},{2,6},{3,7},{4,0},{5,1},{6,2},{7,3},{8,12},{9,13},{10,... | collective-permute-start | bytes 1572872 | tf_op jit(solution)/shard_map/ppermute | solution.py:40
  253.5 17.2 %collective-permute-start.25 = (bf16[128,2048]{1,0:T(8,128)(2,1)S(1)}, bf16[128,2048]{1,0:T(8,128)(2,1)S(1)}, u32[]{:S(2)}, u32[]{:S(2)}) collective-permute-start(bf16[128,2048]{1,0:T(8,128)(2,1)S(1)} %add_convert_fusion.14), channel_id=1, source_target_pairs={{0,24},{1,25},{2,10},{3,11},{4,28},{5,29},{6,14},{7,15},{8,0},{9,1... | collective-permute-start | bytes 1572872 | tf_op jit(solution)/shard_map/ppermute | solution.py:40
  (43 other events, 598.6 us)

commit v2 on v0

v2 whole, which is shorter than its diff:
```python
import functools

import jax
import jax.numpy as jnp
import numpy as np
from jax import lax
from jax.experimental import pallas as pl
from jax.experimental.pallas import tpu as pltpu
from jax.sharding import PartitionSpec as P

AXES = ("expert", "tensor")
CHUNK = 512
ROW_TILE = 16
LANES = 128


def chip_moves():
    def pairs(step):
        found = []
        for z in range(4):
            for x in range(2):
                for y in range(2):
                    for core in range(2):
                        to_z, to_x, to_y, to_core = step(z, x, y, core)
                        source = (z * 2 + x) * 4 + y * 2 + core
                        found.append((source, ((to_z % 4) * 2 + to_x) * 4 + to_y * 2 + to_core))
        return found

    return dict(
        ahead=pairs(lambda z, x, y, core: (z + 1 - 2 * y, x, y, core)),
        back=pairs(lambda z, x, y, core: (z - 1 + 2 * y, x, y, core)),
        x=pairs(lambda z, x, y, core: (z, 1 - x, y, core)),
        y=pairs(lambda z, x, y, core: (z, x, 1 - y, core)),
        core=pairs(lambda z, x, y, core: (z, x, y, 1 - core)),
    )


MOVES = chip_moves()


def move(array, name):
    return lax.ppermute(array, AXES, MOVES[name])


def add(*terms):
    total = terms[0].astype(jnp.float32)
    for term in terms[1:]:
        total = total + term.astype(jnp.float32)
    return total.astype(jnp.bfloat16)


def halves(array, core):
    half = array.shape[1] // 2
    return [
        lax.dynamic_slice_in_dim(array, side * half, half, 1) for side in (core, 1 - core)
    ]


def enter_kernel(backward, parts, sources, group, slots, half, *refs):
    count = 1 if backward else 2
    core_ref = refs[0]
    place_refs = refs[1 : 1 + parts]
    piece_refs = refs[1 + parts : 1 + parts + 2 * sources]
    weight_refs = refs[1 + parts + 2 * sources : 1 + parts + 2 * sources + count]
    if backward:
        factor_refs, (left_ref, right_ref) = refs[1 + parts + 2 * sources + count : -7], refs[-7:-5]
    else:
        left_ref, first_ref, second_ref = refs[-8:-5]
    block_ref, rows_ref, buffer_ref, sem_ref, weight_sem_ref = refs[-5:]
    places = [ref.at[k] for ref in place_refs for k in range(ref.shape[0])]
    step = pl.program_id(0)
    core = core_ref[0]
    experts = rows_ref.shape[0]
    depth = buffer_ref.shape[1]
    tokens = block_ref.shape[1] // sources
    span = group * tokens
    nt = (((1,), (1,)), ((), ()))

    def piece_copy(side, j):
        return pltpu.make_async_copy(
            piece_refs[side * sources + j].at[:, pl.ds(0, half)],
            block_ref.at[side, pl.ds(j * tokens, tokens)],
            sem_ref.at[side * sources + j],
        )

    def weight_copy(n, expert):
        slot = lax.rem(expert, depth)
        return pltpu.make_async_copy(
            weight_refs[n].at[expert], buffer_ref.at[n, slot], weight_sem_ref.at[n, slot]
        )

    @pl.when(step == 0)
    def _():
        for k in range(sources // group):
            for side in range(2):
                for j in range(k * group, (k + 1) * group):
                    piece_copy(side, j).start()
            if k == 0:
                for n in range(count):
                    weight_copy(n, 0).start()
        for expert in range(1, depth):
            for n in range(count):
                weight_copy(n, expert).start()
        for k in range(sources // group):
            for side in range(2):
                for j in range(k * group, (k + 1) * group):
                    piece_copy(side, j).wait()
                base = (core if side == 0 else 1 - core) * half
                for column in range(0, half, CHUNK):
                    block = block_ref[side, pl.ds(k * span, span), pl.ds(column, CHUNK)]
                    picked = jnp.dot(places[k][...], block, preferred_element_type=jnp.float32)
                    to = pl.multiple_of(base + column, CHUNK)
                    rows_ref[:, pl.ds(k * slots, slots), pl.ds(to, CHUNK)] = picked.astype(
                        jnp.bfloat16
                    ).reshape(experts, slots, CHUNK)

    for n in range(count):
        weight_copy(n, step).wait()
    rows = rows_ref[step]
    slot = lax.rem(step, depth)
    products = [
        lax.dot_general(rows, buffer_ref[n, slot], nt, preferred_element_type=jnp.float32)
        for n in range(count)
    ]
    if backward:
        start = 0
        for first_ref, second_ref in zip(factor_refs[0::2], factor_refs[1::2]):
            span_rows = pl.ds(start, first_ref.shape[1])
            product = products[0][start : start + first_ref.shape[1]]
            left_ref[0, span_rows] = (product * first_ref[0]).astype(jnp.bfloat16)
            right_ref[0, span_rows] = (product * second_ref[0]).astype(jnp.bfloat16)
            start += first_ref.shape[1]
    else:
        pre_gate, up_value = products
        sigmoid = jax.nn.sigmoid(pre_gate)
        activated = pre_gate * sigmoid
        left_ref[0] = (activated * up_value).astype(jnp.bfloat16)
        first_ref[0] = up_value * sigmoid * (1.0 + pre_gate * (1.0 - sigmoid))
        second_ref[0] = activated

    @pl.when(step + depth < experts)
    def _():
        for n in range(count):
            weight_copy(n, step + depth).start()


def enter(backward, core, places, pieces, weights, factors):
    experts, hidden, features = weights[0].shape
    sources = len(pieces) // 2
    tokens, half = pieces[0].shape[0], features // 2
    _, height, span = places[0].shape
    groups = sum(place.shape[0] for place in places)
    slots = height // experts
    total = groups * slots
    depth = min(3, experts)
    per_expert = pl.BlockSpec((1, total, hidden), lambda i, c: (i, 0, 0))
    in_specs = [pl.BlockSpec(place.shape, lambda i, c: (0, 0, 0)) for place in places]
    in_specs += [pl.BlockSpec(memory_space=pl.ANY)] * (2 * sources + len(weights))
    in_specs += [
        pl.BlockSpec((1,) + factor.shape[1:], lambda i, c: (i, 0, 0)) for factor in factors
    ]
    values = jax.ShapeDtypeStruct((experts, total, hidden), jnp.bfloat16)
    exact = jax.ShapeDtypeStruct((experts, total, hidden), jnp.float32)
    out_shape = [values, values] if backward else [values, exact, exact]
    return pl.pallas_call(
        functools.partial(enter_kernel, backward, len(places), sources, span // tokens, slots, half),
        grid_spec=pltpu.PrefetchScalarGridSpec(
            num_scalar_prefetch=1,
            grid=(experts,),
            in_specs=in_specs,
            out_specs=[per_expert] * len(out_shape),
            scratch_shapes=[
                pltpu.VMEM((2, sources * tokens, half), jnp.bfloat16),
                pltpu.VMEM((experts, total, features), jnp.bfloat16),
                pltpu.VMEM((len(weights), depth, hidden, features), jnp.bfloat16),
                pltpu.SemaphoreType.DMA((2 * sources,)),
                pltpu.SemaphoreType.DMA((len(weights), depth)),
            ],
        ),
        out_shape=out_shape,
        compiler_params=pltpu.CompilerParams(vmem_limit_bytes=40 * 1024 * 1024),
        cost_estimate=pl.CostEstimate(
            flops=2 * features * (len(weights) * experts * total * hidden + groups * height * span),
            bytes_accessed=len(weights) * experts * hidden * features * 2
            + 2 * sources * tokens * features,
            transcendentals=0,
        ),
        name="enter_backward" if backward else "enter_forward",
    )(core, *places, *pieces, *weights, *factors)


def leave_kernel(parts, count, *refs):
    place_refs = refs[1 : 1 + parts]
    value_refs = refs[1 + parts : -2 - count]
    weight_refs = refs[-2 - count : -2]
    out_ref, rows_ref = refs[-2:]
    step = pl.program_id(0)
    experts, total, half = rows_ref.shape
    _, span, height = place_refs[0].shape
    places = [ref.at[k] for ref in place_refs for k in range(ref.shape[0])]
    slots = height // experts
    width = out_ref.shape[1]
    each = refs[-3].shape[0]
    turns = experts // each

    @pl.when(step < turns)
    def _():
        for n in range(each):
            expert = step * each + n
            values = [
                jnp.concatenate([ref[expert] for ref in value_refs[m::count]], axis=0)
                for m in range(count)
            ]
            for column in range(0, half, CHUNK):
                columns = pl.ds(column, CHUNK)
                result = sum(
                    jnp.dot(value, ref[n, :, columns], preferred_element_type=jnp.float32)
                    for value, ref in zip(values, weight_refs)
                )
                rows_ref[expert, :, columns] = result.astype(jnp.bfloat16)

    @pl.when(step >= turns)
    def _():
        base = (step - turns) * width
        for column in range(0, width, CHUNK // 2):
            columns = pl.ds(pl.multiple_of(base + column, CHUNK // 2), CHUNK // 2)
            for k in range(len(places)):
                rows = rows_ref[:, pl.ds(k * slots, slots), columns].reshape(height, CHUNK // 2)
                out_ref[pl.ds(k * span, span), pl.ds(column, CHUNK // 2)] = jnp.dot(
                    places[k][...], rows, preferred_element_type=jnp.float32
                ).astype(jnp.bfloat16)


def leave(side, places, values, weights):
    experts, hidden, features = weights[0].shape
    _, span, height = places[0].shape
    groups = sum(place.shape[0] for place in places)
    total = groups * (height // experts)
    half = features // 2
    width = half // 2
    each = 2 if experts % 2 == 0 else 1
    turns = experts // each
    whole = lambda shape: pl.BlockSpec(shape, lambda i, s: (0,) * len(shape))
    return pl.pallas_call(
        functools.partial(leave_kernel, len(places), len(weights)),
        grid_spec=pltpu.PrefetchScalarGridSpec(
            num_scalar_prefetch=1,
            grid=(turns + half // width,),
            in_specs=[whole(array.shape) for array in list(places) + list(values)]
            + [
                pl.BlockSpec(
                    (each, hidden, half), lambda i, s: (jnp.minimum(i, turns - 1), 0, s[0])
                )
            ]
            * len(weights),
            out_specs=pl.BlockSpec(
                (groups * span, width), lambda i, s: (0, jnp.maximum(i - turns, 0))
            ),
            scratch_shapes=[pltpu.VMEM((experts, total, half), jnp.bfloat16)],
        ),
        out_shape=jax.ShapeDtypeStruct((groups * span, half), jnp.bfloat16),
        compiler_params=pltpu.CompilerParams(vmem_limit_bytes=40 * 1024 * 1024),
        cost_estimate=pl.CostEstimate(
            flops=2 * half * (len(weights) * experts * total * hidden + groups * height * span),
            bytes_accessed=len(weights) * experts * hidden * half * 2 + 2 * groups * span * half,
            transcendentals=0,
        ),
        name="leave_forward" if len(weights) == 1 else "leave_backward",
    )(side, *places, *values, *weights)


def choice_columns(expert_ids, gate_probs):
    columns = jnp.concatenate([expert_ids.astype(jnp.float32), gate_probs], axis=1)
    columns = jnp.pad(columns, ((0, 0), (0, LANES - columns.shape[1])))
    return columns.astype(jnp.bfloat16)


def route_kernel(sources, group, capacity, *refs):
    first_ref = refs[0]
    choice_refs = refs[1 : 1 + sources]
    ids_ref, probs_ref, rows_ref, earlier_ref, expert_ref, slot_ref = refs[1 + sources : 7 + sources]
    place_ref, place_prob_ref, place_t_ref, place_t_prob_ref = refs[7 + sources :]
    tokens = earlier_ref.shape[0]
    dot = functools.partial(jnp.dot, preferred_element_type=jnp.float32)
    sought = expert_ref[...] + first_ref[0].astype(jnp.float32)
    for j in range(sources):
        k, s = divmod(j, group)
        choice = choice_refs[j][...]
        match = dot(choice, ids_ref[...]) == sought
        weight = jnp.where(match, dot(choice, probs_ref[...]), 0.0).astype(jnp.bfloat16)
        chosen = dot(jnp.where(match, 1.0, 0.0).astype(jnp.bfloat16), rows_ref[...])
        weight = dot(weight, rows_ref[...])
        position = dot(earlier_ref[...], chosen.astype(jnp.bfloat16)) + float(s * capacity)
        here = (chosen > 0.5) & (position == slot_ref[...])
        plain = jnp.where(here, 1.0, 0.0)
        weighted = jnp.where(here, weight, 0.0)
        span = pl.ds(s * tokens, tokens)
        place_t_ref[k, span, :] = plain.astype(jnp.bfloat16)
        place_t_prob_ref[k, span, :] = weighted.astype(jnp.bfloat16)
        place_ref[k, :, span] = plain.T.astype(jnp.bfloat16)
        place_prob_ref[k, :, span] = weighted.T.astype(jnp.bfloat16)


def route(first, choices, column, top, experts, capacity, group):
    sources, tokens = len(choices), choices[0].shape[0]
    groups = sources // group
    slots = -(-group * capacity // ROW_TILE) * ROW_TILE
    height, span = experts * slots, group * tokens
    lanes = np.arange(top * experts)
    rows = np.arange(height)
    columns = np.arange(LANES)[:, None]
    tables = [
        (columns == lanes // experts),
        (columns == lanes // experts + top),
        (lanes[:, None] % experts == rows // slots),
        (np.arange(tokens)[:, None] > np.arange(tokens)),
    ]
    tables = [jnp.asarray(table.astype(np.float32), jnp.bfloat16) for table in tables]
    tables += [
        jnp.asarray((lanes % experts).astype(np.float32)[None]),
        jnp.asarray((rows % slots).astype(np.float32)[None]),
    ]
    whole = lambda shape: pl.BlockSpec(shape, lambda i, f: (0,) * len(shape))
    by_row = jax.ShapeDtypeStruct((groups, height, span), jnp.bfloat16)
    by_token = jax.ShapeDtypeStruct((groups, span, height), jnp.bfloat16)
    out_shape = [by_row, by_row, by_token, by_token]
    return pl.pallas_call(
        functools.partial(route_kernel, sources, group, capacity),
        grid_spec=pltpu.PrefetchScalarGridSpec(
            num_scalar_prefetch=1,
            grid=(1,),
            in_specs=[pl.BlockSpec((tokens, LANES), lambda i, f: (0, column))] * sources
            + [whole(table.shape) for table in tables],
            out_specs=[whole(shape.shape) for shape in out_shape],
        ),
        out_shape=out_shape,
        compiler_params=pltpu.CompilerParams(vmem_limit_bytes=32 * 1024 * 1024),
        name="route",
    )(first, *choices, *tables)


def body(fast, tokens, cotangent, expert_ids, gate_probs, w_gate, w_up, w_down):
    tok_count, features = tokens.shape
    top = expert_ids.shape[1]
    expert_devs = lax.axis_size("expert")
    local_experts = w_gate.shape[0]
    capacity = max(2, 9 * tok_count * top // (8 * local_experts * expert_devs))
    group = max(1, expert_devs // 4)
    half = features // 2
    first = (lax.axis_index("expert") * local_experts).astype(jnp.int32).reshape(1)
    routed = functools.partial(
        route, first, top=top, experts=local_experts, capacity=capacity, group=group
    )
    own_choices = choice_columns(expert_ids, gate_probs)
    if fast:
        return exchange(
            routed, own_choices, tokens, cotangent, w_gate, w_up, w_down
        )

    def split(array):
        blocks = lax.all_gather(array, "expert")
        return [
            blocks[j, :, side * half : (side + 1) * half]
            for side in range(2)
            for j in range(expert_devs)
        ]

    choices = lax.all_gather(own_choices, "expert")
    place, place_prob, place_t, place_t_prob = routed([choices[j] for j in range(expert_devs)], 0)
    zero = jnp.zeros((1,), jnp.int32)
    hidden, *factors = enter(False, zero, [place], split(tokens), (w_gate, w_up), ())
    values = enter(True, zero, [place_prob], split(cotangent), (w_down,), factors)

    def total(table, values, weights):
        partial = jnp.concatenate(
            [leave(zero + side, [table], values, weights) for side in range(2)], axis=1
        )
        own = lax.psum_scatter(partial, "expert", scatter_dimension=0, tiled=True)
        return lax.psum(own, "tensor")

    return total(place_t_prob, (hidden,), (w_down,)), total(place_t, values, (w_gate, w_up))


def exchange(routed, own_choices, tokens, cotangent, w_gate, w_up, w_down):
    half = tokens.shape[1] // 2
    core = lax.axis_index("tensor") % 2
    mine = core.astype(jnp.int32).reshape(1)
    order = ("q0", "r0", "q1", "r1", "q2", "r2", "q3", "r3")

    def phase(live, moves, far=(), **made):
        moved = {name: move(live[old], how) for name, (old, how) in moves.items()}
        moved.update({name + "_far": move(live[name], "core") for name in far})
        return lax.optimization_barrier({**live, **moved, **made})

    def pieces(live, kind, names):
        return [live[kind + name] for name in names] + [live[kind + name + "_far"] for name in names]

    def enter_tokens(live, names):
        tables = live["near" if names is near else "late"]
        return enter(False, live["mine"], tables[:1], pieces(live, "t", names), (w_gate, w_up), ())

    near, late = order[:4], order[4:]
    tq0, tq0_far = halves(tokens, core)
    live = dict(mine=mine, tq0=jnp.concatenate([tq0, own_choices], axis=1), tq0_far=tq0_far)
    cq0, cq0_far = halves(cotangent, core)
    live = phase(live, dict(tq1=("tq0", "ahead"), tr0=("tq0", "x")), cq0=cq0, cq0_far=cq0_far)
    live = phase(
        live,
        dict(tq2=("tq1", "ahead"), tr1=("tq1", "x"), tq3=("tq1", "y")),
        far=("tr0", "tq1"),
    )
    tables = routed([live["t" + name] for name in near], half // LANES)
    live = phase(live, {}, far=("tr1",), near=tables)
    live = phase(
        live,
        dict(tr2=("tq2", "x"), tr3=("tr1", "y"), cq1=("cq0", "ahead")),
        far=("tq2", "tq3"),
        near_values=enter_tokens(live, near),
    )
    tables = routed([live["t" + name] for name in late], half // LANES)
    live = phase(live, {}, far=("tr2", "tr3"), late=tables)
    live = phase(
        live,
        dict(cq2=("cq1", "ahead"), cr1=("cq1", "x"), cq3=("cq1", "y")),
        far=("cq1",),
        late_values=enter_tokens(live, late),
    )
    live = {name: value for name, value in live.items() if name[0] != "t"}

    def leave_tokens(live, side):
        tables = [live["near"][3], live["late"][3]]
        return leave(side, tables, [live["near_values"][0], live["late_values"][0]], (w_down,))

    live = phase(
        live,
        dict(cr0=("cq0", "x"), cr2=("cr1", "ahead"), cr3=("cr1", "y")),
        far=("cq2", "cr1"),
        o_far=leave_tokens(live, 1 - live["mine"]),
    )
    live = phase(
        live,
        dict(o_new=("o_far", "core")),
        far=("cq3", "cr0", "cr2", "cr3"),
        o_near=leave_tokens(live, live["mine"]),
    )
    live.update(merge("o", live.pop("o_new"), live.pop("o_near")))
    del live["o_far"]
    live = lax.optimization_barrier(live)
    place_t = [live["near"][2], live["late"][2]]
    values = enter(
        True,
        live["mine"],
        [live["near"][1], live["late"][1]],
        pieces(live, "c", order),
        (w_down,),
        list(live["near_values"][1:]) + list(live["late_values"][1:]),
    )
    live = {name: value for name, value in live.items() if name[0] in "mo"}
    live = phase(
        live, dict(y=("or3", "y"), z=("or2", "back"), x=("or0", "x")), values=tuple(values)
    )
    live["or1"] = add(live["or1"], live["y"], live["z"])
    g_far = leave(1 - live["mine"], place_t, live["values"], (w_gate, w_up))
    live = phase(
        live, dict(y1=("oq3", "y"), x1=("or1", "x"), z1=("oq2", "back")), g_far=g_far
    )
    live["oq1"] = add(live["oq1"], live["y1"], live["x1"], live["z1"])
    g_near = leave(live["mine"], place_t, live["values"], (w_gate, w_up))
    live = phase(live, dict(g_new=("g_far", "core"), z2=("oq1", "back")), g_near=g_near)
    own = add(live["oq0"], live["x"], live["z2"])
    live = dict(own=own, **merge("g", live["g_new"], live["g_near"]))
    live = phase(live, dict(y=("gr3", "y"), z=("gr2", "back"), x=("gr0", "x")))
    live["gr1"] = add(live["gr1"], live["y"], live["z"])
    live = phase(live, dict(y1=("gq3", "y"), x1=("gr1", "x"), z1=("gq2", "back")))
    live["gq1"] = add(live["gq1"], live["y1"], live["x1"], live["z1"])
    live = phase(live, dict(z2=("gq1", "back"), far=("own", "y")))
    mixed = add(live["own"], live["far"])
    own = add(live["gq0"], live["x"], live["z2"])
    grad_tokens = add(own, move(own, "y"))
    return whole_rows(mixed, core), whole_rows(grad_tokens, core)


def merge(kind, arrived, own):
    rows = own.shape[0] // 8
    names = ("q0", "r0", "q1", "r1", "q2", "r2", "q3", "r3")
    return {
        kind + name: add(own[j * rows : (j + 1) * rows], arrived[j * rows : (j + 1) * rows])
        for j, name in enumerate(names)
    }


def whole_rows(own, core):
    far = move(own, "core")
    return jnp.concatenate([jnp.where(core == 0, own, far), jnp.where(core == 0, far, own)], axis=1)


def solution(mesh):
    fast = mesh.shape["expert"] == 8 and mesh.shape["tensor"] == 4
    return jax.shard_map(
        functools.partial(body, fast),
        mesh=mesh,
        in_specs=(
            P("expert", None),
            P("expert", None),
            P("expert", None),
            P("expert", None),
            P("expert", "tensor", None),
            P("expert", "tensor", None),
            P("expert", "tensor", None),
        ),
        out_specs=(P("expert", None), P("expert", None)),
        check_vma=False,
    )
```

time: 958 us -> 227 us (0.24)
  blocking collectives: 416 us -> 0 us
  waiting for transfers between devices: 333 us -> 71.6 us
  matrix products: 117 us -> 0 us
  Pallas kernels: 0 us -> 79.2 us
  starting transfers between devices: 5.82 us -> 52.2 us
  local copies, waits for them, and re-layouts: 42.9 us -> 10.8 us
  between operations: 14.5 us -> 1.15 us
  other arithmetic: 24.3 us -> 11.3 us
    all_to_all x1 -> x0, blocking collectives: 416 us -> none  [body(): lax.all_to_all(buffer, 'expert', split_axis=0, concat_axis=0, tiled=True)]
    reduce_scatter x1 -> x0, waiting for transfers between devices: 180 us -> none  [body(): lax.psum_scatter(results.astype(jnp.bfloat16), 'tensor', scatter_dimensio...]
    dot_general x11 -> x0, matrix products: 117 us -> none  [the longest x1 22.8 us: expert_work(): jnp.einsum('sich,ihd->sicd', grad_gate, w_gate, preferred_element_type=jn...]
    all_to_all x1 -> x0, waiting for transfers between devices: 104 us -> none  [body(): lax.all_to_all(reduced, 'expert', split_axis=0, concat_axis=0, tiled=True)]
    pallas_call x0 -> x9, Pallas kernels: none -> 79.2 us  [the longest x3 39.7 us: enter(): pl.pallas_call(functools.partial(enter_kernel, backward, len(places), sou...]
    ppermute x0 -> x48, waiting for transfers between devices: none -> 71.6 us  [move(): return lax.ppermute(array, AXES, MOVES[name])]
    ppermute x0 -> x48, starting transfers between devices: none -> 52.2 us  [move(): return lax.ppermute(array, AXES, MOVES[name])]
    psum x1 -> x0, waiting for transfers between devices: 49.8 us -> none  [body(): lax.psum(output_part.astype(jnp.bfloat16), 'tensor').astype(jnp.float32)]
  transfers between devices with their start and end apart: 3 -> 48, of which waited for: 3 -> 22; matrix products, arithmetic and copies ran while one was open for 0% -> 2% of each run, Pallas kernels for 0% -> 35%
where the time goes in v2:
time: 227 us; the launch traced here: 226 us
  Pallas kernels  79.2 us (35%)
  waiting for transfers between devices  71.6 us (32%)
  starting transfers between devices  52.2 us (23%)
  other arithmetic  11.3 us (5%)
  local copies, waits for them, and re-layouts  10.8 us (5%)
    ppermute x48, waiting for transfers between devices, move(): return lax.ppermute(array, AXES, MOVES[name])  71.6 us
    ppermute x48, starting transfers between devices, move(): return lax.ppermute(array, AXES, MOVES[name])  52.2 us
    pallas_call x3, Pallas kernels, enter(): pl.pallas_call(functools.partial(enter_kernel, backward, len(places), sou...  39.7 us
    pallas_call x4, Pallas kernels, leave(): pl.pallas_call(functools.partial(leave_kernel, len(places), len(weights))...  36.7 us
    convert_element_type x10, other arithmetic, add(): return total.astype(jnp.bfloat16)  7.62 us
    unnamed x38, local copies, waits for them, and re-layouts  6.3 us
  transfers between devices with their start and end apart: 48, of which 22 were waited for; matrix products, arithmetic and copies ran while one was open for 2% of the time, Pallas kernels for 35%

profile of v2, /device:TPU:0, one launch (start us, length us, event | category | flops | bytes accessed | tf_op | source)
XLA Modules:
  0.0 226.3 jit_solution(1486717276404806925)
XLA Ops:
  2.2 2.1 constant_dynamic-slice_fusion
  4.4 3.1 %collective-permute-start = (bf16[128,2176]{1,0:T(8,128)(2,1)S(1)}, bf16[128,2176]{1,0:T(8,128)(2,1)S(1)}, u32[]{:S(2)}, u32[]{:S(2)}) collective-permute-start(bf16[128,2176]{1,0:T(8,128)(2,1)S(1)} %fusion.1.refs_1_.refs_2_), channel_id=1, source_target_pairs={{0,8},{1,9},{2,26},{3,27},{4,12},{5,13},{6,30},{7,31},{8,16},{9,17... | collective-permute-start | bytes 1671176 | tf_op jit(solution)/shard_map/ppermute | solution.py:42
  9.0 2.3 %constant_dynamic-slice_fusion.2 = (bf16[128,2048]{1,0:T(8,128)(2,1)}, bf16[128,2048]{1,0:T(8,128)(2,1)}) fusion(bf16[128,4096]{1,0:T(8,128)(2,1)} %param.20, s32[]{:T(128)S(6)} %select_n.38, s32[]{:T(128)S(6)} %select_n.37), kind=kLoop, calls=%fused_computation.37 | loop fusion | bytes 2097160 | tf_op jit(solution)/shard_map/dynamic_slice | solution.py:55
  11.3 10.9 %collective-permute-done.refs_3_.refs_4_ = bf16[128,2176]{1,0:T(8,128)(2,1)S(1)} collective-permute-done((bf16[128,2176]{1,0:T(8,128)(2,1)S(1)}, bf16[128,2176]{1,0:T(8,128)(2,1)S(1)}, u32[]{:S(2)}, u32[]{:S(2)}) %collective-permute-start) | collective-permute-done | bytes 557088 | tf_op jit(solution)/shard_map/ppermute | solution.py:42
  23.1 4.0 %collective-permute-start.4 = (bf16[128,2176]{1,0:T(8,128)(2,1)S(1)}, bf16[128,2176]{1,0:T(8,128)(2,1)S(1)}, u32[]{:S(2)}, u32[]{:S(2)}) collective-permute-start(bf16[128,2176]{1,0:T(8,128)(2,1)S(1)} %collective-permute-done.refs_3_.refs_4_), channel_id=1, source_target_pairs={{0,2},{1,3},{2,0},{3,1},{4,6},{5,7},{6,4},{7,5},{8,10},{9,11},{10,... | collective-permute-start | bytes 1671176 | tf_op jit(solution)/shard_map/ppermute | solution.py:42
  29.5 9.5 %collective-permute-done.3.refs_1_.refs_2_ = bf16[128,2176]{1,0:T(8,128)(2,1)S(1)} collective-permute-done((bf16[128,2176]{1,0:T(8,128)(2,1)S(1)}, bf16[128,2176]{1,0:T(8,128)(2,1)S(1)}, u32[]{:S(2)}, u32[]{:S(2)}) %collective-permute-start.3) | collective-permute-done | bytes 557088 | tf_op jit(solution)/shard_map/ppermute | solution.py:42
  50.1 15.1 %enter_forward.2 = (bf16[8,96,224]{2,1,0:T(8,128)(2,1)S(1)}, f32[8,96,224]{2,1,0:T(8,128)S(1)}, f32[8,96,224]{2,1,0:T(8,128)S(1)}) custom-call(s32[1]{0:T(128)} %bitcast.refs_0_, bf16[2,384,256]{2,1,0:T(8,128)(2,1)S(1)} %get-tuple-element.271.refs_1_, bf16[128,2176]{1,0:T(8,128)(2,1)S(1)} %fusion.1.refs_1_.refs_2_, ...), custom_call_target="tpu_custom_call" | custom-call | flops 4429185024 | bytes 33554432 | tf_op jit(solution)/shard_map/enter_forward/pallas_call | solution.py:165
  68.3 2.4 %collective-permute-start.17 = (bf16[128,2048]{1,0:T(8,128)(2,1)S(1)}, bf16[128,2048]{1,0:T(8,128)(2,1)S(1)}, u32[]{:S(2)}, u32[]{:S(2)}) collective-permute-start(bf16[128,2048]{1,0:T(8,128)(2,1)S(1)} %collective-permute-done.8.refs_5_), channel_id=1, source_target_pairs={{0,2},{1,3},{2,0},{3,1},{4,6},{5,7},{6,4},{7,5},{8,10},{9,11},{10,... | collective-permute-start | bytes 1572872 | tf_op jit(solution)/shard_map/ppermute | solution.py:42
  71.2 13.2 %enter_forward.3 = (bf16[8,96,224]{2,1,0:T(8,128)(2,1)S(1)}, f32[8,96,224]{2,1,0:T(8,128)S(1)}, f32[8,96,224]{2,1,0:T(8,128)S(1)}) custom-call(s32[1]{0:T(128)} %bitcast.refs_0_, bf16[2,384,256]{2,1,0:T(8,128)(2,1)S(1)} %get-tuple-element.311.refs_1_, bf16[128,2176]{1,0:T(8,128)(2,1)S(1)} %collective-permute-done.3.refs_1_.refs_2_, ...), custom_call_target="tpu_custom_call" | custom-call | flops 4429185024 | bytes 33554432 | tf_op jit(solution)/shard_map/enter_forward/pallas_call | solution.py:165
  86.3 1.7 collective-permute-start.22
  88.0 1.7 collective-permute-start.23
  89.8 7.9 %leave_forward.2 = bf16[1024,2048]{1,0:T(8,128)(2,1)S(1)} custom-call(s32[1]{0:T(128)S(6)} %sub.11.refs_0_, bf16[2,256,384]{2,1,0:T(8,128)(2,1)S(1)} %get-tuple-element.374.refs_1_, bf16[2,256,384]{2,1,0:T(8,128)(2,1)S(1)} %get-tuple-element.367.refs_2_, bf16[8,96,224]{2,1,0:T(8,128)(2,1)S(1)} %get-tuple-element.375.refs_3_, ...), custom_call_target="tpu_custom_call" | custom-call | flops 3019898880 | bytes 11534336 | tf_op jit(solution)/shard_map/leave_forward/pallas_call | solution.py:244
  98.9 3.3 %collective-permute-done.22.refs_8_ = bf16[128,2048]{1,0:T(8,128)(2,1)S(1)} collective-permute-done((bf16[128,2048]{1,0:T(8,128)(2,1)S(1)}, bf16[128,2048]{1,0:T(8,128)(2,1)S(1)}, u32[]{:S(2)}, u32[]{:S(2)}) %collective-permute-start.22) | collective-permute-done | bytes 524320 | tf_op jit(solution)/shard_map/ppermute | solution.py:42
  103.3 7.9 %leave_forward.3 = bf16[1024,2048]{1,0:T(8,128)(2,1)S(1)} custom-call(s32[1]{0:T(128)} %bitcast.refs_0_, bf16[2,256,384]{2,1,0:T(8,128)(2,1)S(1)} %get-tuple-element.374.refs_1_, bf16[2,256,384]{2,1,0:T(8,128)(2,1)S(1)} %get-tuple-element.367.refs_2_, bf16[8,96,224]{2,1,0:T(8,128)(2,1)S(1)} %get-tuple-element.375.refs_3_, ...), custom_call_target="tpu_custom_call" | custom-call | flops 3019898880 | bytes 11534336 | tf_op jit(solution)/shard_map/leave_forward/pallas_call | solution.py:244
  112.6 4.1 %add_convert_fusion.16 = (bf16[128,2048]{1,0:T(8,128)(2,1)S(1)}, bf16[128,2048]{1,0:T(8,128)(2,1)S(1)}, bf16[128,2048]{1,0:T(8,128)(2,1)S(1)}, bf16[128,2048]{1,...) fusion(bf16[1024,2048]{1,0:T(8,128)(2,1)} %collective-permute-d, ...), kind=kLoop, calls=%fused_computation.20 | loop fusion | flops 8388608 | bytes 12582912 | tf_op jit(solution)/shard_map/convert_element_type | solution.py:49
  118.6 2.1 collective-permute-start.31
  120.7 11.4 %enter_backward.1 = (bf16[8,192,224]{2,1,0:T(8,128)(2,1)S(1)}, bf16[8,192,224]{2,1,0:T(8,128)(2,1)S(1)}) custom-call(s32[1]{0:T(128)} %bitcast.refs_0_, bf16[2,384,256]{2,1,0:T(8,128)(2,1)S(1)} %copy-done.8, bf16[2,384,256]{2,1,0:T(8,128)(2,1)S(1)} %copy-done.10, bf16[128,2048]{1,0:T(8,128)(2,1)S(1)} %copy-done.2, ...), custom_call_target="tpu_custom_call" | custom-call | flops 6039797760 | bytes 23068672 | tf_op jit(solution)/shard_map/enter_backward/pallas_call | solution.py:165
  134.0 2.3 %collective-permute-start.33 = (bf16[128,2048]{1,0:T(8,128)(2,1)}, bf16[128,2048]{1,0:T(8,128)(2,1)S(1)}, u32[]{:S(2)}, u32[]{:S(2)}) collective-permute-start(bf16[128,2048]{1,0:T(8,128)(2,1)} %get-tuple-element.447), channel_id=1, source_target_pairs={{0,2},{1,3},{2,0},{3,1},{4,6},{5,7},{6,4},{7,5},{8,10},{9,11},{10,... | collective-permute-start | bytes 1572872 | tf_op jit(solution)/shard_map/ppermute | solution.py:42
  137.7 10.4 %leave_backward.2 = bf16[1024,2048]{1,0:T(8,128)(2,1)S(1)} custom-call(s32[1]{0:T(128)S(6)} %sub.12.refs_0_, bf16[2,256,384]{2,1,0:T(8,128)(2,1)S(1)} %get-tuple-element.440.refs_1_, bf16[2,256,384]{2,1,0:T(8,128)(2,1)S(1)} %get-tuple-element.441.refs_2_, bf16[8,192,224]{2,1,0:T(8,128)(2,1)S(1)} %get-tuple-element.454.refs_3_, ...), custom_call_target="tpu_custom_call" | custom-call | flops 4429185024 | bytes 18874368 | tf_op jit(solution)/shard_map/leave_backward/pallas_call | solution.py:244
  148.6 3.5 %collective-permute-start.36 = (bf16[128,2048]{1,0:T(8,128)(2,1)S(1)}, bf16[128,2048]{1,0:T(8,128)(2,1)S(1)}, u32[]{:S(2)}, u32[]{:S(2)}) collective-permute-start(bf16[128,2048]{1,0:T(8,128)(2,1)S(1)} %add_convert_fusion.14), channel_id=1, source_target_pairs={{0,24},{1,25},{2,10},{3,11},{4,28},{5,29},{6,14},{7,15},{8,0},{9,1... | collective-permute-start | bytes 1572872 | tf_op jit(solution)/shard_map/ppermute | solution.py:42
  152.2 10.6 %leave_backward.3 = bf16[1024,2048]{1,0:T(8,128)(2,1)S(1)} custom-call(s32[1]{0:T(128)} %bitcast.refs_0_, bf16[2,256,384]{2,1,0:T(8,128)(2,1)S(1)} %get-tuple-element.440.refs_1_, bf16[2,256,384]{2,1,0:T(8,128)(2,1)S(1)} %get-tuple-element.441.refs_2_, bf16[8,192,224]{2,1,0:T(8,128)(2,1)S(1)} %get-tuple-element.454.refs_3_, ...), custom_call_target="tpu_custom_call" | custom-call | flops 4429185024 | bytes 18874368 | tf_op jit(solution)/shard_map/leave_backward/pallas_call | solution.py:244
  166.3 2.8 %collective-permute-start.38 = (bf16[128,2048]{1,0:T(8,128)(2,1)S(1)}, bf16[128,2048]{1,0:T(8,128)(2,1)S(1)}, u32[]{:S(2)}, u32[]{:S(2)}) collective-permute-start(bf16[128,2048]{1,0:T(8,128)(2,1)S(1)} %get-tuple-element.488), channel_id=1, source_target_pairs={{0,2},{1,3},{2,0},{3,1},{4,6},{5,7},{6,4},{7,5},{8,10},{9,11},{10,... | collective-permute-start | bytes 1572872 | tf_op jit(solution)/shard_map/ppermute | solution.py:42
  170.8 8.4 %collective-permute-done.37 = bf16[128,2048]{1,0:T(8,128)(2,1)S(1)} collective-permute-done((bf16[128,2048]{1,0:T(8,128)(2,1)S(1)}, bf16[128,2048]{1,0:T(8,128)(2,1)S(1)}, u32[]{:S(2)}, u32[]{:S(2)}) %collective-permute-start.37) | collective-permute-done | bytes 524320 | tf_op jit(solution)/shard_map/ppermute | solution.py:42
  183.9 2.1 collective-permute-start.41
  187.4 7.2 %collective-permute-done.40 = bf16[128,2048]{1,0:T(8,128)(2,1)S(1)} collective-permute-done((bf16[128,2048]{1,0:T(8,128)(2,1)S(1)}, bf16[128,2048]{1,0:T(8,128)(2,1)S(1)}, u32[]{:S(2)}, u32[]{:S(2)}) %collective-permute-start.40) | collective-permute-done | bytes 524320 | tf_op jit(solution)/shard_map/ppermute | solution.py:42
  194.5 1.8 collective-permute-done.41
  197.8 2.1 collective-permute-start.43
  201.6 7.6 %collective-permute-done.43 = bf16[128,2048]{1,0:T(8,128)(2,1)S(1)} collective-permute-done((bf16[128,2048]{1,0:T(8,128)(2,1)S(1)}, bf16[128,2048]{1,0:T(8,128)(2,1)S(1)}, u32[]{:S(2)}, u32[]{:S(2)}) %collective-permute-start.43) | collective-permute-done | bytes 524320 | tf_op jit(solution)/shard_map/ppermute | solution.py:42
  209.3 1.9 collective-permute-done.44
  211.4 2.1 collective-permute-start.46
  213.7 8.3 %collective-permute-done.46 = bf16[128,2048]{1,0:T(8,128)(2,1)S(1)} collective-permute-done((bf16[128,2048]{1,0:T(8,128)(2,1)S(1)}, bf16[128,2048]{1,0:T(8,128)(2,1)S(1)}, u32[]{:S(2)}, u32[]{:S(2)}) %collective-permute-start.46) | collective-permute-done | bytes 524320 | tf_op jit(solution)/shard_map/ppermute | solution.py:42
  222.2 1.9 collective-permute-done.47
  (131 shorter events, 49.6 us)
Async XLA Ops:
  4.4 17.7 %collective-permute-start = (bf16[128,2176]{1,0:T(8,128)(2,1)S(1)}, bf16[128,2176]{1,0:T(8,128)(2,1)S(1)}, u32[]{:S(2)}, u32[]{:S(2)}) collective-permute-start(bf16[128,2176]{1,0:T(8,128)(2,1)S(1)} %fusion.1.refs_1_.refs_2_), channel_id=1, source_target_pairs={{0,8},{1,9},{2,26},{3,27},{4,12},{5,13},{6,30},{7,31},{8,16},{9,17... | collective-permute-start | bytes 1671176 | tf_op jit(solution)/shard_map/ppermute | solution.py:42
  7.5 14.7 %collective-permute-start.1 = (bf16[128,2176]{1,0:T(8,128)(2,1)S(1)}, bf16[128,2176]{1,0:T(8,128)(2,1)S(1)}, u32[]{:S(2)}, u32[]{:S(2)}) collective-permute-start(bf16[128,2176]{1,0:T(8,128)(2,1)S(1)} %fusion.1.refs_1_.refs_2_), channel_id=1, source_target_pairs={{0,4},{1,5},{2,6},{3,7},{4,0},{5,1},{6,2},{7,3},{8,12},{9,13},{10,... | collective-permute-start | bytes 1671176 | tf_op jit(solution)/shard_map/ppermute | solution.py:42
  22.1 16.8 %collective-permute-start.3 = (bf16[128,2176]{1,0:T(8,128)(2,1)S(1)}, bf16[128,2176]{1,0:T(8,128)(2,1)S(1)}, u32[]{:S(2)}, u32[]{:S(2)}) collective-permute-start(bf16[128,2176]{1,0:T(8,128)(2,1)S(1)} %collective-permute-done.refs_3_.refs_4_), channel_id=1, source_target_pairs={{0,8},{1,9},{2,26},{3,27},{4,12},{5,13},{6,30},{7,31},{8,16},{9,17... | collective-permute-start | bytes 1671176 | tf_op jit(solution)/shard_map/ppermute | solution.py:42
  23.1 17.1 %collective-permute-start.4 = (bf16[128,2176]{1,0:T(8,128)(2,1)S(1)}, bf16[128,2176]{1,0:T(8,128)(2,1)S(1)}, u32[]{:S(2)}, u32[]{:S(2)}) collective-permute-start(bf16[128,2176]{1,0:T(8,128)(2,1)S(1)} %collective-permute-done.refs_3_.refs_4_), channel_id=1, source_target_pairs={{0,2},{1,3},{2,0},{3,1},{4,6},{5,7},{6,4},{7,5},{8,10},{9,11},{10,... | collective-permute-start | bytes 1671176 | tf_op jit(solution)/shard_map/ppermute | solution.py:42
  27.2 13.0 %collective-permute-start.5 = (bf16[128,2176]{1,0:T(8,128)(2,1)S(1)}, bf16[128,2176]{1,0:T(8,128)(2,1)S(1)}, u32[]{:S(2)}, u32[]{:S(2)}) collective-permute-start(bf16[128,2176]{1,0:T(8,128)(2,1)S(1)} %collective-permute-done.1.refs_2_.refs_3_), channel_id=1, source_target_pairs={{0,1},{1,0},{2,3},{3,2},{4,5},{5,4},{6,7},{7,6},{8,9},{9,8},{10,11... | collective-permute-start | bytes 1671176 | tf_op jit(solution)/shard_map/ppermute | solution.py:42
  27.2 15.0 %collective-permute-start.6 = (bf16[128,2176]{1,0:T(8,128)(2,1)S(1)}, bf16[128,2176]{1,0:T(8,128)(2,1)S(1)}, u32[]{:S(2)}, u32[]{:S(2)}) collective-permute-start(bf16[128,2176]{1,0:T(8,128)(2,1)S(1)} %collective-permute-done.refs_3_.refs_4_), channel_id=1, source_target_pairs={{0,4},{1,5},{2,6},{3,7},{4,0},{5,1},{6,2},{7,3},{8,12},{9,13},{10,... | collective-permute-start | bytes 1671176 | tf_op jit(solution)/shard_map/ppermute | solution.py:42
  44.5 20.8 %collective-permute-start.9 = (bf16[128,2176]{1,0:T(8,128)(2,1)S(1)}, bf16[128,2176]{1,0:T(8,128)(2,1)S(1)}, u32[]{:S(2)}, u32[]{:S(2)}) collective-permute-start(bf16[128,2176]{1,0:T(8,128)(2,1)S(1)} %collective-permute-done.3.refs_1_.refs_2_), channel_id=1, source_target_pairs={{0,1},{1,0},{2,3},{3,2},{4,5},{5,4},{6,7},{7,6},{8,9},{9,8},{10,11... | collective-permute-start | bytes 1671176 | tf_op jit(solution)/shard_map/ppermute | solution.py:42
  45.0 20.3 %collective-permute-start.11 = (bf16[128,2176]{1,0:T(8,128)(2,1)S(1)}, bf16[128,2176]{1,0:T(8,128)(2,1)S(1)}, u32[]{:S(2)}, u32[]{:S(2)}) collective-permute-start(bf16[128,2176]{1,0:T(8,128)(2,1)S(1)} %collective-permute-done.3.refs_1_.refs_2_), channel_id=1, source_target_pairs={{0,4},{1,5},{2,6},{3,7},{4,0},{5,1},{6,2},{7,3},{8,12},{9,13},{10,... | collective-permute-start | bytes 1671176 | tf_op jit(solution)/shard_map/ppermute | solution.py:42
  46.4 18.8 %collective-permute-start.10 = (bf16[128,2176]{1,0:T(8,128)(2,1)S(1)}, bf16[128,2176]{1,0:T(8,128)(2,1)S(1)}, u32[]{:S(2)}, u32[]{:S(2)}) collective-permute-start(bf16[128,2176]{1,0:T(8,128)(2,1)S(1)} %collective-permute-done.4.refs_3_.refs_4_), channel_id=1, source_target_pairs={{0,1},{1,0},{2,3},{3,2},{4,5},{5,4},{6,7},{7,6},{8,9},{9,8},{10,11... | collective-permute-start | bytes 1671176 | tf_op jit(solution)/shard_map/ppermute | solution.py:42
  46.4 18.8 %collective-permute-start.12 = (bf16[128,2176]{1,0:T(8,128)(2,1)S(1)}, bf16[128,2176]{1,0:T(8,128)(2,1)S(1)}, u32[]{:S(2)}, u32[]{:S(2)}) collective-permute-start(bf16[128,2176]{1,0:T(8,128)(2,1)S(1)} %collective-permute-done.6.refs_4_.refs_5_), channel_id=1, source_target_pairs={{0,2},{1,3},{2,0},{3,1},{4,6},{5,7},{6,4},{7,5},{8,10},{9,11},{10,... | collective-permute-start | bytes 1671176 | tf_op jit(solution)/shard_map/ppermute | solution.py:42
  47.0 18.2 %collective-permute-start.8 = (bf16[128,2048]{1,0:T(8,128)(2,1)}, bf16[128,2048]{1,0:T(8,128)(2,1)S(1)}, u32[]{:S(2)}, u32[]{:S(2)}) collective-permute-start(bf16[128,2048]{1,0:T(8,128)(2,1)} %get-tuple-element.417.refs_3_), channel_id=1, source_target_pairs={{0,8},{1,9},{2,26},{3,27},{4,12},{5,13},{6,30},{7,31},{8,16},{9,17... | collective-permute-start | bytes 1572872 | tf_op jit(solution)/shard_map/ppermute | solution.py:42
  68.1 16.3 %collective-permute-start.15 = (bf16[128,2048]{1,0:T(8,128)(2,1)S(1)}, bf16[128,2048]{1,0:T(8,128)(2,1)S(1)}, u32[]{:S(2)}, u32[]{:S(2)}) collective-permute-start(bf16[128,2048]{1,0:T(8,128)(2,1)S(1)} %collective-permute-done.8.refs_5_), channel_id=1, source_target_pairs={{0,1},{1,0},{2,3},{3,2},{4,5},{5,4},{6,7},{7,6},{8,9},{9,8},{10,11... | collective-permute-start | bytes 1572872 | tf_op jit(solution)/shard_map/ppermute | solution.py:42
  68.3 16.2 %collective-permute-start.16 = (bf16[128,2048]{1,0:T(8,128)(2,1)S(1)}, bf16[128,2048]{1,0:T(8,128)(2,1)S(1)}, u32[]{:S(2)}, u32[]{:S(2)}) collective-permute-start(bf16[128,2048]{1,0:T(8,128)(2,1)S(1)} %collective-permute-done.8.refs_5_), channel_id=1, source_target_pairs={{0,8},{1,9},{2,26},{3,27},{4,12},{5,13},{6,30},{7,31},{8,16},{9,17... | collective-permute-start | bytes 1572872 | tf_op jit(solution)/shard_map/ppermute | solution.py:42
  68.3 16.2 %collective-permute-start.17 = (bf16[128,2048]{1,0:T(8,128)(2,1)S(1)}, bf16[128,2048]{1,0:T(8,128)(2,1)S(1)}, u32[]{:S(2)}, u32[]{:S(2)}) collective-permute-start(bf16[128,2048]{1,0:T(8,128)(2,1)S(1)} %collective-permute-done.8.refs_5_), channel_id=1, source_target_pairs={{0,2},{1,3},{2,0},{3,1},{4,6},{5,7},{6,4},{7,5},{8,10},{9,11},{10,... | collective-permute-start | bytes 1572872 | tf_op jit(solution)/shard_map/ppermute | solution.py:42
  70.7 13.8 %collective-permute-start.18 = (bf16[128,2048]{1,0:T(8,128)(2,1)S(1)}, bf16[128,2048]{1,0:T(8,128)(2,1)S(1)}, u32[]{:S(2)}, u32[]{:S(2)}) collective-permute-start(bf16[128,2048]{1,0:T(8,128)(2,1)S(1)} %collective-permute-done.8.refs_5_), channel_id=1, source_target_pairs={{0,4},{1,5},{2,6},{3,7},{4,0},{5,1},{6,2},{7,3},{8,12},{9,13},{10,... | collective-permute-start | bytes 1572872 | tf_op jit(solution)/shard_map/ppermute | solution.py:42
  84.5 13.1 %collective-permute-start.19 = (bf16[128,2048]{1,0:T(8,128)(2,1)S(1)}, bf16[128,2048]{1,0:T(8,128)(2,1)S(1)}, u32[]{:S(2)}, u32[]{:S(2)}) collective-permute-start(bf16[128,2048]{1,0:T(8,128)(2,1)S(1)} %collective-permute-done.16.refs_7_), channel_id=1, source_target_pairs={{0,1},{1,0},{2,3},{3,2},{4,5},{5,4},{6,7},{7,6},{8,9},{9,8},{10,11... | collective-permute-start | bytes 1572872 | tf_op jit(solution)/shard_map/ppermute | solution.py:42
  84.6 14.3 %collective-permute-start.20 = (bf16[128,2048]{1,0:T(8,128)(2,1)S(1)}, bf16[128,2048]{1,0:T(8,128)(2,1)S(1)}, u32[]{:S(2)}, u32[]{:S(2)}) collective-permute-start(bf16[128,2048]{1,0:T(8,128)(2,1)S(1)} %copy-done.2), channel_id=1, source_target_pairs={{0,4},{1,5},{2,6},{3,7},{4,0},{5,1},{6,2},{7,3},{8,12},{9,13},{10,... | collective-permute-start | bytes 1572872 | tf_op jit(solution)/shard_map/ppermute | solution.py:42
  86.1 12.8 %collective-permute-start.21 = (bf16[128,2048]{1,0:T(8,128)(2,1)S(1)}, bf16[128,2048]{1,0:T(8,128)(2,1)S(1)}, u32[]{:S(2)}, u32[]{:S(2)}) collective-permute-start(bf16[128,2048]{1,0:T(8,128)(2,1)S(1)} %collective-permute-done.18.refs_6_), channel_id=1, source_target_pairs={{0,1},{1,0},{2,3},{3,2},{4,5},{5,4},{6,7},{7,6},{8,9},{9,8},{10,11... | collective-permute-start | bytes 1572872 | tf_op jit(solution)/shard_map/ppermute | solution.py:42
  86.3 16.0 %collective-permute-start.22 = (bf16[128,2048]{1,0:T(8,128)(2,1)S(1)}, bf16[128,2048]{1,0:T(8,128)(2,1)S(1)}, u32[]{:S(2)}, u32[]{:S(2)}) collective-permute-start(bf16[128,2048]{1,0:T(8,128)(2,1)S(1)} %collective-permute-done.18.refs_6_), channel_id=1, source_target_pairs={{0,8},{1,9},{2,26},{3,27},{4,12},{5,13},{6,30},{7,31},{8,16},{9,17... | collective-permute-start | bytes 1572872 | tf_op jit(solution)/shard_map/ppermute | solution.py:42
  88.0 14.2 %collective-permute-start.23 = (bf16[128,2048]{1,0:T(8,128)(2,1)S(1)}, bf16[128,2048]{1,0:T(8,128)(2,1)S(1)}, u32[]{:S(2)}, u32[]{:S(2)}) collective-permute-start(bf16[128,2048]{1,0:T(8,128)(2,1)S(1)} %collective-permute-done.18.refs_6_), channel_id=1, source_target_pairs={{0,2},{1,3},{2,0},{3,1},{4,6},{5,7},{6,4},{7,5},{8,10},{9,11},{10,... | collective-permute-start | bytes 1572872 | tf_op jit(solution)/shard_map/ppermute | solution.py:42
  116.7 15.4 %collective-permute-start.29 = (bf16[128,2048]{1,0:T(8,128)(2,1)S(1)}, bf16[128,2048]{1,0:T(8,128)(2,1)S(1)}, u32[]{:S(2)}, u32[]{:S(2)}) collective-permute-start(bf16[128,2048]{1,0:T(8,128)(2,1)S(1)} %get-tuple-element.411), channel_id=1, source_target_pairs={{0,4},{1,5},{2,6},{3,7},{4,0},{5,1},{6,2},{7,3},{8,12},{9,13},{10,... | collective-permute-start | bytes 1572872 | tf_op jit(solution)/shard_map/ppermute | solution.py:42
  117.2 14.9 %collective-permute-start.30 = (bf16[128,2048]{1,0:T(8,128)(2,1)S(1)}, bf16[128,2048]{1,0:T(8,128)(2,1)S(1)}, u32[]{:S(2)}, u32[]{:S(2)}) collective-permute-start(bf16[128,2048]{1,0:T(8,128)(2,1)S(1)} %get-tuple-element.414), channel_id=1, source_target_pairs={{0,2},{1,3},{2,0},{3,1},{4,6},{5,7},{6,4},{7,5},{8,10},{9,11},{10,... | collective-permute-start | bytes 1572872 | tf_op jit(solution)/shard_map/ppermute | solution.py:42
  118.6 13.5 %collective-permute-start.31 = (bf16[128,2048]{1,0:T(8,128)(2,1)S(1)}, bf16[128,2048]{1,0:T(8,128)(2,1)S(1)}, u32[]{:S(2)}, u32[]{:S(2)}) collective-permute-start(bf16[128,2048]{1,0:T(8,128)(2,1)S(1)} %get-tuple-element.413), channel_id=1, source_target_pairs={{0,24},{1,25},{2,10},{3,11},{4,28},{5,29},{6,14},{7,15},{8,0},{9,1... | collective-permute-start | bytes 1572872 | tf_op jit(solution)/shard_map/ppermute | solution.py:42
  132.4 15.7 %collective-permute-start.32 = (bf16[128,2048]{1,0:T(8,128)(2,1)S(1)}, bf16[128,2048]{1,0:T(8,128)(2,1)S(1)}, u32[]{:S(2)}, u32[]{:S(2)}) collective-permute-start(bf16[128,2048]{1,0:T(8,128)(2,1)S(1)} %add_convert_fusion.15), channel_id=1, source_target_pairs={{0,4},{1,5},{2,6},{3,7},{4,0},{5,1},{6,2},{7,3},{8,12},{9,13},{10,... | collective-permute-start | bytes 1572872 | tf_op jit(solution)/shard_map/ppermute | solution.py:42
  134.0 14.2 %collective-permute-start.33 = (bf16[128,2048]{1,0:T(8,128)(2,1)}, bf16[128,2048]{1,0:T(8,128)(2,1)S(1)}, u32[]{:S(2)}, u32[]{:S(2)}) collective-permute-start(bf16[128,2048]{1,0:T(8,128)(2,1)} %get-tuple-element.447), channel_id=1, source_target_pairs={{0,2},{1,3},{2,0},{3,1},{4,6},{5,7},{6,4},{7,5},{8,10},{9,11},{10,... | collective-permute-start | bytes 1572872 | tf_op jit(solution)/shard_map/ppermute | solution.py:42
  148.2 15.8 %collective-permute-start.35 = (bf16[1024,2048]{1,0:T(8,128)(2,1)S(1)}, bf16[1024,2048]{1,0:T(8,128)(2,1)S(1)}, u32[]{:S(2)}, u32[]{:S(2)}) collective-permute-start(bf16[1024,2048]{1,0:T(8,128)(2,1)S(1)} %leave_backward.2), channel_id=1, source_target_pairs={{0,1},{1,0},{2,3},{3,2},{4,5},{5,4},{6,7},{7,6},{8,9},{9,8},{10,11... | collective-permute-start | bytes 12582920 | tf_op jit(solution)/shard_map/ppermute | solution.py:42
  148.6 15.4 %collective-permute-start.36 = (bf16[128,2048]{1,0:T(8,128)(2,1)S(1)}, bf16[128,2048]{1,0:T(8,128)(2,1)S(1)}, u32[]{:S(2)}, u32[]{:S(2)}) collective-permute-start(bf16[128,2048]{1,0:T(8,128)(2,1)S(1)} %add_convert_fusion.14), channel_id=1, source_target_pairs={{0,24},{1,25},{2,10},{3,11},{4,28},{5,29},{6,14},{7,15},{8,0},{9,1... | collective-permute-start | bytes 1572872 | tf_op jit(solution)/shard_map/ppermute | solution.py:42
  165.6 13.6 %collective-permute-start.37 = (bf16[128,2048]{1,0:T(8,128)(2,1)S(1)}, bf16[128,2048]{1,0:T(8,128)(2,1)S(1)}, u32[]{:S(2)}, u32[]{:S(2)}) collective-permute-start(bf16[128,2048]{1,0:T(8,128)(2,1)S(1)} %get-tuple-element.491), channel_id=1, source_target_pairs={{0,4},{1,5},{2,6},{3,7},{4,0},{5,1},{6,2},{7,3},{8,12},{9,13},{10,... | collective-permute-start | bytes 1572872 | tf_op jit(solution)/shard_map/ppermute | solution.py:42
  166.3 14.4 %collective-permute-start.38 = (bf16[128,2048]{1,0:T(8,128)(2,1)S(1)}, bf16[128,2048]{1,0:T(8,128)(2,1)S(1)}, u32[]{:S(2)}, u32[]{:S(2)}) collective-permute-start(bf16[128,2048]{1,0:T(8,128)(2,1)S(1)} %get-tuple-element.488), channel_id=1, source_target_pairs={{0,2},{1,3},{2,0},{3,1},{4,6},{5,7},{6,4},{7,5},{8,10},{9,11},{10,... | collective-permute-start | bytes 1572872 | tf_op jit(solution)/shard_map/ppermute | solution.py:42
  169.1 13.0 %collective-permute-start.39 = (bf16[128,2048]{1,0:T(8,128)(2,1)S(1)}, bf16[128,2048]{1,0:T(8,128)(2,1)S(1)}, u32[]{:S(2)}, u32[]{:S(2)}) collective-permute-start(bf16[128,2048]{1,0:T(8,128)(2,1)S(1)} %get-tuple-element.489), channel_id=1, source_target_pairs={{0,24},{1,25},{2,10},{3,11},{4,28},{5,29},{6,14},{7,15},{8,0},{9,1... | collective-permute-start | bytes 1572872 | tf_op jit(solution)/shard_map/ppermute | solution.py:42
  182.4 12.1 %collective-permute-start.40 = (bf16[128,2048]{1,0:T(8,128)(2,1)S(1)}, bf16[128,2048]{1,0:T(8,128)(2,1)S(1)}, u32[]{:S(2)}, u32[]{:S(2)}) collective-permute-start(bf16[128,2048]{1,0:T(8,128)(2,1)S(1)} %add_convert_fusion.4), channel_id=1, source_target_pairs={{0,4},{1,5},{2,6},{3,7},{4,0},{5,1},{6,2},{7,3},{8,12},{9,13},{10,... | collective-permute-start | bytes 1572872 | tf_op jit(solution)/shard_map/ppermute | solution.py:42
  183.9 12.4 %collective-permute-start.41 = (bf16[128,2048]{1,0:T(8,128)(2,1)S(1)}, bf16[128,2048]{1,0:T(8,128)(2,1)S(1)}, u32[]{:S(2)}, u32[]{:S(2)}) collective-permute-start(bf16[128,2048]{1,0:T(8,128)(2,1)S(1)} %get-tuple-element.470), channel_id=1, source_target_pairs={{0,2},{1,3},{2,0},{3,1},{4,6},{5,7},{6,4},{7,5},{8,10},{9,11},{10,... | collective-permute-start | bytes 1572872 | tf_op jit(solution)/shard_map/ppermute | solution.py:42
  (35 other events, 440.6 us)

commit v3 on v2

--- a/solution.py
+++ b/solution.py
@@ -56,6 +56,15 @@
     ]
 
 
+def table_copies(refs, table_ref, sem_ref):
+    copies, start = [], 0
+    for n, ref in enumerate(refs):
+        place = table_ref.at[pl.ds(start, ref.shape[0])]
+        copies.append(pltpu.make_async_copy(ref, place, sem_ref.at[n]))
+        start += ref.shape[0]
+    return copies
+
+
 def enter_kernel(backward, parts, sources, group, slots, half, *refs):
     count = 1 if backward else 2
     core_ref = refs[0]
@@ -63,11 +72,10 @@
     piece_refs = refs[1 + parts : 1 + parts + 2 * sources]
     weight_refs = refs[1 + parts + 2 * sources : 1 + parts + 2 * sources + count]
     if backward:
-        factor_refs, (left_ref, right_ref) = refs[1 + parts + 2 * sources + count : -7], refs[-7:-5]
+        factor_refs, (left_ref, right_ref) = refs[1 + parts + 2 * sources + count : -9], refs[-9:-7]
     else:
-        left_ref, first_ref, second_ref = refs[-8:-5]
-    block_ref, rows_ref, buffer_ref, sem_ref, weight_sem_ref = refs[-5:]
-    places = [ref.at[k] for ref in place_refs for k in range(ref.shape[0])]
+        left_ref, first_ref, second_ref = refs[-10:-7]
+    block_ref, rows_ref, buffer_ref, table_ref, sem_ref, weight_sem_ref, table_sem_ref = refs[-7:]
     step = pl.program_id(0)
     core = core_ref[0]
     experts = rows_ref.shape[0]
@@ -91,24 +99,26 @@
 
     @pl.when(step == 0)
     def _():
+        tables = table_copies(place_refs, table_ref, table_sem_ref)
+        for copy in tables:
+            copy.start()
         for k in range(sources // group):
             for side in range(2):
                 for j in range(k * group, (k + 1) * group):
                     piece_copy(side, j).start()
-            if k == 0:
-                for n in range(count):
-                    weight_copy(n, 0).start()
-        for expert in range(1, depth):
-            for n in range(count):
-                weight_copy(n, expert).start()
+        for copy in tables:
+            copy.wait()
         for k in range(sources // group):
             for side in range(2):
                 for j in range(k * group, (k + 1) * group):
                     piece_copy(side, j).wait()
+                if 2 * k + side < depth:
+                    for n in range(count):
+                        weight_copy(n, 2 * k + side).start()
                 base = (core if side == 0 else 1 - core) * half
                 for column in range(0, half, CHUNK):
                     block = block_ref[side, pl.ds(k * span, span), pl.ds(column, CHUNK)]
-                    picked = jnp.dot(places[k][...], block, preferred_element_type=jnp.float32)
+                    picked = jnp.dot(table_ref[k], block, preferred_element_type=jnp.float32)
                     to = pl.multiple_of(base + column, CHUNK)
                     rows_ref[:, pl.ds(k * slots, slots), pl.ds(to, CHUNK)] = picked.astype(
                         jnp.bfloat16
@@ -152,10 +162,9 @@
     groups = sum(place.shape[0] for place in places)
     slots = height // experts
     total = groups * slots
-    depth = min(3, experts)
+    depth = min(3, experts, 2 * groups)
     per_expert = pl.BlockSpec((1, total, hidden), lambda i, c: (i, 0, 0))
-    in_specs = [pl.BlockSpec(place.shape, lambda i, c: (0, 0, 0)) for place in places]
-    in_specs += [pl.BlockSpec(memory_space=pl.ANY)] * (2 * sources + len(weights))
+    in_specs = [pl.BlockSpec(memory_space=pl.ANY)] * (len(places) + 2 * sources + len(weights))
     in_specs += [
         pl.BlockSpec((1,) + factor.shape[1:], lambda i, c: (i, 0, 0)) for factor in factors
     ]
@@ -173,14 +182,16 @@
                 pltpu.VMEM((2, sources * tokens, half), jnp.bfloat16),
                 pltpu.VMEM((experts, total, features), jnp.bfloat16),
                 pltpu.VMEM((len(weights), depth, hidden, features), jnp.bfloat16),
+                pltpu.VMEM((groups, height, span), jnp.bfloat16),
                 pltpu.SemaphoreType.DMA((2 * sources,)),
                 pltpu.SemaphoreType.DMA((len(weights), depth)),
+                pltpu.SemaphoreType.DMA((len(places),)),
             ],
         ),
         out_shape=out_shape,
-        compiler_params=pltpu.CompilerParams(vmem_limit_bytes=40 * 1024 * 1024),
+        compiler_params=pltpu.CompilerParams(vmem_limit_bytes=(38 if backward else 46) * 1024 * 1024),
         cost_estimate=pl.CostEstimate(
-            flops=2 * features * (len(weights) * experts * total * hidden + groups * height * span),
+            flops=128 * features * (len(weights) * experts * total * hidden + groups * height * span),
             bytes_accessed=len(weights) * experts * hidden * features * 2
             + 2 * sources * tokens * features,
             transcendentals=0,
@@ -249,23 +260,27 @@
             in_specs=[whole(array.shape) for array in list(places) + list(values)]
             + [
                 pl.BlockSpec(
-                    (each, hidden, half), lambda i, s: (jnp.minimum(i, turns - 1), 0, s[0])
+                    (each, hidden, half),
+                    functools.partial(
+                        lambda wide, i, s: (jnp.minimum(i, turns - 1), 0, s[0] * wide),
+                        int(weight.shape[2] > half),
+                    ),
                 )
-            ]
-            * len(weights),
+                for weight in weights
+            ],
             out_specs=pl.BlockSpec(
                 (groups * span, width), lambda i, s: (0, jnp.maximum(i - turns, 0))
             ),
             scratch_shapes=[pltpu.VMEM((experts, total, half), jnp.bfloat16)],
         ),
         out_shape=jax.ShapeDtypeStruct((groups * span, half), jnp.bfloat16),
-        compiler_params=pltpu.CompilerParams(vmem_limit_bytes=40 * 1024 * 1024),
+        compiler_params=pltpu.CompilerParams(vmem_limit_bytes=(46 if len(weights) < 4 else 40) * 1024 * 1024),
         cost_estimate=pl.CostEstimate(
-            flops=2 * half * (len(weights) * experts * total * hidden + groups * height * span),
+            flops=128 * half * (len(weights) * experts * total * hidden + groups * height * span),
             bytes_accessed=len(weights) * experts * hidden * half * 2 + 2 * groups * span * half,
             transcendentals=0,
         ),
-        name="leave_forward" if len(weights) == 1 else "leave_backward",
+        name="leave",
     )(side, *places, *values, *weights)
 
 
@@ -399,94 +414,111 @@
         tables = live["near" if names is near else "late"]
         return enter(False, live["mine"], tables[:1], pieces(live, "t", names), (w_gate, w_up), ())
 
+    def sibling_half(weight):
+        return lax.dynamic_slice_in_dim(weight, (1 - core) * half, half, 2)
+
+    def block(live, kind, name):
+        rows = tokens.shape[0]
+        start = order.index(name) * rows
+        return live[kind][start : start + rows]
+
     near, late = order[:4], order[4:]
     tq0, tq0_far = halves(tokens, core)
     live = dict(mine=mine, tq0=jnp.concatenate([tq0, own_choices], axis=1), tq0_far=tq0_far)
     cq0, cq0_far = halves(cotangent, core)
-    live = phase(live, dict(tq1=("tq0", "ahead"), tr0=("tq0", "x")), cq0=cq0, cq0_far=cq0_far)
+    live = phase(
+        live,
+        dict(tq1=("tq0", "ahead"), tr0=("tq0", "x")),
+        cq0=cq0,
+        cq0_far=cq0_far,
+        down=sibling_half(w_down),
+        gate=sibling_half(w_gate),
+    )
     live = phase(
         live,
         dict(tq2=("tq1", "ahead"), tr1=("tq1", "x"), tq3=("tq1", "y")),
         far=("tr0", "tq1"),
+        up=sibling_half(w_up),
     )
     tables = routed([live["t" + name] for name in near], half // LANES)
-    live = phase(live, {}, far=("tr1",), near=tables)
-    live = phase(
-        live,
-        dict(tr2=("tq2", "x"), tr3=("tr1", "y"), cq1=("cq0", "ahead")),
-        far=("tq2", "tq3"),
+    live = phase(live, {}, far=("tr1", "tq2", "tq3"), near=tables)
+    live = phase(
+        live,
+        dict(tr2=("tq2", "x"), tr3=("tr1", "y"), cq1=("cq0", "ahead"), down=("down", "core")),
         near_values=enter_tokens(live, near),
     )
     tables = routed([live["t" + name] for name in late], half // LANES)
-    live = phase(live, {}, far=("tr2", "tr3"), late=tables)
-    live = phase(
-        live,
-        dict(cq2=("cq1", "ahead"), cr1=("cq1", "x"), cq3=("cq1", "y")),
+    live["hidden"] = live["near_values"][0]
+    live = phase(live, {}, far=("tr2", "tr3", "hidden"), late=tables)
+    live = phase(
+        live,
+        dict(cq2=("cq1", "ahead"), cr1=("cq1", "x"), cq3=("cq1", "y"), gate=("gate", "core")),
         far=("cq1",),
         late_values=enter_tokens(live, late),
     )
     live = {name: value for name, value in live.items() if name[0] != "t"}
-
-    def leave_tokens(live, side):
-        tables = [live["near"][3], live["late"][3]]
-        return leave(side, tables, [live["near_values"][0], live["late_values"][0]], (w_down,))
-
-    live = phase(
-        live,
-        dict(cr0=("cq0", "x"), cr2=("cr1", "ahead"), cr3=("cr1", "y")),
-        far=("cq2", "cr1"),
-        o_far=leave_tokens(live, 1 - live["mine"]),
-    )
-    live = phase(
-        live,
-        dict(o_new=("o_far", "core")),
-        far=("cq3", "cr0", "cr2", "cr3"),
-        o_near=leave_tokens(live, live["mine"]),
-    )
-    live.update(merge("o", live.pop("o_new"), live.pop("o_near")))
-    del live["o_far"]
-    live = lax.optimization_barrier(live)
+    live["late_hidden"] = live["late_values"][0]
+    live = phase(live, {}, far=("late_hidden", "cq2", "cr1", "cq3"))
+    tables = [live["near"][3], live["late"][3]]
+    names = ("hidden", "hidden_far", "late_hidden", "late_hidden_far")
+    live = phase(
+        live,
+        dict(cr0=("cq0", "x"), cr2=("cr1", "ahead"), cr3=("cr1", "y"), up=("up", "core")),
+        o=leave(live["mine"], tables, [live[name] for name in names], (w_down, live["down"])),
+    )
+    live.update({"o" + name: block(live, "o", name) for name in ("r3", "r2", "r0")})
+    live = phase(live, {}, far=("cr0", "cr2", "cr3"))
+    tables = [live["near"][1], live["late"][1]]
+    factors = list(live["near_values"][1:]) + list(live["late_values"][1:])
+    left, right = enter(True, live["mine"], tables, pieces(live, "c", order), (w_down,), factors)
     place_t = [live["near"][2], live["late"][2]]
-    values = enter(
-        True,
-        live["mine"],
-        [live["near"][1], live["late"][1]],
-        pieces(live, "c", order),
-        (w_down,),
-        list(live["near_values"][1:]) + list(live["late_values"][1:]),
-    )
-    live = {name: value for name, value in live.items() if name[0] in "mo"}
-    live = phase(
-        live, dict(y=("or3", "y"), z=("or2", "back"), x=("or0", "x")), values=tuple(values)
-    )
-    live["or1"] = add(live["or1"], live["y"], live["z"])
-    g_far = leave(1 - live["mine"], place_t, live["values"], (w_gate, w_up))
-    live = phase(
-        live, dict(y1=("oq3", "y"), x1=("or1", "x"), z1=("oq2", "back")), g_far=g_far
-    )
-    live["oq1"] = add(live["oq1"], live["y1"], live["x1"], live["z1"])
-    g_near = leave(live["mine"], place_t, live["values"], (w_gate, w_up))
-    live = phase(live, dict(g_new=("g_far", "core"), z2=("oq1", "back")), g_near=g_near)
-    own = add(live["oq0"], live["x"], live["z2"])
-    live = dict(own=own, **merge("g", live["g_new"], live["g_near"]))
-    live = phase(live, dict(y=("gr3", "y"), z=("gr2", "back"), x=("gr0", "x")))
-    live["gr1"] = add(live["gr1"], live["y"], live["z"])
-    live = phase(live, dict(y1=("gq3", "y"), x1=("gr1", "x"), z1=("gq2", "back")))
-    live["gq1"] = add(live["gq1"], live["y1"], live["x1"], live["z1"])
-    live = phase(live, dict(z2=("gq1", "back"), far=("own", "y")))
-    mixed = add(live["own"], live["far"])
-    own = add(live["gq0"], live["x"], live["z2"])
-    grad_tokens = add(own, move(own, "y"))
-    return whole_rows(mixed, core), whole_rows(grad_tokens, core)
-
-
-def merge(kind, arrived, own):
-    rows = own.shape[0] // 8
-    names = ("q0", "r0", "q1", "r1", "q2", "r2", "q3", "r3")
-    return {
-        kind + name: add(own[j * rows : (j + 1) * rows], arrived[j * rows : (j + 1) * rows])
-        for j, name in enumerate(names)
-    }
+    live = {name: value for name, value in live.items() if name[0] in "mogu"}
+    live = phase(
+        live,
+        dict(oy=("or3", "y"), oz=("or2", "back"), ox=("or0", "x")),
+        left=left,
+        right=right,
+    )
+    live = phase(
+        live,
+        {},
+        far=("left", "right"),
+        or1=add(block(live, "o", "r1"), live["oy"], live["oz"]),
+        oq3=block(live, "o", "q3"),
+        oq2=block(live, "o", "q2"),
+    )
+    weights = (w_gate, w_up, live["gate"], live["up"])
+    names = ("left", "right", "left_far", "right_far")
+    live = phase(
+        live,
+        dict(oy=("oq3", "y"), oq=("or1", "x"), oz=("oq2", "back")),
+        g=leave(live["mine"], place_t, [live[name] for name in names], weights),
+    )
+    slack = move(add(block(live, "o", "q1"), live["oy"], live["oq"], live["oz"]), "back")
+    live.update({"g" + name: block(live, "g", name) for name in ("r3", "r2")})
+    live = phase(
+        live,
+        dict(gy=("gr3", "y"), gx=("gr2", "x")),
+        gq3=block(live, "g", "q3"),
+        gr0=block(live, "g", "r0"),
+    )
+    live["oz"] = slack
+    live["gr1"] = add(block(live, "g", "r1"), live["gy"])
+    live["gq2"] = add(block(live, "g", "q2"), live["gx"])
+    live = phase(
+        live,
+        dict(gy=("gq3", "y"), gx=("gr1", "x"), gz=("gq2", "back")),
+        mixed=add(block(live, "o", "q0"), live["ox"], live["oz"]),
+    )
+    slack = move(live["mixed"], "y")
+    live["gq1"] = add(block(live, "g", "q1"), live["gy"], live["gx"], live["gz"])
+    live = phase(live, dict(gz=("gq1", "back"), gx=("gr0", "x")))
+    live["oy"] = slack
+    live["grad"] = add(block(live, "g", "q0"), live["gx"], live["gz"])
+    live = phase(
+        live, dict(gy=("grad", "y")), mixed=whole_rows(add(live["mixed"], live["oy"]), core)
+    )
+    return live["mixed"], whole_rows(add(live["grad"], live["gy"]), core)
 
 
 def whole_rows(own, core):

time: 227 us -> 219 us (0.965)
  local copies, waits for them, and re-layouts: 10.8 us -> 32.4 us
  waiting for transfers between devices: 71.6 us -> 58 us
  Pallas kernels: 79.2 us -> 70.3 us
  starting transfers between devices: 52.2 us -> 44.5 us
    dynamic_slice x0 -> x2, local copies, waits for them, and re-layouts: none -> 18.2 us  [sibling_half(): return lax.dynamic_slice_in_dim(weight, (1 - core) * half, half, 2)]
    ppermute x48 -> x53, waiting for transfers between devices: 71.6 us -> 58 us  [move(): return lax.ppermute(array, AXES, MOVES[name])]
    pallas_call x4 -> x2, Pallas kernels: 36.7 us -> 25.7 us  [leave(): pl.pallas_call(functools.partial(leave_kernel, len(places), len(weights))...]
    ppermute x48 -> x53, starting transfers between devices: 52.2 us -> 44.5 us  [move(): return lax.ppermute(array, AXES, MOVES[name])]
    slice x0 -> x3, local copies, waits for them, and re-layouts: none -> 3.73 us  [block(): return live[kind][start:start + rows]]
    unnamed x38 -> x44, local copies, waits for them, and re-layouts: 6.3 us -> 6.94 us
    convert_element_type x10 -> x8, other arithmetic: 7.62 us -> 7.92 us  [add(): return total.astype(jnp.bfloat16)]
  transfers between devices with their start and end apart: 48 -> 53, of which waited for: 22 -> 24; matrix products, arithmetic and copies ran while one was open for 2% -> 15% of each run, Pallas kernels for 35% -> 32%
where the time goes in v3:
time: 219 us; the launch traced here: 218 us
  Pallas kernels  70.3 us (32%)
  waiting for transfers between devices  58 us (26%)
  starting transfers between devices  44.5 us (20%)
  local copies, waits for them, and re-layouts  32.4 us (15%)
  other arithmetic  11.6 us (5%)
    ppermute x53, waiting for transfers between devices, move(): return lax.ppermute(array, AXES, MOVES[name])  58 us
    ppermute x53, starting transfers between devices, move(): return lax.ppermute(array, AXES, MOVES[name])  44.5 us
    pallas_call x3, Pallas kernels, enter(): pl.pallas_call(functools.partial(enter_kernel, backward, len(places), sou...  40.1 us
    pallas_call x2, Pallas kernels, leave(): pl.pallas_call(functools.partial(leave_kernel, len(places), len(weights))...  25.7 us
    dynamic_slice x2, local copies, waits for them, and re-layouts, sibling_half(): return lax.dynamic_slice_in_dim(weight, (1 - core) * half, half, 2)  18.2 us
    convert_element_type x8, other arithmetic, add(): return total.astype(jnp.bfloat16)  7.92 us
    unnamed x44, local copies, waits for them, and re-layouts  6.94 us
    pallas_call x2, Pallas kernels, route(): pl.pallas_call(functools.partial(route_kernel, sources, group, capacity),...  4.42 us
  transfers between devices with their start and end apart: 53, of which 24 were waited for; matrix products, arithmetic and copies ran while one was open for 15% of the time, Pallas kernels for 32%

profile of v3, /device:TPU:0, one launch (start us, length us, event | category | flops | bytes accessed | tf_op | source)
XLA Modules:
  0.0 217.9 jit_solution(1937694116344325360)
XLA Ops:
  3.5 3.1 %collective-permute-start = (bf16[128,2176]{1,0:T(8,128)(2,1)S(1)}, bf16[128,2176]{1,0:T(8,128)(2,1)S(1)}, u32[]{:S(2)}, u32[]{:S(2)}) collective-permute-start(bf16[128,2176]{1,0:T(8,128)(2,1)S(1)} %fusion.1.refs_1_.refs_2_), channel_id=1, source_target_pairs={{0,8},{1,9},{2,26},{3,27},{4,12},{5,13},{6,30},{7,31},{8,16},{9,17... | collective-permute-start | bytes 1671176 | tf_op jit(solution)/shard_map/ppermute | solution.py:42
  8.1 2.1 constant_dynamic-slice_fusion.5
  10.2 10.8 %constant_dynamic-slice_fusion.3 = (bf16[8,224,2048]{2,1,0:T(8,128)(2,1)}, bf16[8,224,2048]{2,1,0:T(8,128)(2,1)}) fusion(bf16[8,224,4096]{2,1,0:T(8,128)(2,1)} %refs_7_.5, s32[]{:T(128)S(6)} %select_n.40, bf16[8,224,4096]{2,1,0:T(8,128)(2,1)} %refs_19_.1), kind=kLoop, calls=%fused_computation.23 | loop fusion | bytes 29360132 | tf_op jit(solution)/shard_map/dynamic_slice | solution.py:418
  22.8 3.7 %collective-permute-start.4 = (bf16[128,2176]{1,0:T(8,128)(2,1)S(1)}, bf16[128,2176]{1,0:T(8,128)(2,1)S(1)}, u32[]{:S(2)}, u32[]{:S(2)}) collective-permute-start(bf16[128,2176]{1,0:T(8,128)(2,1)S(1)} %collective-permute-done.refs_3_.refs_4_), channel_id=1, source_target_pairs={{0,2},{1,3},{2,0},{3,1},{4,6},{5,7},{6,4},{7,5},{8,10},{9,11},{10,... | collective-permute-start | bytes 1671176 | tf_op jit(solution)/shard_map/ppermute | solution.py:42
  28.0 7.5 %constant_dynamic-slice_fusion = bf16[8,224,2048]{2,1,0:T(8,128)(2,1)} fusion(bf16[8,224,4096]{2,1,0:T(8,128)(2,1)} %refs_8_.3, s32[]{:T(128)S(6)} %select_n.40), kind=kLoop, calls=%fused_computation.20 | loop fusion | bytes 14680068 | tf_op jit(solution)/shard_map/dynamic_slice | solution.py:418
  36.2 2.1 collective-permute-done.3.refs_1_.refs_2_
  42.2 2.2 %route.2 = (bf16[2,384,256]{2,1,0:T(8,128)(2,1)S(1)}, bf16[2,384,256]{2,1,0:T(8,128)(2,1)S(1)}, bf16[2,256,384]{2,1,0:T(8,128)(2,1)S(1)}, bf16[2,256,384]{2,1,0:T(8,128)(2,1)S(1)}) custom-call(s32[1]{0:T(128)} %bitcast.1.refs_0_, bf16[128,2176]{1,0:T(8,128)(2,1)S(1)} %fusion.1.refs_1_.refs_2_, bf16[128,2176]{1,0:T(8,128)(2,1)S(1)} %collective-permute-done.1.refs_2_.refs_3_, ...), custom_call_target="tpu_custom_call" | custom-call | tf_op jit(solution)/shard_map/route/pallas_call | solution.py:342
  49.6 13.3 %enter_forward.2 = (bf16[8,96,224]{2,1,0:T(8,128)(2,1)S(1)}, f32[8,96,224]{2,1,0:T(8,128)S(1)}, f32[8,96,224]{2,1,0:T(8,128)S(1)}) custom-call(s32[1]{0:T(128)} %bitcast.refs_0_, bf16[2,384,256]{2,1,0:T(8,128)(2,1)S(1)} %get-tuple-element.297.refs_1_, bf16[128,2176]{1,0:T(8,128)(2,1)S(1)} %fusion.1.refs_1_.refs_2_, ...), custom_call_target="tpu_custom_call" | custom-call | flops 283467841536 | bytes 33554432 | tf_op jit(solution)/shard_map/enter_forward/pallas_call | solution.py:174
  63.9 2.2 %route.3 = (bf16[2,384,256]{2,1,0:T(8,128)(2,1)S(1)}, bf16[2,384,256]{2,1,0:T(8,128)(2,1)S(1)}, bf16[2,256,384]{2,1,0:T(8,128)(2,1)S(1)}, bf16[2,256,384]{2,1,0:T(8,128)(2,1)S(1)}) custom-call(s32[1]{0:T(128)} %bitcast.1.refs_0_, bf16[128,2176]{1,0:T(8,128)(2,1)} %collective-permute-done.3.refs_1_.refs_2_, ...), custom_call_target="tpu_custom_call" | custom-call | tf_op jit(solution)/shard_map/route/pallas_call | solution.py:342
  67.4 2.5 %collective-permute-start.19 = (bf16[128,2048]{1,0:T(8,128)(2,1)}, bf16[128,2048]{1,0:T(8,128)(2,1)}, u32[]{:S(2)}, u32[]{:S(2)}) collective-permute-start(bf16[128,2048]{1,0:T(8,128)(2,1)} %collective-permute-done.10.refs_5_), channel_id=1, source_target_pairs={{0,2},{1,3},{2,0},{3,1},{4,6},{5,7},{6,4},{7,5},{8,10},{9,11},{10,... | collective-permute-start | bytes 1572872 | tf_op jit(solution)/shard_map/ppermute | solution.py:42
  70.4 14.3 %enter_forward.3 = (bf16[8,96,224]{2,1,0:T(8,128)(2,1)S(1)}, f32[8,96,224]{2,1,0:T(8,128)S(1)}, f32[8,96,224]{2,1,0:T(8,128)S(1)}) custom-call(s32[1]{0:T(128)} %bitcast.refs_0_, bf16[2,384,256]{2,1,0:T(8,128)(2,1)S(1)} %get-tuple-element.347.refs_1_, bf16[128,2176]{1,0:T(8,128)(2,1)} %collective-permute-done.3.refs_1_.refs_2_, ...), custom_call_target="tpu_custom_call" | custom-call | flops 283467841536 | bytes 33554432 | tf_op jit(solution)/shard_map/enter_forward/pallas_call | solution.py:174
  86.0 2.7 %collective-permute-done.25.refs_6_ = bf16[8,96,224]{2,1,0:T(8,128)(2,1)S(1)} collective-permute-done((bf16[8,96,224]{2,1,0:T(8,128)(2,1)S(1)}, bf16[8,96,224]{2,1,0:T(8,128)(2,1)S(1)}, u32[]{:S(2)}, u32[]{:S(2)}) %collective-permute-start.25) | collective-permute-done | bytes 344096 | tf_op jit(solution)/shard_map/ppermute | solution.py:42
  91.1 1.5 collective-permute-start.27
  92.6 1.9 collective-permute-start.28
  96.0 10.5 %leave.2 = bf16[1024,2048]{1,0:T(8,128)(2,1)S(1)} custom-call(s32[1]{0:T(128)} %bitcast.refs_0_, bf16[2,256,384]{2,1,0:T(8,128)(2,1)S(1)} %get-tuple-element.417.refs_1_, bf16[2,256,384]{2,1,0:T(8,128)(2,1)S(1)} %get-tuple-element.409.refs_2_, bf16[8,96,224]{2,1,0:T(8,128)(2,1)S(1)} %copy-done.19, bf16[8,96,224]{2,1,0:T(8,128)(2,1)S(1)} %copy-done.21, ...), custom_call_target="tpu_custom_call" | custom-call | flops 283467841536 | bytes 18874368 | tf_op jit(solution)/shard_map/leave/pallas_call | solution.py:255
  106.5 2.7 %collective-permute-done.26.refs_4_ = bf16[128,2048]{1,0:T(8,128)(2,1)} collective-permute-done((bf16[128,2048]{1,0:T(8,128)(2,1)}, bf16[128,2048]{1,0:T(8,128)(2,1)}, u32[]{:S(2)}, u32[]{:S(2)}) %collective-permute-start.26) | collective-permute-done | bytes 524320 | tf_op jit(solution)/shard_map/ppermute | solution.py:42
  114.5 2.3 %collective-permute-start.35 = (bf16[128,2048]{1,0:T(8,128)(2,1)}, bf16[128,2048]{1,0:T(8,128)(2,1)}, u32[]{:S(2)}, u32[]{:S(2)}) collective-permute-start(bf16[128,2048]{1,0:T(8,128)(2,1)} %get-tuple-element.473), channel_id=1, source_target_pairs={{0,24},{1,25},{2,10},{3,11},{4,28},{5,29},{6,14},{7,15},{8,0},{9,1... | collective-permute-start | bytes 1572872 | tf_op jit(solution)/shard_map/ppermute | solution.py:42
  116.8 12.5 %enter_backward.1 = (bf16[8,192,224]{2,1,0:T(8,128)(2,1)S(1)}, bf16[8,192,224]{2,1,0:T(8,128)(2,1)S(1)}) custom-call(s32[1]{0:T(128)} %bitcast.refs_0_, bf16[2,384,256]{2,1,0:T(8,128)(2,1)S(1)} %get-tuple-element.448.refs_1_, bf16[2,384,256]{2,1,0:T(8,128)(2,1)S(1)} %get-tuple-element.449.refs_2_, bf16[128,2048]{1,0:T(8,128)(2,1)} %get-tuple-element.450.refs_3_, ...), custom_call_target="tpu_custom_call" | custom-call | flops 386547056640 | bytes 23068672 | tf_op jit(solution)/shard_map/enter_backward/pallas_call | solution.py:174
  129.9 2.3 %fusion.3 = (bf16[128,2048]{1,0:T(8,128)(2,1)}, bf16[128,2048]{1,0:T(8,128)(2,1)}) fusion(bf16[1024,2048]{1,0:T(8,128)(2,1)} %copy-done.1), kind=kLoop, calls=%fused_computation.28 | loop fusion | bytes 2097152 | tf_op jit(solution)/shard_map/slice | solution.py:423
  132.2 2.4 %add_convert_fusion.8 = bf16[128,2048]{1,0:T(8,128)(2,1)} fusion(bf16[128,2048]{1,0:T(8,128)(2,1)} %collective-permute-done.35, bf16[128,2048]{1,0:T(8,128)(2,1)} %collective-permute-done.34, bf16[1024,2048]{1,0:T(8,128)(2,1)} %copy-done.1), kind=kLoop, calls=%fused_computation.12 | loop fusion | flops 1572864 | bytes 2097152 | tf_op jit(solution)/shard_map/convert_element_type | solution.py:49
  135.1 2.5 %collective-permute-start.39 = (bf16[128,2048]{1,0:T(8,128)(2,1)}, bf16[128,2048]{1,0:T(8,128)(2,1)}, u32[]{:S(2)}, u32[]{:S(2)}) collective-permute-start(bf16[128,2048]{1,0:T(8,128)(2,1)} %get-tuple-element.498), channel_id=1, source_target_pairs={{0,2},{1,3},{2,0},{3,1},{4,6},{5,7},{6,4},{7,5},{8,10},{9,11},{10,... | collective-permute-start | bytes 1572872 | tf_op jit(solution)/shard_map/ppermute | solution.py:42
  138.5 15.2 %leave.3 = bf16[1024,2048]{1,0:T(8,128)(2,1)S(1)} custom-call(s32[1]{0:T(128)} %bitcast.refs_0_, bf16[2,256,384]{2,1,0:T(8,128)(2,1)S(1)} %get-tuple-element.487.refs_1_, bf16[2,256,384]{2,1,0:T(8,128)(2,1)S(1)} %get-tuple-element.488.refs_2_, bf16[8,192,224]{2,1,0:T(8,128)(2,1)S(1)} %get-tuple-element.489.refs_3_, ...), custom_call_target="tpu_custom_call" | custom-call | flops 463856467968 | bytes 33554432 | tf_op jit(solution)/shard_map/leave/pallas_call | solution.py:255
  154.0 1.5 collective-permute-start.41
  155.5 1.8 add_convert_fusion.5
  157.4 3.0 %collective-permute-start.46 = (bf16[128,2048]{1,0:T(8,128)(2,1)S(1)}, bf16[128,2048]{1,0:T(8,128)(2,1)S(1)}, u32[]{:S(2)}, u32[]{:S(2)}) collective-permute-start(bf16[128,2048]{1,0:T(8,128)(2,1)S(1)} %add_convert_fusion.5), channel_id=1, source_target_pairs={{0,24},{1,25},{2,10},{3,11},{4,28},{5,29},{6,14},{7,15},{8,0},{9,1... | collective-permute-start | bytes 1572872 | tf_op jit(solution)/shard_map/ppermute | solution.py:42
  160.4 6.8 %collective-permute-done.41 = bf16[128,2048]{1,0:T(8,128)(2,1)S(1)} collective-permute-done((bf16[128,2048]{1,0:T(8,128)(2,1)S(1)}, bf16[128,2048]{1,0:T(8,128)(2,1)S(1)}, u32[]{:S(2)}, u32[]{:S(2)}) %collective-permute-start.41) | collective-permute-done | bytes 524320 | tf_op jit(solution)/shard_map/ppermute | solution.py:42
  173.5 7.1 %collective-permute-done.43 = bf16[128,2048]{1,0:T(8,128)(2,1)S(1)} collective-permute-done((bf16[128,2048]{1,0:T(8,128)(2,1)S(1)}, bf16[128,2048]{1,0:T(8,128)(2,1)S(1)}, u32[]{:S(2)}, u32[]{:S(2)}) %collective-permute-start.43) | collective-permute-done | bytes 524320 | tf_op jit(solution)/shard_map/ppermute | solution.py:42
  182.9 3.7 %collective-permute-start.48 = (bf16[128,2048]{1,0:T(8,128)(2,1)S(1)}, bf16[128,2048]{1,0:T(8,128)(2,1)S(1)}, u32[]{:S(2)}, u32[]{:S(2)}) collective-permute-start(bf16[128,2048]{1,0:T(8,128)(2,1)S(1)} %add_convert_fusion.3), channel_id=1, source_target_pairs={{0,24},{1,25},{2,10},{3,11},{4,28},{5,29},{6,14},{7,15},{8,0},{9,1... | collective-permute-start | bytes 1572872 | tf_op jit(solution)/shard_map/ppermute | solution.py:42
  187.1 9.4 %collective-permute-done.48 = bf16[128,2048]{1,0:T(8,128)(2,1)S(1)} collective-permute-done((bf16[128,2048]{1,0:T(8,128)(2,1)S(1)}, bf16[128,2048]{1,0:T(8,128)(2,1)S(1)}, u32[]{:S(2)}, u32[]{:S(2)}) %collective-permute-start.48) | collective-permute-done | bytes 524320 | tf_op jit(solution)/shard_map/ppermute | solution.py:42
  196.5 2.2 %collective-permute-done.47 = bf16[128,2048]{1,0:T(8,128)(2,1)S(1)} collective-permute-done((bf16[128,2048]{1,0:T(8,128)(2,1)S(1)}, bf16[128,2048]{1,0:T(8,128)(2,1)S(1)}, u32[]{:S(2)}, u32[]{:S(2)}) %collective-permute-start.47) | collective-permute-done | bytes 524320 | tf_op jit(solution)/shard_map/ppermute | solution.py:42
  202.2 12.4 %collective-permute-done.49 = bf16[128,2048]{1,0:T(8,128)(2,1)S(1)} collective-permute-done((bf16[128,2048]{1,0:T(8,128)(2,1)S(1)}, bf16[128,2048]{1,0:T(8,128)(2,1)S(1)}, u32[]{:S(2)}, u32[]{:S(2)}) %collective-permute-start.49) | collective-permute-done | bytes 524320 | tf_op jit(solution)/shard_map/ppermute | solution.py:42
  214.8 1.9 collective-permute-done.52
  (149 shorter events, 46.7 us)
Async XLA Ops:
  3.5 17.7 %collective-permute-start = (bf16[128,2176]{1,0:T(8,128)(2,1)S(1)}, bf16[128,2176]{1,0:T(8,128)(2,1)S(1)}, u32[]{:S(2)}, u32[]{:S(2)}) collective-permute-start(bf16[128,2176]{1,0:T(8,128)(2,1)S(1)} %fusion.1.refs_1_.refs_2_), channel_id=1, source_target_pairs={{0,8},{1,9},{2,26},{3,27},{4,12},{5,13},{6,30},{7,31},{8,16},{9,17... | collective-permute-start | bytes 1671176 | tf_op jit(solution)/shard_map/ppermute | solution.py:42
  6.6 14.7 %collective-permute-start.1 = (bf16[128,2176]{1,0:T(8,128)(2,1)S(1)}, bf16[128,2176]{1,0:T(8,128)(2,1)S(1)}, u32[]{:S(2)}, u32[]{:S(2)}) collective-permute-start(bf16[128,2176]{1,0:T(8,128)(2,1)S(1)} %fusion.1.refs_1_.refs_2_), channel_id=1, source_target_pairs={{0,4},{1,5},{2,6},{3,7},{4,0},{5,1},{6,2},{7,3},{8,12},{9,13},{10,... | collective-permute-start | bytes 1671176 | tf_op jit(solution)/shard_map/ppermute | solution.py:42
  21.3 14.1 %collective-permute-start.2 = (bf16[128,2176]{1,0:T(8,128)(2,1)S(1)}, bf16[128,2176]{1,0:T(8,128)(2,1)S(1)}, u32[]{:S(2)}, u32[]{:S(2)}) collective-permute-start(bf16[128,2176]{1,0:T(8,128)(2,1)S(1)} %collective-permute-done.refs_3_.refs_4_), channel_id=1, source_target_pairs={{0,1},{1,0},{2,3},{3,2},{4,5},{5,4},{6,7},{7,6},{8,9},{9,8},{10,11... | collective-permute-start | bytes 1671176 | tf_op jit(solution)/shard_map/ppermute | solution.py:42
  21.4 16.9 %collective-permute-start.3 = (bf16[128,2176]{1,0:T(8,128)(2,1)S(1)}, bf16[128,2176]{1,0:T(8,128)(2,1)}, u32[]{:S(2)}, u32[]{:S(2)}) collective-permute-start(bf16[128,2176]{1,0:T(8,128)(2,1)S(1)} %collective-permute-done.refs_3_.refs_4_), channel_id=1, source_target_pairs={{0,8},{1,9},{2,26},{3,27},{4,12},{5,13},{6,30},{7,31},{8,16},{9,17... | collective-permute-start | bytes 1671176 | tf_op jit(solution)/shard_map/ppermute | solution.py:42
  22.8 16.7 %collective-permute-start.4 = (bf16[128,2176]{1,0:T(8,128)(2,1)S(1)}, bf16[128,2176]{1,0:T(8,128)(2,1)S(1)}, u32[]{:S(2)}, u32[]{:S(2)}) collective-permute-start(bf16[128,2176]{1,0:T(8,128)(2,1)S(1)} %collective-permute-done.refs_3_.refs_4_), channel_id=1, source_target_pairs={{0,2},{1,3},{2,0},{3,1},{4,6},{5,7},{6,4},{7,5},{8,10},{9,11},{10,... | collective-permute-start | bytes 1671176 | tf_op jit(solution)/shard_map/ppermute | solution.py:42
  26.5 13.0 %collective-permute-start.5 = (bf16[128,2176]{1,0:T(8,128)(2,1)S(1)}, bf16[128,2176]{1,0:T(8,128)(2,1)S(1)}, u32[]{:S(2)}, u32[]{:S(2)}) collective-permute-start(bf16[128,2176]{1,0:T(8,128)(2,1)S(1)} %collective-permute-done.1.refs_2_.refs_3_), channel_id=1, source_target_pairs={{0,1},{1,0},{2,3},{3,2},{4,5},{5,4},{6,7},{7,6},{8,9},{9,8},{10,11... | collective-permute-start | bytes 1671176 | tf_op jit(solution)/shard_map/ppermute | solution.py:42
  26.5 15.1 %collective-permute-start.6 = (bf16[128,2176]{1,0:T(8,128)(2,1)S(1)}, bf16[128,2176]{1,0:T(8,128)(2,1)}, u32[]{:S(2)}, u32[]{:S(2)}) collective-permute-start(bf16[128,2176]{1,0:T(8,128)(2,1)S(1)} %collective-permute-done.refs_3_.refs_4_), channel_id=1, source_target_pairs={{0,4},{1,5},{2,6},{3,7},{4,0},{5,1},{6,2},{7,3},{8,12},{9,13},{10,... | collective-permute-start | bytes 1671176 | tf_op jit(solution)/shard_map/ppermute | solution.py:42
  45.5 17.8 %collective-permute-start.11 = (bf16[8,224,2048]{2,1,0:T(8,128)(2,1)}, bf16[8,224,2048]{2,1,0:T(8,128)(2,1)}, u32[]{:S(2)}, u32[]{:S(2)}) collective-permute-start(bf16[8,224,2048]{2,1,0:T(8,128)(2,1)} %get-tuple-element.294), channel_id=1, source_target_pairs={{0,1},{1,0},{2,3},{3,2},{4,5},{5,4},{6,7},{7,6},{8,9},{9,8},{10,11... | collective-permute-start | bytes 22020104 | tf_op jit(solution)/shard_map/ppermute | solution.py:42
  45.6 17.6 %collective-permute-start.12 = (bf16[128,2176]{1,0:T(8,128)(2,1)}, bf16[128,2176]{1,0:T(8,128)(2,1)}, u32[]{:S(2)}, u32[]{:S(2)}) collective-permute-start(bf16[128,2176]{1,0:T(8,128)(2,1)} %collective-permute-done.3.refs_1_.refs_2_), channel_id=1, source_target_pairs={{0,4},{1,5},{2,6},{3,7},{4,0},{5,1},{6,2},{7,3},{8,12},{9,13},{10,... | collective-permute-start | bytes 1671176 | tf_op jit(solution)/shard_map/ppermute | solution.py:42
  47.1 16.1 %collective-permute-start.13 = (bf16[128,2176]{1,0:T(8,128)(2,1)}, bf16[128,2176]{1,0:T(8,128)(2,1)}, u32[]{:S(2)}, u32[]{:S(2)}) collective-permute-start(bf16[128,2176]{1,0:T(8,128)(2,1)} %collective-permute-done.6.refs_4_.refs_5_), channel_id=1, source_target_pairs={{0,2},{1,3},{2,0},{3,1},{4,6},{5,7},{6,4},{7,5},{8,10},{9,11},{10,... | collective-permute-start | bytes 1671176 | tf_op jit(solution)/shard_map/ppermute | solution.py:42
  47.5 15.7 %collective-permute-start.10 = (bf16[128,2048]{1,0:T(8,128)(2,1)}, bf16[128,2048]{1,0:T(8,128)(2,1)}, u32[]{:S(2)}, u32[]{:S(2)}) collective-permute-start(bf16[128,2048]{1,0:T(8,128)(2,1)} %get-tuple-element.450.refs_3_), channel_id=1, source_target_pairs={{0,8},{1,9},{2,26},{3,27},{4,12},{5,13},{6,30},{7,31},{8,16},{9,17... | collective-permute-start | bytes 1572872 | tf_op jit(solution)/shard_map/ppermute | solution.py:42
  67.2 17.6 %collective-permute-start.17 = (bf16[128,2048]{1,0:T(8,128)(2,1)}, bf16[128,2048]{1,0:T(8,128)(2,1)}, u32[]{:S(2)}, u32[]{:S(2)}) collective-permute-start(bf16[128,2048]{1,0:T(8,128)(2,1)} %collective-permute-done.10.refs_5_), channel_id=1, source_target_pairs={{0,1},{1,0},{2,3},{3,2},{4,5},{5,4},{6,7},{7,6},{8,9},{9,8},{10,11... | collective-permute-start | bytes 1572872 | tf_op jit(solution)/shard_map/ppermute | solution.py:42
  67.4 17.4 %collective-permute-start.18 = (bf16[128,2048]{1,0:T(8,128)(2,1)}, bf16[128,2048]{1,0:T(8,128)(2,1)}, u32[]{:S(2)}, u32[]{:S(2)}) collective-permute-start(bf16[128,2048]{1,0:T(8,128)(2,1)} %collective-permute-done.10.refs_5_), channel_id=1, source_target_pairs={{0,8},{1,9},{2,26},{3,27},{4,12},{5,13},{6,30},{7,31},{8,16},{9,17... | collective-permute-start | bytes 1572872 | tf_op jit(solution)/shard_map/ppermute | solution.py:42
  67.4 17.4 %collective-permute-start.19 = (bf16[128,2048]{1,0:T(8,128)(2,1)}, bf16[128,2048]{1,0:T(8,128)(2,1)}, u32[]{:S(2)}, u32[]{:S(2)}) collective-permute-start(bf16[128,2048]{1,0:T(8,128)(2,1)} %collective-permute-done.10.refs_5_), channel_id=1, source_target_pairs={{0,2},{1,3},{2,0},{3,1},{4,6},{5,7},{6,4},{7,5},{8,10},{9,11},{10,... | collective-permute-start | bytes 1572872 | tf_op jit(solution)/shard_map/ppermute | solution.py:42
  69.9 14.9 %collective-permute-start.20 = (bf16[128,2048]{1,0:T(8,128)(2,1)}, bf16[128,2048]{1,0:T(8,128)(2,1)}, u32[]{:S(2)}, u32[]{:S(2)}) collective-permute-start(bf16[128,2048]{1,0:T(8,128)(2,1)} %collective-permute-done.10.refs_5_), channel_id=1, source_target_pairs={{0,4},{1,5},{2,6},{3,7},{4,0},{5,1},{6,2},{7,3},{8,12},{9,13},{10,... | collective-permute-start | bytes 1572872 | tf_op jit(solution)/shard_map/ppermute | solution.py:42
  70.4 14.4 %collective-permute-start.21 = (bf16[8,224,2048]{2,1,0:T(8,128)(2,1)}, bf16[8,224,2048]{2,1,0:T(8,128)(2,1)}, u32[]{:S(2)}, u32[]{:S(2)}) collective-permute-start(bf16[8,224,2048]{2,1,0:T(8,128)(2,1)} %get-tuple-element.344), channel_id=1, source_target_pairs={{0,1},{1,0},{2,3},{3,2},{4,5},{5,4},{6,7},{7,6},{8,9},{9,8},{10,11... | collective-permute-start | bytes 22020104 | tf_op jit(solution)/shard_map/ppermute | solution.py:42
  91.1 18.1 %collective-permute-start.27 = (bf16[128,2048]{1,0:T(8,128)(2,1)}, bf16[128,2048]{1,0:T(8,128)(2,1)}, u32[]{:S(2)}, u32[]{:S(2)}) collective-permute-start(bf16[128,2048]{1,0:T(8,128)(2,1)} %collective-permute-done.20.refs_6_), channel_id=1, source_target_pairs={{0,8},{1,9},{2,26},{3,27},{4,12},{5,13},{6,30},{7,31},{8,16},{9,17... | collective-permute-start | bytes 1572872 | tf_op jit(solution)/shard_map/ppermute | solution.py:42
  92.6 16.6 %collective-permute-start.28 = (bf16[128,2048]{1,0:T(8,128)(2,1)}, bf16[128,2048]{1,0:T(8,128)(2,1)}, u32[]{:S(2)}, u32[]{:S(2)}) collective-permute-start(bf16[128,2048]{1,0:T(8,128)(2,1)} %collective-permute-done.20.refs_6_), channel_id=1, source_target_pairs={{0,2},{1,3},{2,0},{3,1},{4,6},{5,7},{6,4},{7,5},{8,10},{9,11},{10,... | collective-permute-start | bytes 1572872 | tf_op jit(solution)/shard_map/ppermute | solution.py:42
  94.5 14.7 %collective-permute-start.29 = (bf16[8,224,2048]{2,1,0:T(8,128)(2,1)}, bf16[8,224,2048]{2,1,0:T(8,128)(2,1)}, u32[]{:S(2)}, u32[]{:S(2)}) collective-permute-start(bf16[8,224,2048]{2,1,0:T(8,128)(2,1)} %constant_dynamic-slice_fusion), channel_id=1, source_target_pairs={{0,1},{1,0},{2,3},{3,2},{4,5},{5,4},{6,7},{7,6},{8,9},{9,8},{10,11... | collective-permute-start | bytes 22020104 | tf_op jit(solution)/shard_map/ppermute | solution.py:42
  94.5 14.7 %collective-permute-start.26 = (bf16[128,2048]{1,0:T(8,128)(2,1)}, bf16[128,2048]{1,0:T(8,128)(2,1)}, u32[]{:S(2)}, u32[]{:S(2)}) collective-permute-start(bf16[128,2048]{1,0:T(8,128)(2,1)} %get-tuple-element.450.refs_3_), channel_id=1, source_target_pairs={{0,4},{1,5},{2,6},{3,7},{4,0},{5,1},{6,2},{7,3},{8,12},{9,13},{10,... | collective-permute-start | bytes 1572872 | tf_op jit(solution)/shard_map/ppermute | solution.py:42
  112.9 16.4 %collective-permute-start.33 = (bf16[128,2048]{1,0:T(8,128)(2,1)}, bf16[128,2048]{1,0:T(8,128)(2,1)}, u32[]{:S(2)}, u32[]{:S(2)}) collective-permute-start(bf16[128,2048]{1,0:T(8,128)(2,1)} %get-tuple-element.472), channel_id=1, source_target_pairs={{0,4},{1,5},{2,6},{3,7},{4,0},{5,1},{6,2},{7,3},{8,12},{9,13},{10,... | collective-permute-start | bytes 1572872 | tf_op jit(solution)/shard_map/ppermute | solution.py:42
  114.3 15.0 %collective-permute-start.34 = (bf16[128,2048]{1,0:T(8,128)(2,1)}, bf16[128,2048]{1,0:T(8,128)(2,1)}, u32[]{:S(2)}, u32[]{:S(2)}) collective-permute-start(bf16[128,2048]{1,0:T(8,128)(2,1)} %get-tuple-element.474), channel_id=1, source_target_pairs={{0,2},{1,3},{2,0},{3,1},{4,6},{5,7},{6,4},{7,5},{8,10},{9,11},{10,... | collective-permute-start | bytes 1572872 | tf_op jit(solution)/shard_map/ppermute | solution.py:42
  114.5 14.8 %collective-permute-start.35 = (bf16[128,2048]{1,0:T(8,128)(2,1)}, bf16[128,2048]{1,0:T(8,128)(2,1)}, u32[]{:S(2)}, u32[]{:S(2)}) collective-permute-start(bf16[128,2048]{1,0:T(8,128)(2,1)} %get-tuple-element.473), channel_id=1, source_target_pairs={{0,24},{1,25},{2,10},{3,11},{4,28},{5,29},{6,14},{7,15},{8,0},{9,1... | collective-permute-start | bytes 1572872 | tf_op jit(solution)/shard_map/ppermute | solution.py:42
  134.6 19.2 %collective-permute-start.38 = (bf16[128,2048]{1,0:T(8,128)(2,1)}, bf16[128,2048]{1,0:T(8,128)(2,1)}, u32[]{:S(2)}, u32[]{:S(2)}) collective-permute-start(bf16[128,2048]{1,0:T(8,128)(2,1)} %add_convert_fusion.8), channel_id=1, source_target_pairs={{0,4},{1,5},{2,6},{3,7},{4,0},{5,1},{6,2},{7,3},{8,12},{9,13},{10,... | collective-permute-start | bytes 1572872 | tf_op jit(solution)/shard_map/ppermute | solution.py:42
  135.1 18.7 %collective-permute-start.39 = (bf16[128,2048]{1,0:T(8,128)(2,1)}, bf16[128,2048]{1,0:T(8,128)(2,1)}, u32[]{:S(2)}, u32[]{:S(2)}) collective-permute-start(bf16[128,2048]{1,0:T(8,128)(2,1)} %get-tuple-element.498), channel_id=1, source_target_pairs={{0,2},{1,3},{2,0},{3,1},{4,6},{5,7},{6,4},{7,5},{8,10},{9,11},{10,... | collective-permute-start | bytes 1572872 | tf_op jit(solution)/shard_map/ppermute | solution.py:42
  137.6 16.1 %collective-permute-start.40 = (bf16[128,2048]{1,0:T(8,128)(2,1)}, bf16[128,2048]{1,0:T(8,128)(2,1)}, u32[]{:S(2)}, u32[]{:S(2)}) collective-permute-start(bf16[128,2048]{1,0:T(8,128)(2,1)} %get-tuple-element.497), channel_id=1, source_target_pairs={{0,24},{1,25},{2,10},{3,11},{4,28},{5,29},{6,14},{7,15},{8,0},{9,1... | collective-permute-start | bytes 1572872 | tf_op jit(solution)/shard_map/ppermute | solution.py:42
  154.0 13.1 %collective-permute-start.41 = (bf16[128,2048]{1,0:T(8,128)(2,1)S(1)}, bf16[128,2048]{1,0:T(8,128)(2,1)S(1)}, u32[]{:S(2)}, u32[]{:S(2)}) collective-permute-start(bf16[128,2048]{1,0:T(8,128)(2,1)S(1)} %get-tuple-element.529), channel_id=1, source_target_pairs={{0,4},{1,5},{2,6},{3,7},{4,0},{5,1},{6,2},{7,3},{8,12},{9,13},{10,... | collective-permute-start | bytes 1572872 | tf_op jit(solution)/shard_map/ppermute | solution.py:42
  155.5 12.8 %collective-permute-start.42 = (bf16[128,2048]{1,0:T(8,128)(2,1)S(1)}, bf16[128,2048]{1,0:T(8,128)(2,1)S(1)}, u32[]{:S(2)}, u32[]{:S(2)}) collective-permute-start(bf16[128,2048]{1,0:T(8,128)(2,1)S(1)} %get-tuple-element.528), channel_id=1, source_target_pairs={{0,2},{1,3},{2,0},{3,1},{4,6},{5,7},{6,4},{7,5},{8,10},{9,11},{10,... | collective-permute-start | bytes 1572872 | tf_op jit(solution)/shard_map/ppermute | solution.py:42
  157.4 14.7 %collective-permute-start.46 = (bf16[128,2048]{1,0:T(8,128)(2,1)S(1)}, bf16[128,2048]{1,0:T(8,128)(2,1)S(1)}, u32[]{:S(2)}, u32[]{:S(2)}) collective-permute-start(bf16[128,2048]{1,0:T(8,128)(2,1)S(1)} %add_convert_fusion.5), channel_id=1, source_target_pairs={{0,24},{1,25},{2,10},{3,11},{4,28},{5,29},{6,14},{7,15},{8,0},{9,1... | collective-permute-start | bytes 1572872 | tf_op jit(solution)/shard_map/ppermute | solution.py:42
  169.4 12.5 %collective-permute-start.45 = (bf16[128,2048]{1,0:T(8,128)(2,1)S(1)}, bf16[128,2048]{1,0:T(8,128)(2,1)S(1)}, u32[]{:S(2)}, u32[]{:S(2)}) collective-permute-start(bf16[128,2048]{1,0:T(8,128)(2,1)S(1)} %get-tuple-element.527), channel_id=1, source_target_pairs={{0,24},{1,25},{2,10},{3,11},{4,28},{5,29},{6,14},{7,15},{8,0},{9,1... | collective-permute-start | bytes 1572872 | tf_op jit(solution)/shard_map/ppermute | solution.py:42
  182.9 13.7 %collective-permute-start.48 = (bf16[128,2048]{1,0:T(8,128)(2,1)S(1)}, bf16[128,2048]{1,0:T(8,128)(2,1)S(1)}, u32[]{:S(2)}, u32[]{:S(2)}) collective-permute-start(bf16[128,2048]{1,0:T(8,128)(2,1)S(1)} %add_convert_fusion.3), channel_id=1, source_target_pairs={{0,24},{1,25},{2,10},{3,11},{4,28},{5,29},{6,14},{7,15},{8,0},{9,1... | collective-permute-start | bytes 1572872 | tf_op jit(solution)/shard_map/ppermute | solution.py:42
  200.3 14.4 %collective-permute-start.49 = (bf16[128,2048]{1,0:T(8,128)(2,1)S(1)}, bf16[128,2048]{1,0:T(8,128)(2,1)S(1)}, u32[]{:S(2)}, u32[]{:S(2)}) collective-permute-start(bf16[128,2048]{1,0:T(8,128)(2,1)S(1)} %add_convert_fusion.2), channel_id=1, source_target_pairs={{0,2},{1,3},{2,0},{3,1},{4,6},{5,7},{6,4},{7,5},{8,10},{9,11},{10,... | collective-permute-start | bytes 1572872 | tf_op jit(solution)/shard_map/ppermute | solution.py:42
  (43 other events, 388.1 us)

commit v4 on v3

--- a/solution.py
+++ b/solution.py
@@ -290,6 +290,32 @@
     return columns.astype(jnp.bfloat16)
 
 
+def first_kernel(core_ref, half_ref, ids_ref, probs_ref, out_ref):
+    tokens, half = half_ref.shape
+    out_ref[:, pl.ds(0, half)] = half_ref[...]
+    ids, probs = ids_ref[...].astype(jnp.float32), probs_ref[...]
+    rest = jnp.zeros((LANES - 2 * ids.shape[0], tokens), jnp.float32)
+    columns = jnp.concatenate([ids, probs, rest], axis=0).T
+    out_ref[:, pl.ds(half, LANES)] = columns.astype(jnp.bfloat16)
+
+
+def first_piece(core, tokens, expert_ids, gate_probs):
+    count, features = tokens.shape
+    half = features // 2
+    whole = pl.BlockSpec((expert_ids.shape[1], count), lambda i, c: (0, 0))
+    return pl.pallas_call(
+        first_kernel,
+        grid_spec=pltpu.PrefetchScalarGridSpec(
+            num_scalar_prefetch=1,
+            grid=(1,),
+            in_specs=[pl.BlockSpec((count, half), lambda i, c: (0, c[0])), whole, whole],
+            out_specs=pl.BlockSpec((count, half + LANES), lambda i, c: (0, 0)),
+        ),
+        out_shape=jax.ShapeDtypeStruct((count, half + LANES), jnp.bfloat16),
+        name="first_piece",
+    )(core, tokens, expert_ids.T, gate_probs.T)
+
+
 def route_kernel(sources, group, capacity, *refs):
     first_ref = refs[0]
     choice_refs = refs[1 : 1 + sources]
@@ -369,7 +395,7 @@
     own_choices = choice_columns(expert_ids, gate_probs)
     if fast:
         return exchange(
-            routed, own_choices, tokens, cotangent, w_gate, w_up, w_down
+            routed, expert_ids, gate_probs, tokens, cotangent, w_gate, w_up, w_down
         )
 
     def split(array):
@@ -396,7 +422,7 @@
     return total(place_t_prob, (hidden,), (w_down,)), total(place_t, values, (w_gate, w_up))
 
 
-def exchange(routed, own_choices, tokens, cotangent, w_gate, w_up, w_down):
+def exchange(routed, expert_ids, gate_probs, tokens, cotangent, w_gate, w_up, w_down):
     half = tokens.shape[1] // 2
     core = lax.axis_index("tensor") % 2
     mine = core.astype(jnp.int32).reshape(1)
@@ -423,8 +449,8 @@
         return live[kind][start : start + rows]
 
     near, late = order[:4], order[4:]
-    tq0, tq0_far = halves(tokens, core)
-    live = dict(mine=mine, tq0=jnp.concatenate([tq0, own_choices], axis=1), tq0_far=tq0_far)
+    tq0 = first_piece(mine, tokens, expert_ids, gate_probs)
+    live = dict(mine=mine, tq0=tq0, tq0_far=halves(tokens, core)[1])
     cq0, cq0_far = halves(cotangent, core)
     live = phase(
         live,

time: 219 us -> 218 us (level)
    unnamed x44 -> x46, local copies, waits for them, and re-layouts: 6.94 us -> 7 us
where the time goes in v4:
time: 218 us; the launch traced here: 217 us
  Pallas kernels  72.3 us (33%)
  waiting for transfers between devices  57.8 us (27%)
  starting transfers between devices  44.5 us (20%)
  local copies, waits for them, and re-layouts  31.3 us (14%)
  other arithmetic  10.2 us (5%)
    ppermute x53, waiting for transfers between devices, move(): return lax.ppermute(array, AXES, MOVES[name])  57.8 us
    ppermute x53, starting transfers between devices, move(): return lax.ppermute(array, AXES, MOVES[name])  44.5 us
    pallas_call x3, Pallas kernels, enter(): pl.pallas_call(functools.partial(enter_kernel, backward, len(places), sou...  40.1 us
    pallas_call x2, Pallas kernels, leave(): pl.pallas_call(functools.partial(leave_kernel, len(places), len(weights))...  25.7 us
    dynamic_slice x2, local copies, waits for them, and re-layouts, sibling_half(): return lax.dynamic_slice_in_dim(weight, (1 - core) * half, half, 2)  18.2 us
    convert_element_type x8, other arithmetic, add(): return total.astype(jnp.bfloat16)  7.92 us
    unnamed x46, local copies, waits for them, and re-layouts  7 us
    pallas_call x2, Pallas kernels, route(): pl.pallas_call(functools.partial(route_kernel, sources, group, capacity),...  4.42 us
  transfers between devices with their start and end apart: 53, of which 24 were waited for; matrix products, arithmetic and copies ran while one was open for 15% of the time, Pallas kernels for 32%

profile of v4, /device:TPU:0, one launch (start us, length us, event | category | flops | bytes accessed | tf_op | source)
XLA Modules:
  0.0 217.2 jit_solution(8000671236851256832)
XLA Ops:
  0.6 2.0 first_piece.1.refs_1_.refs_2_
  2.6 3.0 %collective-permute-start = (bf16[128,2176]{1,0:T(8,128)(2,1)}, bf16[128,2176]{1,0:T(8,128)(2,1)S(1)}, u32[]{:S(2)}, u32[]{:S(2)}) collective-permute-start(bf16[128,2176]{1,0:T(8,128)(2,1)} %first_piece.1.refs_1_.refs_2_), channel_id=1, source_target_pairs={{0,8},{1,9},{2,26},{3,27},{4,12},{5,13},{6,30},{7,31},{8,16},{9,17... | collective-permute-start | bytes 1671176 | tf_op jit(solution)/shard_map/ppermute | solution.py:42
  7.1 2.3 %constant_dynamic-slice_fusion.4 = (bf16[128,2048]{1,0:T(8,128)(2,1)S(1)}, bf16[128,2048]{1,0:T(8,128)(2,1)}, bf16[128,2048]{1,0:T(8,128)(2,1)S(1)}) fusion(bf16[128,4096]{1,0:T(8,128)(2,1)} %param.20, s32[]{:T(128)S(6)} %select_n.39, s32[]{:T(128)S(6)} %select_n.38, bf16[128,4096]{1,0:T(8,128)(2,1)} %half_ref.1), kind=kLoop, calls=%fused_computation.19 | loop fusion | bytes 3145736 | tf_op jit(solution)/shard_map/dynamic_slice | solution.py:55
  9.4 10.8 %constant_dynamic-slice_fusion.2 = (bf16[8,224,2048]{2,1,0:T(8,128)(2,1)}, bf16[8,224,2048]{2,1,0:T(8,128)(2,1)}) fusion(bf16[8,224,4096]{2,1,0:T(8,128)(2,1)} %refs_7_.5, s32[]{:T(128)S(6)} %select_n.39, bf16[8,224,4096]{2,1,0:T(8,128)(2,1)} %refs_19_.1), kind=kLoop, calls=%fused_computation.17 | loop fusion | bytes 29360132 | tf_op jit(solution)/shard_map/dynamic_slice | solution.py:444
  22.0 3.7 %collective-permute-start.4 = (bf16[128,2176]{1,0:T(8,128)(2,1)S(1)}, bf16[128,2176]{1,0:T(8,128)(2,1)S(1)}, u32[]{:S(2)}, u32[]{:S(2)}) collective-permute-start(bf16[128,2176]{1,0:T(8,128)(2,1)S(1)} %collective-permute-done.refs_3_.refs_4_), channel_id=1, source_target_pairs={{0,2},{1,3},{2,0},{3,1},{4,6},{5,7},{6,4},{7,5},{8,10},{9,11},{10,... | collective-permute-start | bytes 1671176 | tf_op jit(solution)/shard_map/ppermute | solution.py:42
  27.2 7.5 %constant_dynamic-slice_fusion = bf16[8,224,2048]{2,1,0:T(8,128)(2,1)} fusion(bf16[8,224,4096]{2,1,0:T(8,128)(2,1)} %refs_8_.3, s32[]{:T(128)S(6)} %select_n.39), kind=kLoop, calls=%fused_computation.15 | loop fusion | bytes 14680068 | tf_op jit(solution)/shard_map/dynamic_slice | solution.py:444
  35.5 2.0 collective-permute-done.3.refs_1_.refs_2_
  41.5 2.2 %route.2 = (bf16[2,384,256]{2,1,0:T(8,128)(2,1)S(1)}, bf16[2,384,256]{2,1,0:T(8,128)(2,1)S(1)}, bf16[2,256,384]{2,1,0:T(8,128)(2,1)S(1)}, bf16[2,256,384]{2,1,0:T(8,128)(2,1)S(1)}) custom-call(s32[1]{0:T(128)} %bitcast.3.refs_0_, bf16[128,2176]{1,0:T(8,128)(2,1)S(1)} %copy-done.2, bf16[128,2176]{1,0:T(8,128)(2,1)S(1)} %collective-permute-done.1.refs_2_.refs_3_, ...), custom_call_target="tpu_custom_call" | custom-call | tf_op jit(solution)/shard_map/route/pallas_call | solution.py:368
  48.9 13.4 %enter_forward.2 = (bf16[8,96,224]{2,1,0:T(8,128)(2,1)S(1)}, f32[8,96,224]{2,1,0:T(8,128)S(1)}, f32[8,96,224]{2,1,0:T(8,128)S(1)}) custom-call(s32[1]{0:T(128)} %bitcast.core_ref.refs_0_, bf16[2,384,256]{2,1,0:T(8,128)(2,1)S(1)} %get-tuple-element.297.refs_1_, bf16[128,2176]{1,0:T(8,128)(2,1)S(1)} %copy-done.2, ...), custom_call_target="tpu_custom_call" | custom-call | flops 283467841536 | bytes 33554432 | tf_op jit(solution)/shard_map/enter_forward/pallas_call | solution.py:174
  63.2 2.2 %route.3 = (bf16[2,384,256]{2,1,0:T(8,128)(2,1)S(1)}, bf16[2,384,256]{2,1,0:T(8,128)(2,1)S(1)}, bf16[2,256,384]{2,1,0:T(8,128)(2,1)S(1)}, bf16[2,256,384]{2,1,0:T(8,128)(2,1)S(1)}) custom-call(s32[1]{0:T(128)} %bitcast.3.refs_0_, bf16[128,2176]{1,0:T(8,128)(2,1)} %collective-permute-done.3.refs_1_.refs_2_, ...), custom_call_target="tpu_custom_call" | custom-call | tf_op jit(solution)/shard_map/route/pallas_call | solution.py:368
  66.7 2.5 %collective-permute-start.19 = (bf16[128,2048]{1,0:T(8,128)(2,1)}, bf16[128,2048]{1,0:T(8,128)(2,1)}, u32[]{:S(2)}, u32[]{:S(2)}) collective-permute-start(bf16[128,2048]{1,0:T(8,128)(2,1)} %collective-permute-done.10.refs_5_), channel_id=1, source_target_pairs={{0,2},{1,3},{2,0},{3,1},{4,6},{5,7},{6,4},{7,5},{8,10},{9,11},{10,... | collective-permute-start | bytes 1572872 | tf_op jit(solution)/shard_map/ppermute | solution.py:42
  69.7 14.3 %enter_forward.3 = (bf16[8,96,224]{2,1,0:T(8,128)(2,1)S(1)}, f32[8,96,224]{2,1,0:T(8,128)S(1)}, f32[8,96,224]{2,1,0:T(8,128)S(1)}) custom-call(s32[1]{0:T(128)} %bitcast.core_ref.refs_0_, bf16[2,384,256]{2,1,0:T(8,128)(2,1)S(1)} %get-tuple-element.347.refs_1_, bf16[128,2176]{1,0:T(8,128)(2,1)} %collective-permute-done.3.refs_1_.refs_2_, ...), custom_call_target="tpu_custom_call" | custom-call | flops 283467841536 | bytes 33554432 | tf_op jit(solution)/shard_map/enter_forward/pallas_call | solution.py:174
  85.3 2.7 %collective-permute-done.25.refs_6_ = bf16[8,96,224]{2,1,0:T(8,128)(2,1)S(1)} collective-permute-done((bf16[8,96,224]{2,1,0:T(8,128)(2,1)S(1)}, bf16[8,96,224]{2,1,0:T(8,128)(2,1)S(1)}, u32[]{:S(2)}, u32[]{:S(2)}) %collective-permute-start.25) | collective-permute-done | bytes 344096 | tf_op jit(solution)/shard_map/ppermute | solution.py:42
  91.9 1.9 collective-permute-start.28
  95.3 10.5 %leave.2 = bf16[1024,2048]{1,0:T(8,128)(2,1)S(1)} custom-call(s32[1]{0:T(128)} %bitcast.core_ref.refs_0_, bf16[2,256,384]{2,1,0:T(8,128)(2,1)S(1)} %get-tuple-element.417.refs_1_, bf16[2,256,384]{2,1,0:T(8,128)(2,1)S(1)} %get-tuple-element.409.refs_2_, bf16[8,96,224]{2,1,0:T(8,128)(2,1)S(1)} %copy-done.20, bf16[8,96,224]{2,1,0:T(8,128)(2,1)S(1)} %copy-done.22, ...), custom_call_target="tpu_custom_call" | custom-call | flops 283467841536 | bytes 18874368 | tf_op jit(solution)/shard_map/leave/pallas_call | solution.py:255
  105.9 2.6 %collective-permute-done.26.refs_4_ = bf16[128,2048]{1,0:T(8,128)(2,1)} collective-permute-done((bf16[128,2048]{1,0:T(8,128)(2,1)}, bf16[128,2048]{1,0:T(8,128)(2,1)}, u32[]{:S(2)}, u32[]{:S(2)}) %collective-permute-start.26) | collective-permute-done | bytes 524320 | tf_op jit(solution)/shard_map/ppermute | solution.py:42
  113.8 2.3 %collective-permute-start.35 = (bf16[128,2048]{1,0:T(8,128)(2,1)}, bf16[128,2048]{1,0:T(8,128)(2,1)}, u32[]{:S(2)}, u32[]{:S(2)}) collective-permute-start(bf16[128,2048]{1,0:T(8,128)(2,1)} %get-tuple-element.473), channel_id=1, source_target_pairs={{0,24},{1,25},{2,10},{3,11},{4,28},{5,29},{6,14},{7,15},{8,0},{9,1... | collective-permute-start | bytes 1572872 | tf_op jit(solution)/shard_map/ppermute | solution.py:42
  116.1 12.5 %enter_backward.1 = (bf16[8,192,224]{2,1,0:T(8,128)(2,1)S(1)}, bf16[8,192,224]{2,1,0:T(8,128)(2,1)S(1)}) custom-call(s32[1]{0:T(128)} %bitcast.core_ref.refs_0_, bf16[2,384,256]{2,1,0:T(8,128)(2,1)S(1)} %get-tuple-element.448.refs_1_, bf16[2,384,256]{2,1,0:T(8,128)(2,1)S(1)} %get-tuple-element.449.refs_2_, bf16[128,2048]{1,0:T(8,128)(2,1)} %get-tuple-element.450.refs_3_, ...), custom_call_target="tpu_custom_call" | custom-call | flops 386547056640 | bytes 23068672 | tf_op jit(solution)/shard_map/enter_backward/pallas_call | solution.py:174
  129.2 2.3 %fusion.1 = (bf16[128,2048]{1,0:T(8,128)(2,1)}, bf16[128,2048]{1,0:T(8,128)(2,1)}) fusion(bf16[1024,2048]{1,0:T(8,128)(2,1)} %copy-done.1), kind=kLoop, calls=%fused_computation.22 | loop fusion | bytes 2097152 | tf_op jit(solution)/shard_map/slice | solution.py:449
  131.5 2.4 %add_convert_fusion.8 = bf16[128,2048]{1,0:T(8,128)(2,1)} fusion(bf16[128,2048]{1,0:T(8,128)(2,1)} %collective-permute-done.35, bf16[128,2048]{1,0:T(8,128)(2,1)} %collective-permute-done.34, bf16[1024,2048]{1,0:T(8,128)(2,1)} %copy-done.1), kind=kLoop, calls=%fused_computation.10 | loop fusion | flops 1572864 | bytes 2097152 | tf_op jit(solution)/shard_map/convert_element_type | solution.py:49
  134.4 2.5 %collective-permute-start.39 = (bf16[128,2048]{1,0:T(8,128)(2,1)}, bf16[128,2048]{1,0:T(8,128)(2,1)}, u32[]{:S(2)}, u32[]{:S(2)}) collective-permute-start(bf16[128,2048]{1,0:T(8,128)(2,1)} %get-tuple-element.498), channel_id=1, source_target_pairs={{0,2},{1,3},{2,0},{3,1},{4,6},{5,7},{6,4},{7,5},{8,10},{9,11},{10,... | collective-permute-start | bytes 1572872 | tf_op jit(solution)/shard_map/ppermute | solution.py:42
  137.8 15.2 %leave.3 = bf16[1024,2048]{1,0:T(8,128)(2,1)S(1)} custom-call(s32[1]{0:T(128)} %bitcast.core_ref.refs_0_, bf16[2,256,384]{2,1,0:T(8,128)(2,1)S(1)} %get-tuple-element.487.refs_1_, bf16[2,256,384]{2,1,0:T(8,128)(2,1)S(1)} %get-tuple-element.488.refs_2_, bf16[8,192,224]{2,1,0:T(8,128)(2,1)S(1)} %get-tuple-element.489.refs_3_, ...), custom_call_target="tpu_custom_call" | custom-call | flops 463856467968 | bytes 33554432 | tf_op jit(solution)/shard_map/leave/pallas_call | solution.py:255
  153.3 1.5 collective-permute-start.41
  154.8 1.8 add_convert_fusion.5
  156.7 3.0 %collective-permute-start.46 = (bf16[128,2048]{1,0:T(8,128)(2,1)S(1)}, bf16[128,2048]{1,0:T(8,128)(2,1)S(1)}, u32[]{:S(2)}, u32[]{:S(2)}) collective-permute-start(bf16[128,2048]{1,0:T(8,128)(2,1)S(1)} %add_convert_fusion.5), channel_id=1, source_target_pairs={{0,24},{1,25},{2,10},{3,11},{4,28},{5,29},{6,14},{7,15},{8,0},{9,1... | collective-permute-start | bytes 1572872 | tf_op jit(solution)/shard_map/ppermute | solution.py:42
  159.7 6.7 %collective-permute-done.41 = bf16[128,2048]{1,0:T(8,128)(2,1)S(1)} collective-permute-done((bf16[128,2048]{1,0:T(8,128)(2,1)S(1)}, bf16[128,2048]{1,0:T(8,128)(2,1)S(1)}, u32[]{:S(2)}, u32[]{:S(2)}) %collective-permute-start.41) | collective-permute-done | bytes 524320 | tf_op jit(solution)/shard_map/ppermute | solution.py:42
  172.9 7.1 %collective-permute-done.43 = bf16[128,2048]{1,0:T(8,128)(2,1)S(1)} collective-permute-done((bf16[128,2048]{1,0:T(8,128)(2,1)S(1)}, bf16[128,2048]{1,0:T(8,128)(2,1)S(1)}, u32[]{:S(2)}, u32[]{:S(2)}) %collective-permute-start.43) | collective-permute-done | bytes 524320 | tf_op jit(solution)/shard_map/ppermute | solution.py:42
  182.1 3.7 %collective-permute-start.48 = (bf16[128,2048]{1,0:T(8,128)(2,1)S(1)}, bf16[128,2048]{1,0:T(8,128)(2,1)S(1)}, u32[]{:S(2)}, u32[]{:S(2)}) collective-permute-start(bf16[128,2048]{1,0:T(8,128)(2,1)S(1)} %add_convert_fusion.3), channel_id=1, source_target_pairs={{0,24},{1,25},{2,10},{3,11},{4,28},{5,29},{6,14},{7,15},{8,0},{9,1... | collective-permute-start | bytes 1572872 | tf_op jit(solution)/shard_map/ppermute | solution.py:42
  186.4 9.4 %collective-permute-done.48 = bf16[128,2048]{1,0:T(8,128)(2,1)S(1)} collective-permute-done((bf16[128,2048]{1,0:T(8,128)(2,1)S(1)}, bf16[128,2048]{1,0:T(8,128)(2,1)S(1)}, u32[]{:S(2)}, u32[]{:S(2)}) %collective-permute-start.48) | collective-permute-done | bytes 524320 | tf_op jit(solution)/shard_map/ppermute | solution.py:42
  195.8 2.2 %collective-permute-done.47 = bf16[128,2048]{1,0:T(8,128)(2,1)S(1)} collective-permute-done((bf16[128,2048]{1,0:T(8,128)(2,1)S(1)}, bf16[128,2048]{1,0:T(8,128)(2,1)S(1)}, u32[]{:S(2)}, u32[]{:S(2)}) %collective-permute-start.47) | collective-permute-done | bytes 524320 | tf_op jit(solution)/shard_map/ppermute | solution.py:42
  201.5 12.4 %collective-permute-done.49 = bf16[128,2048]{1,0:T(8,128)(2,1)S(1)} collective-permute-done((bf16[128,2048]{1,0:T(8,128)(2,1)S(1)}, bf16[128,2048]{1,0:T(8,128)(2,1)S(1)}, u32[]{:S(2)}, u32[]{:S(2)}) %collective-permute-start.49) | collective-permute-done | bytes 524320 | tf_op jit(solution)/shard_map/ppermute | solution.py:42
  214.1 1.9 collective-permute-done.52
  (146 shorter events, 45.5 us)
Async XLA Ops:
  2.6 17.9 %collective-permute-start = (bf16[128,2176]{1,0:T(8,128)(2,1)}, bf16[128,2176]{1,0:T(8,128)(2,1)S(1)}, u32[]{:S(2)}, u32[]{:S(2)}) collective-permute-start(bf16[128,2176]{1,0:T(8,128)(2,1)} %first_piece.1.refs_1_.refs_2_), channel_id=1, source_target_pairs={{0,8},{1,9},{2,26},{3,27},{4,12},{5,13},{6,30},{7,31},{8,16},{9,17... | collective-permute-start | bytes 1671176 | tf_op jit(solution)/shard_map/ppermute | solution.py:42
  5.6 14.9 %collective-permute-start.1 = (bf16[128,2176]{1,0:T(8,128)(2,1)}, bf16[128,2176]{1,0:T(8,128)(2,1)S(1)}, u32[]{:S(2)}, u32[]{:S(2)}) collective-permute-start(bf16[128,2176]{1,0:T(8,128)(2,1)} %first_piece.1.refs_1_.refs_2_), channel_id=1, source_target_pairs={{0,4},{1,5},{2,6},{3,7},{4,0},{5,1},{6,2},{7,3},{8,12},{9,13},{10,... | collective-permute-start | bytes 1671176 | tf_op jit(solution)/shard_map/ppermute | solution.py:42
  20.6 14.1 %collective-permute-start.2 = (bf16[128,2176]{1,0:T(8,128)(2,1)S(1)}, bf16[128,2176]{1,0:T(8,128)(2,1)S(1)}, u32[]{:S(2)}, u32[]{:S(2)}) collective-permute-start(bf16[128,2176]{1,0:T(8,128)(2,1)S(1)} %collective-permute-done.refs_3_.refs_4_), channel_id=1, source_target_pairs={{0,1},{1,0},{2,3},{3,2},{4,5},{5,4},{6,7},{7,6},{8,9},{9,8},{10,11... | collective-permute-start | bytes 1671176 | tf_op jit(solution)/shard_map/ppermute | solution.py:42
  20.6 16.9 %collective-permute-start.3 = (bf16[128,2176]{1,0:T(8,128)(2,1)S(1)}, bf16[128,2176]{1,0:T(8,128)(2,1)}, u32[]{:S(2)}, u32[]{:S(2)}) collective-permute-start(bf16[128,2176]{1,0:T(8,128)(2,1)S(1)} %collective-permute-done.refs_3_.refs_4_), channel_id=1, source_target_pairs={{0,8},{1,9},{2,26},{3,27},{4,12},{5,13},{6,30},{7,31},{8,16},{9,17... | collective-permute-start | bytes 1671176 | tf_op jit(solution)/shard_map/ppermute | solution.py:42
  22.0 16.7 %collective-permute-start.4 = (bf16[128,2176]{1,0:T(8,128)(2,1)S(1)}, bf16[128,2176]{1,0:T(8,128)(2,1)S(1)}, u32[]{:S(2)}, u32[]{:S(2)}) collective-permute-start(bf16[128,2176]{1,0:T(8,128)(2,1)S(1)} %collective-permute-done.refs_3_.refs_4_), channel_id=1, source_target_pairs={{0,2},{1,3},{2,0},{3,1},{4,6},{5,7},{6,4},{7,5},{8,10},{9,11},{10,... | collective-permute-start | bytes 1671176 | tf_op jit(solution)/shard_map/ppermute | solution.py:42
  25.8 13.0 %collective-permute-start.5 = (bf16[128,2176]{1,0:T(8,128)(2,1)S(1)}, bf16[128,2176]{1,0:T(8,128)(2,1)S(1)}, u32[]{:S(2)}, u32[]{:S(2)}) collective-permute-start(bf16[128,2176]{1,0:T(8,128)(2,1)S(1)} %collective-permute-done.1.refs_2_.refs_3_), channel_id=1, source_target_pairs={{0,1},{1,0},{2,3},{3,2},{4,5},{5,4},{6,7},{7,6},{8,9},{9,8},{10,11... | collective-permute-start | bytes 1671176 | tf_op jit(solution)/shard_map/ppermute | solution.py:42
  25.8 15.1 %collective-permute-start.6 = (bf16[128,2176]{1,0:T(8,128)(2,1)S(1)}, bf16[128,2176]{1,0:T(8,128)(2,1)}, u32[]{:S(2)}, u32[]{:S(2)}) collective-permute-start(bf16[128,2176]{1,0:T(8,128)(2,1)S(1)} %collective-permute-done.refs_3_.refs_4_), channel_id=1, source_target_pairs={{0,4},{1,5},{2,6},{3,7},{4,0},{5,1},{6,2},{7,3},{8,12},{9,13},{10,... | collective-permute-start | bytes 1671176 | tf_op jit(solution)/shard_map/ppermute | solution.py:42
  44.8 17.8 %collective-permute-start.11 = (bf16[8,224,2048]{2,1,0:T(8,128)(2,1)}, bf16[8,224,2048]{2,1,0:T(8,128)(2,1)}, u32[]{:S(2)}, u32[]{:S(2)}) collective-permute-start(bf16[8,224,2048]{2,1,0:T(8,128)(2,1)} %get-tuple-element.294), channel_id=1, source_target_pairs={{0,1},{1,0},{2,3},{3,2},{4,5},{5,4},{6,7},{7,6},{8,9},{9,8},{10,11... | collective-permute-start | bytes 22020104 | tf_op jit(solution)/shard_map/ppermute | solution.py:42
  44.9 17.6 %collective-permute-start.12 = (bf16[128,2176]{1,0:T(8,128)(2,1)}, bf16[128,2176]{1,0:T(8,128)(2,1)}, u32[]{:S(2)}, u32[]{:S(2)}) collective-permute-start(bf16[128,2176]{1,0:T(8,128)(2,1)} %collective-permute-done.3.refs_1_.refs_2_), channel_id=1, source_target_pairs={{0,4},{1,5},{2,6},{3,7},{4,0},{5,1},{6,2},{7,3},{8,12},{9,13},{10,... | collective-permute-start | bytes 1671176 | tf_op jit(solution)/shard_map/ppermute | solution.py:42
  46.4 16.1 %collective-permute-start.13 = (bf16[128,2176]{1,0:T(8,128)(2,1)}, bf16[128,2176]{1,0:T(8,128)(2,1)}, u32[]{:S(2)}, u32[]{:S(2)}) collective-permute-start(bf16[128,2176]{1,0:T(8,128)(2,1)} %collective-permute-done.6.refs_4_.refs_5_), channel_id=1, source_target_pairs={{0,2},{1,3},{2,0},{3,1},{4,6},{5,7},{6,4},{7,5},{8,10},{9,11},{10,... | collective-permute-start | bytes 1671176 | tf_op jit(solution)/shard_map/ppermute | solution.py:42
  46.8 15.7 %collective-permute-start.10 = (bf16[128,2048]{1,0:T(8,128)(2,1)}, bf16[128,2048]{1,0:T(8,128)(2,1)}, u32[]{:S(2)}, u32[]{:S(2)}) collective-permute-start(bf16[128,2048]{1,0:T(8,128)(2,1)} %get-tuple-element.450.refs_3_), channel_id=1, source_target_pairs={{0,8},{1,9},{2,26},{3,27},{4,12},{5,13},{6,30},{7,31},{8,16},{9,17... | collective-permute-start | bytes 1572872 | tf_op jit(solution)/shard_map/ppermute | solution.py:42
  66.5 17.6 %collective-permute-start.17 = (bf16[128,2048]{1,0:T(8,128)(2,1)}, bf16[128,2048]{1,0:T(8,128)(2,1)}, u32[]{:S(2)}, u32[]{:S(2)}) collective-permute-start(bf16[128,2048]{1,0:T(8,128)(2,1)} %collective-permute-done.10.refs_5_), channel_id=1, source_target_pairs={{0,1},{1,0},{2,3},{3,2},{4,5},{5,4},{6,7},{7,6},{8,9},{9,8},{10,11... | collective-permute-start | bytes 1572872 | tf_op jit(solution)/shard_map/ppermute | solution.py:42
  66.7 17.4 %collective-permute-start.18 = (bf16[128,2048]{1,0:T(8,128)(2,1)}, bf16[128,2048]{1,0:T(8,128)(2,1)}, u32[]{:S(2)}, u32[]{:S(2)}) collective-permute-start(bf16[128,2048]{1,0:T(8,128)(2,1)} %collective-permute-done.10.refs_5_), channel_id=1, source_target_pairs={{0,8},{1,9},{2,26},{3,27},{4,12},{5,13},{6,30},{7,31},{8,16},{9,17... | collective-permute-start | bytes 1572872 | tf_op jit(solution)/shard_map/ppermute | solution.py:42
  66.7 17.4 %collective-permute-start.19 = (bf16[128,2048]{1,0:T(8,128)(2,1)}, bf16[128,2048]{1,0:T(8,128)(2,1)}, u32[]{:S(2)}, u32[]{:S(2)}) collective-permute-start(bf16[128,2048]{1,0:T(8,128)(2,1)} %collective-permute-done.10.refs_5_), channel_id=1, source_target_pairs={{0,2},{1,3},{2,0},{3,1},{4,6},{5,7},{6,4},{7,5},{8,10},{9,11},{10,... | collective-permute-start | bytes 1572872 | tf_op jit(solution)/shard_map/ppermute | solution.py:42
  69.2 14.9 %collective-permute-start.20 = (bf16[128,2048]{1,0:T(8,128)(2,1)}, bf16[128,2048]{1,0:T(8,128)(2,1)}, u32[]{:S(2)}, u32[]{:S(2)}) collective-permute-start(bf16[128,2048]{1,0:T(8,128)(2,1)} %collective-permute-done.10.refs_5_), channel_id=1, source_target_pairs={{0,4},{1,5},{2,6},{3,7},{4,0},{5,1},{6,2},{7,3},{8,12},{9,13},{10,... | collective-permute-start | bytes 1572872 | tf_op jit(solution)/shard_map/ppermute | solution.py:42
  69.7 14.4 %collective-permute-start.21 = (bf16[8,224,2048]{2,1,0:T(8,128)(2,1)}, bf16[8,224,2048]{2,1,0:T(8,128)(2,1)}, u32[]{:S(2)}, u32[]{:S(2)}) collective-permute-start(bf16[8,224,2048]{2,1,0:T(8,128)(2,1)} %get-tuple-element.344), channel_id=1, source_target_pairs={{0,1},{1,0},{2,3},{3,2},{4,5},{5,4},{6,7},{7,6},{8,9},{9,8},{10,11... | collective-permute-start | bytes 22020104 | tf_op jit(solution)/shard_map/ppermute | solution.py:42
  90.4 18.0 %collective-permute-start.27 = (bf16[128,2048]{1,0:T(8,128)(2,1)}, bf16[128,2048]{1,0:T(8,128)(2,1)}, u32[]{:S(2)}, u32[]{:S(2)}) collective-permute-start(bf16[128,2048]{1,0:T(8,128)(2,1)} %collective-permute-done.20.refs_6_), channel_id=1, source_target_pairs={{0,8},{1,9},{2,26},{3,27},{4,12},{5,13},{6,30},{7,31},{8,16},{9,17... | collective-permute-start | bytes 1572872 | tf_op jit(solution)/shard_map/ppermute | solution.py:42
  91.9 16.5 %collective-permute-start.28 = (bf16[128,2048]{1,0:T(8,128)(2,1)}, bf16[128,2048]{1,0:T(8,128)(2,1)}, u32[]{:S(2)}, u32[]{:S(2)}) collective-permute-start(bf16[128,2048]{1,0:T(8,128)(2,1)} %collective-permute-done.20.refs_6_), channel_id=1, source_target_pairs={{0,2},{1,3},{2,0},{3,1},{4,6},{5,7},{6,4},{7,5},{8,10},{9,11},{10,... | collective-permute-start | bytes 1572872 | tf_op jit(solution)/shard_map/ppermute | solution.py:42
  93.8 14.7 %collective-permute-start.29 = (bf16[8,224,2048]{2,1,0:T(8,128)(2,1)}, bf16[8,224,2048]{2,1,0:T(8,128)(2,1)}, u32[]{:S(2)}, u32[]{:S(2)}) collective-permute-start(bf16[8,224,2048]{2,1,0:T(8,128)(2,1)} %constant_dynamic-slice_fusion), channel_id=1, source_target_pairs={{0,1},{1,0},{2,3},{3,2},{4,5},{5,4},{6,7},{7,6},{8,9},{9,8},{10,11... | collective-permute-start | bytes 22020104 | tf_op jit(solution)/shard_map/ppermute | solution.py:42
  93.8 14.7 %collective-permute-start.26 = (bf16[128,2048]{1,0:T(8,128)(2,1)}, bf16[128,2048]{1,0:T(8,128)(2,1)}, u32[]{:S(2)}, u32[]{:S(2)}) collective-permute-start(bf16[128,2048]{1,0:T(8,128)(2,1)} %get-tuple-element.450.refs_3_), channel_id=1, source_target_pairs={{0,4},{1,5},{2,6},{3,7},{4,0},{5,1},{6,2},{7,3},{8,12},{9,13},{10,... | collective-permute-start | bytes 1572872 | tf_op jit(solution)/shard_map/ppermute | solution.py:42
  112.2 16.4 %collective-permute-start.33 = (bf16[128,2048]{1,0:T(8,128)(2,1)}, bf16[128,2048]{1,0:T(8,128)(2,1)}, u32[]{:S(2)}, u32[]{:S(2)}) collective-permute-start(bf16[128,2048]{1,0:T(8,128)(2,1)} %get-tuple-element.472), channel_id=1, source_target_pairs={{0,4},{1,5},{2,6},{3,7},{4,0},{5,1},{6,2},{7,3},{8,12},{9,13},{10,... | collective-permute-start | bytes 1572872 | tf_op jit(solution)/shard_map/ppermute | solution.py:42
  113.6 15.0 %collective-permute-start.34 = (bf16[128,2048]{1,0:T(8,128)(2,1)}, bf16[128,2048]{1,0:T(8,128)(2,1)}, u32[]{:S(2)}, u32[]{:S(2)}) collective-permute-start(bf16[128,2048]{1,0:T(8,128)(2,1)} %get-tuple-element.474), channel_id=1, source_target_pairs={{0,2},{1,3},{2,0},{3,1},{4,6},{5,7},{6,4},{7,5},{8,10},{9,11},{10,... | collective-permute-start | bytes 1572872 | tf_op jit(solution)/shard_map/ppermute | solution.py:42
  113.8 14.8 %collective-permute-start.35 = (bf16[128,2048]{1,0:T(8,128)(2,1)}, bf16[128,2048]{1,0:T(8,128)(2,1)}, u32[]{:S(2)}, u32[]{:S(2)}) collective-permute-start(bf16[128,2048]{1,0:T(8,128)(2,1)} %get-tuple-element.473), channel_id=1, source_target_pairs={{0,24},{1,25},{2,10},{3,11},{4,28},{5,29},{6,14},{7,15},{8,0},{9,1... | collective-permute-start | bytes 1572872 | tf_op jit(solution)/shard_map/ppermute | solution.py:42
  133.9 19.2 %collective-permute-start.38 = (bf16[128,2048]{1,0:T(8,128)(2,1)}, bf16[128,2048]{1,0:T(8,128)(2,1)}, u32[]{:S(2)}, u32[]{:S(2)}) collective-permute-start(bf16[128,2048]{1,0:T(8,128)(2,1)} %add_convert_fusion.8), channel_id=1, source_target_pairs={{0,4},{1,5},{2,6},{3,7},{4,0},{5,1},{6,2},{7,3},{8,12},{9,13},{10,... | collective-permute-start | bytes 1572872 | tf_op jit(solution)/shard_map/ppermute | solution.py:42
  134.4 18.6 %collective-permute-start.39 = (bf16[128,2048]{1,0:T(8,128)(2,1)}, bf16[128,2048]{1,0:T(8,128)(2,1)}, u32[]{:S(2)}, u32[]{:S(2)}) collective-permute-start(bf16[128,2048]{1,0:T(8,128)(2,1)} %get-tuple-element.498), channel_id=1, source_target_pairs={{0,2},{1,3},{2,0},{3,1},{4,6},{5,7},{6,4},{7,5},{8,10},{9,11},{10,... | collective-permute-start | bytes 1572872 | tf_op jit(solution)/shard_map/ppermute | solution.py:42
  136.9 16.1 %collective-permute-start.40 = (bf16[128,2048]{1,0:T(8,128)(2,1)}, bf16[128,2048]{1,0:T(8,128)(2,1)}, u32[]{:S(2)}, u32[]{:S(2)}) collective-permute-start(bf16[128,2048]{1,0:T(8,128)(2,1)} %get-tuple-element.497), channel_id=1, source_target_pairs={{0,24},{1,25},{2,10},{3,11},{4,28},{5,29},{6,14},{7,15},{8,0},{9,1... | collective-permute-start | bytes 1572872 | tf_op jit(solution)/shard_map/ppermute | solution.py:42
  153.3 13.1 %collective-permute-start.41 = (bf16[128,2048]{1,0:T(8,128)(2,1)S(1)}, bf16[128,2048]{1,0:T(8,128)(2,1)S(1)}, u32[]{:S(2)}, u32[]{:S(2)}) collective-permute-start(bf16[128,2048]{1,0:T(8,128)(2,1)S(1)} %get-tuple-element.529), channel_id=1, source_target_pairs={{0,4},{1,5},{2,6},{3,7},{4,0},{5,1},{6,2},{7,3},{8,12},{9,13},{10,... | collective-permute-start | bytes 1572872 | tf_op jit(solution)/shard_map/ppermute | solution.py:42
  154.8 12.8 %collective-permute-start.42 = (bf16[128,2048]{1,0:T(8,128)(2,1)S(1)}, bf16[128,2048]{1,0:T(8,128)(2,1)S(1)}, u32[]{:S(2)}, u32[]{:S(2)}) collective-permute-start(bf16[128,2048]{1,0:T(8,128)(2,1)S(1)} %get-tuple-element.528), channel_id=1, source_target_pairs={{0,2},{1,3},{2,0},{3,1},{4,6},{5,7},{6,4},{7,5},{8,10},{9,11},{10,... | collective-permute-start | bytes 1572872 | tf_op jit(solution)/shard_map/ppermute | solution.py:42
  156.7 14.7 %collective-permute-start.46 = (bf16[128,2048]{1,0:T(8,128)(2,1)S(1)}, bf16[128,2048]{1,0:T(8,128)(2,1)S(1)}, u32[]{:S(2)}, u32[]{:S(2)}) collective-permute-start(bf16[128,2048]{1,0:T(8,128)(2,1)S(1)} %add_convert_fusion.5), channel_id=1, source_target_pairs={{0,24},{1,25},{2,10},{3,11},{4,28},{5,29},{6,14},{7,15},{8,0},{9,1... | collective-permute-start | bytes 1572872 | tf_op jit(solution)/shard_map/ppermute | solution.py:42
  168.6 12.5 %collective-permute-start.45 = (bf16[128,2048]{1,0:T(8,128)(2,1)S(1)}, bf16[128,2048]{1,0:T(8,128)(2,1)S(1)}, u32[]{:S(2)}, u32[]{:S(2)}) collective-permute-start(bf16[128,2048]{1,0:T(8,128)(2,1)S(1)} %get-tuple-element.527), channel_id=1, source_target_pairs={{0,24},{1,25},{2,10},{3,11},{4,28},{5,29},{6,14},{7,15},{8,0},{9,1... | collective-permute-start | bytes 1572872 | tf_op jit(solution)/shard_map/ppermute | solution.py:42
  182.1 13.7 %collective-permute-start.48 = (bf16[128,2048]{1,0:T(8,128)(2,1)S(1)}, bf16[128,2048]{1,0:T(8,128)(2,1)S(1)}, u32[]{:S(2)}, u32[]{:S(2)}) collective-permute-start(bf16[128,2048]{1,0:T(8,128)(2,1)S(1)} %add_convert_fusion.3), channel_id=1, source_target_pairs={{0,24},{1,25},{2,10},{3,11},{4,28},{5,29},{6,14},{7,15},{8,0},{9,1... | collective-permute-start | bytes 1572872 | tf_op jit(solution)/shard_map/ppermute | solution.py:42
  199.5 14.4 %collective-permute-start.49 = (bf16[128,2048]{1,0:T(8,128)(2,1)S(1)}, bf16[128,2048]{1,0:T(8,128)(2,1)S(1)}, u32[]{:S(2)}, u32[]{:S(2)}) collective-permute-start(bf16[128,2048]{1,0:T(8,128)(2,1)S(1)} %add_convert_fusion.2), channel_id=1, source_target_pairs={{0,2},{1,3},{2,0},{3,1},{4,6},{5,7},{6,4},{7,5},{8,10},{9,11},{10,... | collective-permute-start | bytes 1572872 | tf_op jit(solution)/shard_map/ppermute | solution.py:42
  (44 other events, 409.2 us)
